TPU v7x, 32 devices: a whole 2x2x4 slice. The times are simulated.
32 devices in a mesh: ctx: 16 (over z, x, core), ch: 2 (over y).
Axes of the slice: x: 2, y: 2, z: 4, core: 2. Of those that a mesh axis runs over, the one named last changes fastest.
Arguments:
- qkv: bfloat16 [3, 8192, 4096], P(None, 'ctx', 'ch'), may hold values from -6 to 6
- short_filter: float32 [3, 3, 4096], P(None, None, 'ch'), may hold values from -3 to 3
- long_filter: bfloat16 [2048, 4096], P(None, 'ch'), may hold values from -0.125 to 0.125
- skip: float32 [4096], P('ch'), may hold values from -1 to 1
- shard_doc: int32 [16], replicated, may hold values from 0 to 3, as said below
- live: int32 [16], replicated, may hold values from 1 to 512
Outputs:
- filtered: bfloat16 [2, 2048, 8192], P(None, 'ctx', 'ch')
Inputs may be any that keep to these rules, and one draw needn't show every extreme that they name: `shard_doc`: documents occupy whole consecutive shards in order; each document spans 1 to 8 shards and one spans exactly 8. Read only for a shard that ends a document; its tokens at offsets from live on are padding.
All inputs are finite; a program needn't handle non-finite values.
Results may differ from a plain program's by a relative error of at most 0.012.
Values may be sent and summed in bfloat16 or wider, within the bound.
No kernel may reach another device: no remote copies, remote signals or barrier semaphores. Data moves between devices by JAX's collectives and lax.ppermute only.
A program may use at most 256 MiB of HBM per device.

v0:
```python
import functools

import jax
import jax.numpy as jnp
from jax import lax
from jax.experimental import pallas as pl
from jax.experimental.pallas import tpu as pltpu
from jax.sharding import PartitionSpec as P

LANES = 128
UNROLL = 4
VMEM = 56 << 20


def short_kernel(doc, live, border, taps, qkv, qs_out, gated_out):
    shards = doc.shape[0]
    here = lax.axis_index("ctx")
    tok = qkv.shape[1]
    before = jnp.maximum(here - 1, 0)
    after = jnp.minimum(here + 1, shards - 1)
    joined = (here > 0) & (doc[before] == doc[here])
    closing = (here == shards - 1) | (doc[after] != doc[here])
    limit = jnp.where(closing, live[here], tok)

    def short(a):
        x = qkv[a].astype(jnp.float32)
        edge = jnp.where(joined, border[a].astype(jnp.float32), 0.0)
        once = jnp.concatenate([edge[1:2], x[:-1]], axis=0)
        twice = jnp.concatenate([edge, x[:-2]], axis=0)
        return taps[a, 0:1, :] * x + taps[a, 1:2, :] * once + taps[a, 2:3, :] * twice

    rows = lax.broadcasted_iota(jnp.int32, qkv.shape[1:], 0)
    keep = jnp.where(rows < limit, 1.0, 0.0)
    qs_out[...] = short(0).astype(jnp.bfloat16).T
    gated_out[...] = (short(1) * short(2) * keep).astype(jnp.bfloat16).T


def short_and_gate(qkv, border, short_filter, shard_doc, live):
    _, tok, width = qkv.shape
    block = min(256, width)
    smem = pl.BlockSpec(memory_space=pltpu.SMEM)
    out = pl.BlockSpec((block, tok), lambda i: (i, 0))
    return pl.pallas_call(
        short_kernel,
        grid=(width // block,),
        in_specs=[
            smem,
            smem,
            pl.BlockSpec((3, 2, block), lambda i: (0, 0, i)),
            pl.BlockSpec((3, 3, block), lambda i: (0, 0, i)),
            pl.BlockSpec((3, tok, block), lambda i: (0, 0, i)),
        ],
        out_specs=[out, out],
        out_shape=[jax.ShapeDtypeStruct((width, tok), jnp.bfloat16)] * 2,
        compiler_params=pltpu.CompilerParams(vmem_limit_bytes=VMEM),
        name="short_and_gate",
    )(shard_doc, live, border, short_filter, qkv)


def conv_kernel(doc, live, skip, filt, gated, queries, out, taps, masks, wide, one, mixed):
    shards, chans, tok = gated.shape
    per = tok // LANES
    blocks = shards * per
    lag_blocks = masks.shape[0]
    pad = lag_blocks - 1
    step = pl.program_id(0)

    @pl.when(step == 0)
    def _():
        taps[...] = filt[...].astype(jnp.float32).T
        wide[pl.ds(0, pad * chans), :] = jnp.zeros((pad * chans, LANES), jnp.float32)
        start = jnp.int32(0)
        rows = lax.broadcasted_iota(jnp.int32, (per, LANES), 0)
        runs = []
        for s in range(shards):
            if s > 0:
                start = jnp.where(doc[s] == doc[s - 1], start, s)
            runs.append(rows + (s - start) * per)
        run = jnp.concatenate(runs, axis=0)
        for k in range(lag_blocks):
            masks[k] = jnp.where(run >= k, 1.0, 0.0).astype(jnp.bfloat16)

    for s in range(shards):
        for b in range(per):
            rows = pl.ds((pad + s * per + b) * chans, chans)
            wide[rows, :] = gated[s, :, b * LANES : (b + 1) * LANES].astype(jnp.float32)

    def channel(c, slot):
        row = taps[pl.ds(step * chans + c, 1), :]
        row = jnp.concatenate([row, jnp.zeros((1, LANES), jnp.float32)], axis=1)
        spread = jnp.broadcast_to(row, (16, row.shape[1]))
        band = pltpu.roll(spread, 0, 1, stride=1, stride_axis=0).astype(jnp.bfloat16)
        bands = [band] + [pltpu.roll(band, 16 * q, 1) for q in range(1, LANES // 16)]
        toeplitz = jnp.concatenate(bands, axis=0)
        weights = jnp.concatenate(
            [toeplitz[:, k * LANES : (k + 1) * LANES] for k in range(lag_blocks)], axis=0
        )
        one[slot] = wide[pl.ds(c, blocks + pad, stride=chans), :]
        lagged = [
            one[slot, pl.ds(pad - k, blocks), :].astype(jnp.bfloat16) * masks[k]
            for k in range(lag_blocks)
        ]
        mixed[pl.ds(c, blocks, stride=chans), :] = jnp.dot(
            jnp.concatenate(lagged, axis=1), weights, preferred_element_type=jnp.float32
        )

    def group(i, _):
        for slot in range(UNROLL):
            channel(i * UNROLL + slot, slot)
        return 0

    lax.fori_loop(0, chans // UNROLL, group, 0)

    direct = skip[...]
    places = lax.broadcasted_iota(jnp.int32, (1, tok), 1)
    for s in range(shards):
        if s < shards - 1:
            limit = jnp.where(doc[s] != doc[s + 1], live[s], tok)
        else:
            limit = live[s]
        keep = jnp.where(places < limit, 1.0, 0.0)
        conv = jnp.concatenate(
            [mixed[pl.ds((s * per + b) * chans, chans), :] for b in range(per)], axis=1
        )
        total = conv + direct * gated[s].astype(jnp.float32)
        done = queries[s].astype(jnp.float32) * total * keep
        halves, _, half_tok = out.shape
        first = s * tok
        out[first // half_tok, :, pl.ds(first % half_tok, tok)] = done.astype(jnp.bfloat16)


def long_conv(gated, queries, filt, skip, shard_doc, live, halves):
    shards, width, tok = gated.shape
    lags = filt.shape[0]
    chans = min(32, width)
    blocks = shards * tok // LANES
    lag_blocks = lags // LANES + 1
    half_tok = shards * tok // halves
    smem = pl.BlockSpec(memory_space=pltpu.SMEM)
    slab = pl.BlockSpec((shards, chans, tok), lambda i: (0, i, 0))
    return pl.pallas_call(
        conv_kernel,
        grid=(width // chans,),
        in_specs=[
            smem,
            smem,
            pl.BlockSpec((chans, 1), lambda i: (i, 0)),
            pl.BlockSpec((lags, width), lambda i: (0, 0)),
            slab,
            slab,
        ],
        out_specs=pl.BlockSpec((halves, chans, half_tok), lambda i: (0, i, 0)),
        out_shape=jax.ShapeDtypeStruct((halves, width, half_tok), jnp.bfloat16),
        scratch_shapes=[
            pltpu.VMEM((width, lags), jnp.float32),
            pltpu.VMEM((lag_blocks, blocks, LANES), jnp.bfloat16),
            pltpu.VMEM(((blocks + lag_blocks - 1) * chans, LANES), jnp.float32),
            pltpu.VMEM((UNROLL, blocks + lag_blocks - 1, LANES), jnp.float32),
            pltpu.VMEM((blocks * chans, LANES), jnp.float32),
        ],
        compiler_params=pltpu.CompilerParams(
            vmem_limit_bytes=VMEM, dimension_semantics=("arbitrary",)
        ),
        name="long_conv",
    )(shard_doc, live, skip[:, None], filt, gated, queries)


def local(qkv, short_filter, long_filter, skip, shard_doc, live):
    shards = lax.axis_size("ctx")
    here = lax.axis_index("ctx")
    tok, width = qkv.shape[1:]
    part = width // shards
    route = [(i, i + 1) for i in range(shards - 1)]
    border = lax.ppermute(qkv[:, tok - 2 :, :], "ctx", route)
    queries, gated = short_and_gate(qkv, border, short_filter, shard_doc, live)
    gated = lax.all_to_all(gated.reshape(shards, part, tok), "ctx", 0, 0)
    queries = lax.all_to_all(queries.reshape(shards, part, tok), "ctx", 0, 0)
    filt = lax.dynamic_slice_in_dim(long_filter, here * part, part, axis=1)
    direct = lax.dynamic_slice_in_dim(skip, here * part, part, axis=0)
    out = long_conv(gated, queries, filt, direct, shard_doc, live, lax.axis_size("ch"))
    return lax.all_to_all(out, "ch", 0, 0)


def solution(mesh):
    return jax.shard_map(
        local,
        mesh=mesh,
        in_specs=(P(None, "ctx", "ch"), P(None, None, "ch"), P(None, "ch"), P("ch"), P(), P()),
        out_specs=P(None, "ctx", "ch"),
        check_vma=False,
    )
```

profile of v0, /device:TPU:10, one launch (start us, length us, event | category | flops | bytes accessed | tf_op | source)
XLA Modules:
  0.0 193.7 jit_solution(219834631564348785)
XLA Ops:
  0.0 0.0 copy-start
  0.0 0.9 slice.3
  0.9 1.9 collective-permute-start
  2.9 3.2 %collective-permute-done.border = bf16[3,2,2048]{2,1,0:T(2,128)(2,1)S(1)} collective-permute-done((bf16[3,2,2048]{2,1,0:T(2,128)(2,1)S(1)}, bf16[3,2,2048]{2,1,0:T(2,128)(2,1)S(1)}, u32[]{:S(2)}, u32[]{:S(2)}) %collective-permute-start) | collective-permute-done | bytes 24608 | tf_op jit(solution)/shard_map/ppermute | solution.py:174
  6.1 0.0 copy-start.2
  6.1 0.6 copy-done.2
  6.7 9.3 %short_and_gate.1 = (bf16[2048,512]{1,0:T(8,128)(2,1)}, bf16[2048,512]{1,0:T(8,128)(2,1)}) custom-call(s32[16]{0:T(128)} %doc.3, s32[16]{0:T(128)} %live.3, bf16[3,2,2048]{2,1,0:T(2,128)(2,1)} %copy-done.2, f32[3,3,2048]{2,1,0:T(4,128)} %taps.1, bf16[3,512,2048]{2,1,0:T(8,128)(2,1)} %qkv.1), custom_call_target="tpu_custom_call" | custom-call | tf_op jit(solution)/shard_map/short_and_gate/pallas_call | solution.py:43
  16.0 53.5 %all_to_all.15.queries = bf16[16,128,512]{2,1,0:T(8,128)(2,1)} all-to-all(bf16[16,128,512]{2,1,0:T(8,128)(2,1)} %bitcast.5), channel_id=1, replica_groups=mesh['ctx'=16,'ch'=2] {'ctx'}, dimensions={0} | all-to-all | bytes 4194304 | tf_op jit(solution)/shard_map/all_to_all | solution.py:177
  69.5 5.3 %all-to-all-start = ((bf16[16,128,512]{2,1,0:T(8,128)(2,1)}), bf16[16,128,512]{2,1,0:T(8,128)(2,1)S(1)}, u32[]{:S(2)}, u32[]{:S(2)}) async-start(bf16[16,128,512]{2,1,0:T(8,128)(2,1)} %bitcast.4), calls=%async_computation | async-start | bytes 4194304 | tf_op jit(solution)/shard_map/all_to_all | solution.py:176
  74.7 0.0 copy-done
  74.7 0.1 dynamic-slice_bitcast_fusion
  74.8 0.7 copy.7.skip
  75.6 1.9 constant_dynamic-slice_fusion.filt
  77.4 44.6 %all-to-all-done.gated = bf16[16,128,512]{2,1,0:T(8,128)(2,1)S(1)} async-done(((bf16[16,128,512]{2,1,0:T(8,128)(2,1)}), bf16[16,128,512]{2,1,0:T(8,128)(2,1)S(1)}, u32[]{:S(2)}, u32[]{:S(2)}) %all-to-all-start) | async-done | bytes 2097184 | tf_op jit(solution)/shard_map/all_to_all | solution.py:176
  122.0 0.0 copy-start.1
  122.0 1.3 copy-done.1
  123.3 39.8 %long_conv.1 = bf16[2,128,4096]{2,1,0:T(8,128)(2,1)} custom-call(s32[16]{0:T(128)} %doc.3, s32[16]{0:T(128)} %live.3, f32[128,1]{1,0:T(8,128)} %copy.7.skip, bf16[2048,128]{1,0:T(8,128)(2,1)} %constant_dynamic-slice_fusion.filt, bf16[16,128,512]{2,1,0:T(8,128)(2,1)} %copy-done.1, bf16[16,128,512]{2,1,0:T(8,128)(2,1)} %all_to_all.15.queries), custom_call_target="tpu_custom_call" | custom-call | tf_op jit(solution)/shard_map/long_conv/pallas_call | solution.py:141
  163.1 29.3 %all_to_all.16 = bf16[2,128,4096]{2,1,0:T(8,128)(2,1)S(1)} all-to-all(bf16[2,128,4096]{2,1,0:T(8,128)(2,1)} %long_conv.1), channel_id=1, replica_groups=mesh['ctx'=16,'ch'=2] {'ch'}, dimensions={0} | all-to-all | bytes 4194304 | tf_op jit(solution)/shard_map/all_to_all | solution.py:181
  192.4 1.3 copy.9
Async XLA Ops:
  0.0 74.7 %copy-start = (f32[2048]{0:T(1024)S(1)}, f32[2048]{0:T(1024)}, u32[]{:S(2)}) copy-start(f32[2048]{0:T(1024)} %param.9) | copy-start | bytes 24580
  0.9 5.1 %collective-permute-start = (bf16[3,2,2048]{2,1,0:T(2,128)(2,1)S(1)}, bf16[3,2,2048]{2,1,0:T(2,128)(2,1)S(1)}, u32[]{:S(2)}, u32[]{:S(2)}) collective-permute-start(bf16[3,2,2048]{2,1,0:T(2,128)(2,1)S(1)} %slice.3), channel_id=1, source_target_pairs={{0,2},{2,4},{4,6},{6,8},{8,10},{10,12},{12,14},{14,16},{16,18},{18... | collective-permute-start | bytes 73736 | tf_op jit(solution)/shard_map/ppermute | solution.py:174
  6.1 0.6 copy-start.2
  69.5 52.5 %all-to-all-start = ((bf16[16,128,512]{2,1,0:T(8,128)(2,1)}), bf16[16,128,512]{2,1,0:T(8,128)(2,1)S(1)}, u32[]{:S(2)}, u32[]{:S(2)}) async-start(bf16[16,128,512]{2,1,0:T(8,128)(2,1)} %bitcast.4), calls=%async_computation | async-start | bytes 4194304 | tf_op jit(solution)/shard_map/all_to_all | solution.py:176
  122.0 1.3 copy-start.1
where the time goes:
time: 194 us
  blocking collectives  82.8 us (43%)
  Pallas kernels  49.1 us (25%)
  waiting for transfers between devices  47.8 us (25%)
  starting transfers between devices  7.19 us (4%)
  local copies, waits for them, and re-layouts  6.87 us (4%)
    all_to_all x1, blocking collectives, local(): queries = lax.all_to_all(queries.reshape(shards, part, tok), 'ctx', 0, 0)  53.5 us
    all_to_all x1, waiting for transfers between devices, local(): gated = lax.all_to_all(gated.reshape(shards, part, tok), 'ctx', 0, 0)  44.6 us
    pallas_call x1, Pallas kernels, long_conv(): pl.pallas_call(conv_kernel, grid=(width // chans,), in_specs=[smem, smem,...  39.8 us
    all_to_all x1, blocking collectives, local(): return lax.all_to_all(out, 'ch', 0, 0)  29.3 us
    pallas_call x1, Pallas kernels, short_and_gate(): pl.pallas_call(short_kernel, grid=(width // block,), in_specs=[smem, smem...  9.28 us
    all_to_all x1, starting transfers between devices, local(): gated = lax.all_to_all(gated.reshape(shards, part, tok), 'ctx', 0, 0)  5.27 us
  transfers between devices with their start and end apart: 2, of which 2 were waited for; matrix products, arithmetic and copies ran while one was open for 1% of the time, Pallas kernels for 0%

commit v1 on v0

v1 whole, which is shorter than its diff:
```python
import functools

import jax
import jax.numpy as jnp
from jax import lax
from jax.experimental import pallas as pl
from jax.experimental.pallas import tpu as pltpu
from jax.sharding import PartitionSpec as P

LANES = 128
UNROLL = 8
ROWS = 64
CORES = 2
FLYING = 5
VMEM = 56 << 20


def short_kernel(count, doc, live, *refs):
    borders, taps, slabs = refs[:count], refs[count : 2 * count], refs[2 * count : 3 * count]
    outs, tall, turned = refs[3 * count : -2], refs[-2], refs[-1]
    shards = doc.shape[0]
    here = lax.axis_index("ctx")
    tok = slabs[0].shape[1]
    before = jnp.maximum(here - 1, 0)
    after = jnp.minimum(here + 1, shards - 1)
    joined = (here > 0) & (doc[before] == doc[here])
    closing = (here == shards - 1) | (doc[after] != doc[here])
    limit = jnp.where(closing, live[here], tok)

    def short(a):
        x = slabs[a][0].astype(jnp.float32)
        edge = jnp.where(joined, borders[a][0].astype(jnp.float32), 0.0)
        tall[a, 6:8, :] = edge
        tall[a, pl.ds(8, tok), :] = x
        once = tall[a, pl.ds(7, tok), :]
        twice = tall[a, pl.ds(6, tok), :]
        tap = taps[a]
        return tap[0, 0:1, :] * x + tap[0, 1:2, :] * once + tap[0, 2:3, :] * twice

    value = short(0)
    if count == 2:
        rows = lax.broadcasted_iota(jnp.int32, value.shape, 0)
        value = value * short(1) * jnp.where(rows < limit, 1.0, 0.0)
    value = value.astype(jnp.bfloat16).T
    if len(outs) == 1:
        part = outs[0].shape[1]
        for j in range(outs[0].shape[0]):
            outs[0][j] = value[j * part : (j + 1) * part]
    else:
        turned[...] = value
        part = outs[0].shape[1]
        for k, out in enumerate(outs):
            for j in range(out.shape[0]):
                row = (CORES * j + ((here % CORES) ^ k)) * part
                out[j] = turned[pl.ds(pl.multiple_of(row, part), part), :]


def short_convs(qkv, border, short_filter, shard_doc, live, which, split):
    _, tok, width = qkv.shape
    shards = shard_doc.shape[0]
    part = width // shards
    block = min(width, 512)
    smem = pl.BlockSpec(memory_space=pltpu.SMEM)
    count = len(which)

    def spec(rows, a):
        return pl.BlockSpec((1, rows, block), lambda i: (a, 0, i))

    many = CORES if split else 1
    rows = block // part // many
    return pl.pallas_call(
        functools.partial(short_kernel, count),
        grid=(width // block,),
        in_specs=[smem] * 2
        + [spec(2, a) for a in which]
        + [spec(3, a) for a in which]
        + [spec(tok, a) for a in which],
        out_specs=[pl.BlockSpec((rows, part, tok), lambda i: (i, 0, 0))] * many,
        out_shape=[jax.ShapeDtypeStruct((shards // many, part, tok), jnp.bfloat16)] * many,
        scratch_shapes=[
            pltpu.VMEM((count, tok + 8, block), jnp.float32),
            pltpu.VMEM((block, tok), jnp.bfloat16),
        ],
        compiler_params=pltpu.CompilerParams(vmem_limit_bytes=VMEM),
        name="short_" + "".join("qkv"[a] for a in which),
    )(shard_doc, live, *[border] * count, *[short_filter] * count, *[qkv] * count)


def pair_up_kernel(*refs):
    blocks, outs = refs[:CORES], refs[CORES:]
    here = lax.axis_index("ctx")
    for k, block in enumerate(blocks):
        row = (here % CORES) ^ k
        for far, out in enumerate(outs):
            out[row] = block[(here // CORES) ^ far]


def pair_up(blocks):
    chips, part, tok = blocks[0].shape
    vmem = pl.BlockSpec(memory_space=pltpu.VMEM)
    return pl.pallas_call(
        pair_up_kernel,
        in_specs=[vmem] * CORES,
        out_specs=[vmem] * chips,
        out_shape=[jax.ShapeDtypeStruct((CORES, part, tok), jnp.bfloat16)] * chips,
        compiler_params=pltpu.CompilerParams(vmem_limit_bytes=VMEM),
        name="pair_up",
    )(*blocks)


def conv_kernel(doc, live, skip, filt, gated, out, taps, masks, wide, one, late, mixed):
    shards, chans, tok = gated.shape
    pitch = chans + 1
    per = tok // LANES
    fine = tok // ROWS
    blocks = shards * fine
    pairs = masks.shape[0] - 1
    pad = 8 * (pairs - 1)
    step = pl.program_id(0)
    lags = taps.shape[1]
    spans = lags // (4 * ROWS) + 1

    @pl.when(step == 0)
    def _():
        taps[...] = filt[...].astype(jnp.float32).T
        wide[pl.ds(0, pad * pitch), :] = jnp.zeros((pad * pitch, LANES), jnp.float32)
        late[:, pl.ds(0, 8), :] = jnp.zeros((late.shape[0], 8, LANES), jnp.float32)
        start = jnp.int32(0)
        rows = lax.broadcasted_iota(jnp.int32, (fine, LANES), 0)
        left = lax.broadcasted_iota(jnp.int32, (blocks, LANES), 1) < ROWS
        runs = []
        for s in range(shards):
            if s > 0:
                start = jnp.where(doc[s] == doc[s - 1], start, s)
            runs.append(rows + (s - start) * fine)
        run = jnp.concatenate(runs, axis=0)
        for m in range(pairs):
            reach = jnp.where(left, 8 * m, 8 * m + 4)
            masks[m] = jnp.where(run >= reach, 1.0, 0.0).astype(jnp.bfloat16)
        masks[pairs] = jnp.where(run >= 2, 1.0, 0.0).astype(jnp.bfloat16)

    left = lax.broadcasted_iota(jnp.int32, (chans, LANES), 1) < ROWS
    older = [(jnp.zeros((chans, LANES), jnp.float32),) * 2] * 2
    for s in range(shards):
        for b in range(per):
            here = gated[s, :, b * LANES : (b + 1) * LANES].astype(jnp.float32)
            turned = pltpu.roll(here, ROWS, 1)
            row = pad + s * fine + 2 * b
            wide[pl.ds(row * pitch, chans), :] = jnp.where(left, here, older[0][1])
            wide[pl.ds((row + 1) * pitch, chans), :] = jnp.where(left, turned, older[0][0])
            older = [older[1], (here, turned)]

    def channel(c, slot):
        row = taps[pl.ds(step * chans + c, 1), :]
        row = jnp.concatenate([row, jnp.zeros((1, 4 * ROWS), jnp.float32)], axis=1)
        spread = jnp.broadcast_to(row, (16, row.shape[1]))
        band = pltpu.roll(spread, 0, 1, stride=1, stride_axis=0).astype(jnp.bfloat16)
        bands = [band] + [pltpu.roll(band, 16 * q, 1) for q in range(1, ROWS // 16)]
        toeplitz = jnp.concatenate(bands, axis=0)
        slices = [toeplitz[:, k * 4 * ROWS : (k + 1) * 4 * ROWS] for k in range(spans)]
        slices += [jnp.zeros_like(slices[0])] * (2 * pairs - spans)
        weights = jnp.concatenate(slices, axis=0)
        one[slot] = wide[pl.ds(c, blocks + pad, stride=pitch), :]
        lagged = [
            one[slot, pl.ds(pad - 8 * m, blocks), :].astype(jnp.bfloat16) * masks[m]
            for m in range(pairs)
        ]
        sums = jnp.dot(
            jnp.concatenate(lagged, axis=1), weights, preferred_element_type=jnp.float32
        )
        late[slot, pl.ds(8, blocks), :] = sums[:, LANES:]
        behind = late[slot, pl.ds(6, blocks), :] * masks[pairs].astype(jnp.float32)
        mixed[pl.ds(c, blocks, stride=pitch), :] = sums[:, :LANES] + behind

    def group(i, _):
        for slot in range(UNROLL):
            channel(i * UNROLL + slot, slot)
        return 0

    lax.fori_loop(0, chans // UNROLL, group, 0)

    direct = skip[...]
    places = lax.broadcasted_iota(jnp.int32, (1, tok), 1)
    for s in range(shards):
        if s < shards - 1:
            limit = jnp.where(doc[s] != doc[s + 1], live[s], tok)
        else:
            limit = live[s]
        keep = jnp.where(places < limit, 1.0, 0.0)
        sums = []
        for b in range(per):
            row = s * fine + 2 * b
            after = mixed[pl.ds((row + 1) * pitch, chans), :]
            if row > 0:
                spill = mixed[pl.ds((row - 1) * pitch, chans), :]
                if b == 0:
                    spill = jnp.where(doc[s] == doc[s - 1], spill, 0.0)
            else:
                spill = jnp.zeros_like(after)
            sums.append(
                mixed[pl.ds(row * pitch, chans), :]
                + pltpu.roll(jnp.where(left, after, spill), ROWS, 1)
            )
        conv = jnp.concatenate(sums, axis=1)
        total = (conv + direct * gated[s].astype(jnp.float32)) * keep
        out[s] = total.astype(jnp.bfloat16)


def long_conv(gated, filt, skip, shard_doc, live):
    shards, width, tok = gated.shape
    lags, part = filt.shape
    chans = min(32, width)
    blocks = shards * tok // ROWS
    pairs = (lags // (4 * ROWS) + 2) // 2
    tall = blocks + 8 * (pairs - 1)
    smem = pl.BlockSpec(memory_space=pltpu.SMEM)
    slab = pl.BlockSpec((shards, chans, tok), lambda i: (0, i, 0))
    return pl.pallas_call(
        conv_kernel,
        grid=(width // chans,),
        in_specs=[
            smem,
            smem,
            pl.BlockSpec((chans, 1), lambda i: (i, 0)),
            pl.BlockSpec((lags, part), lambda i: (0, 0)),
            slab,
        ],
        out_specs=slab,
        out_shape=jax.ShapeDtypeStruct((shards, width, tok), jnp.bfloat16),
        scratch_shapes=[
            pltpu.VMEM((part, lags), jnp.float32),
            pltpu.VMEM((pairs + 1, blocks, LANES), jnp.bfloat16),
            pltpu.VMEM((tall * (chans + 1), LANES), jnp.float32),
            pltpu.VMEM((UNROLL, tall, LANES), jnp.float32),
            pltpu.VMEM((UNROLL, blocks + 8, LANES), jnp.float32),
            pltpu.VMEM((blocks * (chans + 1), LANES), jnp.float32),
        ],
        compiler_params=pltpu.CompilerParams(
            vmem_limit_bytes=VMEM, dimension_semantics=("arbitrary",)
        ),
        cost_estimate=pl.CostEstimate(
            flops=2 * width * shards * tok * lags,
            bytes_accessed=width * shards * tok * 4 + lags * part * 2,
            transcendentals=0,
        ),
        name="long_conv",
    )(shard_doc, live, skip, filt, gated)


def gate_kernel(fars, *refs):
    blocks, conv, own, sent = refs[:-3], refs[-3], refs[-2], refs[-1]
    shards, _, tok = conv.shape
    halves = sent.shape[0] + 1
    per = shards // halves
    span = len(fars) // halves
    here = lax.axis_index("ctx")
    mine = lax.axis_index("ch")
    for far, block in zip(fars, blocks):
        chip = (here // CORES) ^ far
        first = chip * CORES
        away = (first // per + halves - mine) % halves
        values = [
            (block[k].astype(jnp.float32) * conv[first + k].astype(jnp.float32)).astype(
                jnp.bfloat16
            )
            for k in range(CORES)
        ]
        value = jnp.concatenate(values, axis=1)
        start = chip % span * (CORES * tok)
        column = pl.ds(pl.multiple_of(start, CORES * tok), CORES * tok)

        @pl.when(away == 0)
        def _():
            own[:, column] = value

        @pl.when(away != 0)
        def _():
            sent[away - 1, :, column] = value


def gate(fars, blocks, conv, halves):
    _, width, tok = blocks[0].shape
    shards = conv.shape[0]
    chans = min(64, width)
    wide = len(fars) // halves * CORES * tok
    return pl.pallas_call(
        functools.partial(gate_kernel, fars),
        grid=(width // chans,),
        in_specs=[pl.BlockSpec((CORES, chans, tok), lambda i: (0, i, 0))] * len(blocks)
        + [pl.BlockSpec((shards, chans, tok), lambda i: (0, i, 0))],
        out_specs=[
            pl.BlockSpec((chans, wide), lambda i: (i, 0)),
            pl.BlockSpec((halves - 1, chans, wide), lambda i: (0, i, 0)),
        ],
        out_shape=[
            jax.ShapeDtypeStruct((width, wide), jnp.bfloat16),
            jax.ShapeDtypeStruct((halves - 1, width, wide), jnp.bfloat16),
        ],
        compiler_params=pltpu.CompilerParams(vmem_limit_bytes=VMEM),
        name="gate",
    )(*blocks, conv)


def local(qkv, short_filter, long_filter, skip, shard_doc, live):
    shards = lax.axis_size("ctx")
    halves = lax.axis_size("ch")
    here = lax.axis_index("ctx")
    mine = lax.axis_index("ch")
    tok, width = qkv.shape[1:]
    part = width // shards
    chips = shards // CORES
    span = chips // halves
    border = lax.ppermute(
        qkv[:, tok - 2 :, :], "ctx", [(i, i + 1) for i in range(shards - 1)]
    )
    filt = lax.dynamic_slice_in_dim(long_filter, here * part, part, axis=1)
    direct = lax.dynamic_slice_in_dim(skip, here * part, part, axis=0)[:, None]
    out = jnp.zeros((halves, part, shards * tok // halves), jnp.bfloat16)

    def short(which, split):
        return short_convs(qkv, border, short_filter, shard_doc, live, which, split)

    def across(block, distance):
        return lax.ppermute(block, "ctx", [(i, i ^ distance) for i in range(shards)])

    (gated,) = short((1, 2), False)
    qkv, gated = lax.optimization_barrier((qkv, gated))
    queries = short((0,), True)
    gated = lax.all_to_all(gated, "ctx", 0, 0)
    queries = [queries[0]] + [across(queries[k], k) for k in range(1, CORES)]
    queries = pair_up(queries)
    cuts = [0, span // 2, span * 3 // 4, span]
    groups = [
        [near + h * span for near in range(low, high) for h in reversed(range(halves))]
        for low, high in zip(cuts, cuts[1:])
    ]
    order = [far for fars in groups for far in fars if far]
    got = {0: queries[0]}

    def launch(fars, after):
        blocks, after = lax.optimization_barrier(([queries[far] for far in fars], after))
        for far, block in zip(fars, blocks):
            got[far] = across(block, far * CORES)
        return after

    gated = launch(order[:FLYING], gated)
    conv = long_conv(gated, filt, direct, shard_doc, live)
    conv = launch(order[FLYING:], conv)
    arrived = [[got[far] for far in fars] for fars in groups]
    for fars, blocks in zip(groups, arrived):
        own, sent = gate(fars, blocks, conv, halves)
        wide = own.shape[1]
        first = (here // CORES) % span ^ fars[-1]
        start = first // (len(fars) // halves) * wide
        out = lax.dynamic_update_slice(out, own[None], (mine, 0, start))
        for d in range(1, halves):
            route = [(j, (j + d) % halves) for j in range(halves)]
            came = lax.ppermute(sent[d - 1], "ch", route)
            source = lax.rem(mine + halves - d, halves)
            out = lax.dynamic_update_slice(out, came[None], (source, 0, start))
    return out


def solution(mesh):
    return jax.shard_map(
        local,
        mesh=mesh,
        in_specs=(P(None, "ctx", "ch"), P(None, None, "ch"), P(None, "ch"), P("ch"), P(), P()),
        out_specs=P(None, "ctx", "ch"),
        check_vma=False,
    )
```

time: 194 us -> 137 us (0.71)
  the two profiles are of different devices: /device:TPU:10 before, /device:TPU:0 now
where the time goes in v1:
time: 137 us
  Pallas kernels  48.2 us (35%)
  waiting for transfers between devices  44.7 us (33%)
  starting transfers between devices  34.5 us (25%)
  local copies, waits for them, and re-layouts  9.19 us (7%)
    all_to_all x1, waiting for transfers between devices, local(): gated = lax.all_to_all(gated, 'ctx', 0, 0)  29.3 us
    pallas_call x1, Pallas kernels, long_conv(): pl.pallas_call(conv_kernel, grid=(width // chans,), in_specs=[smem, smem,...  26.1 us
    ppermute x8, starting transfers between devices, across(): lax.ppermute(block, 'ctx', [(i, i ^ distance) for i in range(shards)])  18.3 us
    pallas_call x2, Pallas kernels, short_convs(): pl.pallas_call(functools.partial(short_kernel, count), grid=(width // blo...  11.1 us
    ppermute x8, waiting for transfers between devices, across(): lax.ppermute(block, 'ctx', [(i, i ^ distance) for i in range(shards)])  10.5 us
    all_to_all x1, starting transfers between devices, local(): gated = lax.all_to_all(gated, 'ctx', 0, 0)  9.31 us
    pallas_call x3, Pallas kernels, gate(): pl.pallas_call(functools.partial(gate_kernel, fars), grid=(width // chans...  8.06 us
    ppermute x3, starting transfers between devices, local(): came = lax.ppermute(sent[d - 1], 'ch', route)  4.57 us
  transfers between devices with their start and end apart: 13, of which 6 were waited for; matrix products, arithmetic and copies ran while one was open for 2% of the time, Pallas kernels for 31%

profile of v1, /device:TPU:0, one launch (start us, length us, event | category | flops | bytes accessed | tf_op | source)
XLA Modules:
  0.0 136.7 jit_solution(15103877062742528180)
XLA Ops:
  0.0 0.9 slice.3
  0.9 2.4 %collective-permute-start = (bf16[3,2,2048]{2,1,0:T(2,128)(2,1)S(1)}, bf16[3,2,2048]{2,1,0:T(2,128)(2,1)S(1)}, u32[]{:S(2)}, u32[]{:S(2)}) collective-permute-start(bf16[3,2,2048]{2,1,0:T(2,128)(2,1)S(1)} %slice.3), channel_id=1, source_target_pairs={{0,2},{2,4},{4,6},{6,8},{8,10},{10,12},{12,14},{14,16},{16,18},{18... | collective-permute-start | bytes 73736 | tf_op jit(solution)/shard_map/ppermute | solution.py:313
  3.3 0.8 collective-permute-done.refs_0_.refs_1_
  4.7 6.4 %short_kv.1 = bf16[16,128,512]{2,1,0:T(8,128)(2,1)} custom-call(s32[16]{0:T(128)} %doc.5, s32[16]{0:T(128)} %live.5, bf16[3,2,2048]{2,1,0:T(2,128)(2,1)} %copy-done.14, bf16[3,2,2048]{2,1,0:T(2,128)(2,1)} %copy-done.14, f32[3,3,2048]{2,1,0:T(4,128)} %refs_1_.1, f32[3,3,2048]{2,1,0:T(4,128)} %refs_1_.1, bf16[3,512,2048]{2,1,0:T(8,128)(2,1)} %refs_2_.2, ...), custom_call_target="tpu_custom_call" | custom-call | tf_op jit(solution)/shard_map/short_kv/pallas_call | solution.py:71
  11.1 9.3 %all-to-all-start = ((bf16[16,128,512]{2,1,0:T(8,128)(2,1)}), bf16[16,128,512]{2,1,0:T(8,128)(2,1)S(1)}, u32[]{:S(2)}, u32[]{:S(2)}) async-start(bf16[16,128,512]{2,1,0:T(8,128)(2,1)} %short_kv.1), calls=%async_computation | async-start | bytes 4194304 | tf_op jit(solution)/shard_map/all_to_all | solution.py:329
  20.4 4.7 %short_q.1 = (bf16[8,128,512]{2,1,0:T(8,128)(2,1)}, bf16[8,128,512]{2,1,0:T(8,128)(2,1)}) custom-call(s32[16]{0:T(128)} %doc.5, s32[16]{0:T(128)} %live.5, bf16[3,2,2048]{2,1,0:T(2,128)(2,1)} %copy-done.14, f32[3,3,2048]{2,1,0:T(4,128)} %refs_1_.1, bf16[3,512,2048]{2,1,0:T(8,128)(2,1)} %refs_2_.2), custom_call_target="tpu_custom_call" | custom-call | tf_op jit(solution)/shard_map/short_q/pallas_call | solution.py:71
  25.6 0.7 copy.7.skip
  26.4 1.9 %constant_dynamic-slice_fusion.filt = bf16[2048,128]{1,0:T(8,128)(2,1)} fusion(bf16[2048,2048]{1,0:T(8,128)(2,1)} %param.8, s32[]{:T(128)S(6)} %select_n.48), kind=kLoop, calls=%fused_computation.6 | loop fusion | bytes 1048580 | tf_op jit(solution)/shard_map/dynamic_slice | solution.py:316
  28.2 1.0 copy-done.3
  29.2 3.0 %pair_up.1 = (bf16[2,128,512]{2,1,0:T(8,128)(2,1)}, bf16[2,128,512]{2,1,0:T(8,128)(2,1)}, bf16[2,128,512]{2,1,0:T(8,128)(2,1)}, bf16[2,128,512]{2,1,0:T(8,128)(2...) custom-call(bf16[8,128,512]{2,1,0:T(8,128)(2,1)} %get-tuple-element., ...), custom_call_target="tpu_custom_call" | custom-call | tf_op jit(solution)/shard_map/pair_up/pallas_call | solution.py:101
  32.2 29.3 %all-to-all-done.gated = bf16[16,128,512]{2,1,0:T(8,128)(2,1)S(1)} async-done(((bf16[16,128,512]{2,1,0:T(8,128)(2,1)}), bf16[16,128,512]{2,1,0:T(8,128)(2,1)S(1)}, u32[]{:S(2)}, u32[]{:S(2)}) %all-to-all-start) | async-done | bytes 2097184 | tf_op jit(solution)/shard_map/all_to_all | solution.py:329
  61.6 9.4 %collective-permute-start.2 = (bf16[2,128,512]{2,1,0:T(8,128)(2,1)}, bf16[2,128,512]{2,1,0:T(8,128)(2,1)S(1)}, u32[]{:S(2)}, u32[]{:S(2)}) collective-permute-start(bf16[2,128,512]{2,1,0:T(8,128)(2,1)} %get-tuple-element.41), channel_id=1, source_target_pairs={{0,16},{2,18},{4,20},{6,22},{8,24},{10,26},{12,28},{14,30},{16,0},... | collective-permute-start | bytes 786440 | tf_op jit(solution)/shard_map/ppermute | solution.py:324
  71.0 1.5 %collective-permute-start.4 = (bf16[2,128,512]{2,1,0:T(8,128)(2,1)}, bf16[2,128,512]{2,1,0:T(8,128)(2,1)S(1)}, u32[]{:S(2)}, u32[]{:S(2)}) collective-permute-start(bf16[2,128,512]{2,1,0:T(8,128)(2,1)} %get-tuple-element.44), channel_id=1, source_target_pairs={{0,4},{2,6},{4,0},{6,2},{8,12},{10,14},{12,8},{14,10},{16,20},{18,... | collective-permute-start | bytes 786440 | tf_op jit(solution)/shard_map/ppermute | solution.py:324
  72.5 26.1 %long_conv.1.refs_4_.refs_2_ = bf16[16,128,512]{2,1,0:T(8,128)(2,1)} custom-call(s32[16]{0:T(128)} %doc.5, s32[16]{0:T(128)} %live.5, f32[128,1]{1,0:T(8,128)} %copy.7.skip, bf16[2048,128]{1,0:T(8,128)(2,1)} %constant_dynamic-slice_fusion.filt, bf16[16,128,512]{2,1,0:T(8,128)(2,1)} %copy-done.2), custom_call_target="tpu_custom_call" | custom-call | flops 4294967296 | bytes 4718592 | tf_op jit(solution)/shard_map/long_conv/pallas_call | solution.py:218
  98.6 1.9 %collective-permute-start.6 = (bf16[2,128,512]{2,1,0:T(8,128)(2,1)S(1)}, bf16[2,128,512]{2,1,0:T(8,128)(2,1)S(1)}, u32[]{:S(2)}, u32[]{:S(2)}) collective-permute-start(bf16[2,128,512]{2,1,0:T(8,128)(2,1)S(1)} %copy-done.18), channel_id=1, source_target_pairs={{0,24},{2,26},{4,28},{6,30},{8,16},{10,18},{12,20},{14,22},{16,8},... | collective-permute-start | bytes 786440 | tf_op jit(solution)/shard_map/ppermute | solution.py:324
  100.5 1.5 %collective-permute-start.7 = (bf16[2,128,512]{2,1,0:T(8,128)(2,1)S(1)}, bf16[2,128,512]{2,1,0:T(8,128)(2,1)S(1)}, u32[]{:S(2)}, u32[]{:S(2)}) collective-permute-start(bf16[2,128,512]{2,1,0:T(8,128)(2,1)S(1)} %copy-done.17), channel_id=1, source_target_pairs={{0,8},{2,10},{4,12},{6,14},{8,0},{10,2},{12,4},{14,6},{16,24},{18,... | collective-permute-start | bytes 786440 | tf_op jit(solution)/shard_map/ppermute | solution.py:324
  102.0 2.0 %collective-permute-start.10 = (bf16[2,128,512]{2,1,0:T(8,128)(2,1)S(1)}, bf16[2,128,512]{2,1,0:T(8,128)(2,1)S(1)}, u32[]{:S(2)}, u32[]{:S(2)}) collective-permute-start(bf16[2,128,512]{2,1,0:T(8,128)(2,1)S(1)} %copy-done.16), channel_id=1, source_target_pairs={{0,12},{2,14},{4,8},{6,10},{8,4},{10,6},{12,0},{14,2},{16,28},{18,... | collective-permute-start | bytes 786440 | tf_op jit(solution)/shard_map/ppermute | solution.py:324
  104.0 1.5 %collective-permute-start.9 = (bf16[2,128,512]{2,1,0:T(8,128)(2,1)S(1)}, bf16[2,128,512]{2,1,0:T(8,128)(2,1)S(1)}, u32[]{:S(2)}, u32[]{:S(2)}) collective-permute-start(bf16[2,128,512]{2,1,0:T(8,128)(2,1)S(1)} %copy-done.15), channel_id=1, source_target_pairs={{0,28},{2,30},{4,24},{6,26},{8,20},{10,22},{12,16},{14,18},{16,12}... | collective-permute-start | bytes 786440 | tf_op jit(solution)/shard_map/ppermute | solution.py:324
  105.5 0.7 copy-done.11
  106.2 3.0 %gate.3 = (bf16[128,2048]{1,0:T(8,128)(2,1)}, bf16[1,128,2048]{2,1,0:T(8,128)(2,1)}) custom-call(bf16[2,128,512]{2,1,0:T(8,128)(2,1)} %copy-done.9, bf16[2,128,512]{2,1,0:T(8,128)(2,1)} %get-tuple-element.42.refs_1_, bf16[2,128,512]{2,1,0:T(8,128)(2,1)} %copy-done.10, bf16[2,128,512]{2,1,0:T(8,128)(2,1)} %copy-done.11, ...), custom_call_target="tpu_custom_call" | custom-call | tf_op jit(solution)/shard_map/gate/pallas_call | solution.py:286
  109.1 1.5 %collective-permute-start.5 = (bf16[128,2048]{1,0:T(8,128)(2,1)}, bf16[128,2048]{1,0:T(8,128)(2,1)S(1)}, u32[]{:S(2)}, u32[]{:S(2)}) collective-permute-start(bf16[128,2048]{1,0:T(8,128)(2,1)} %bitcast.17), channel_id=1, source_target_pairs={{0,1},{1,0},{2,3},{3,2},{4,5},{5,4},{6,7},{7,6},{8,9},{9,8},{10,11... | collective-permute-start | bytes 1572872 | tf_op jit(solution)/shard_map/ppermute | solution.py:358
  110.7 2.8 %collective-permute-done.7.refs_1_ = bf16[2,128,512]{2,1,0:T(8,128)(2,1)S(1)} collective-permute-done((bf16[2,128,512]{2,1,0:T(8,128)(2,1)S(1)}, bf16[2,128,512]{2,1,0:T(8,128)(2,1)S(1)}, u32[]{:S(2)}, u32[]{:S(2)}) %collective-permute-start.7) | collective-permute-done | bytes 262176 | tf_op jit(solution)/shard_map/ppermute | solution.py:324
  113.5 0.7 copy-done.8
  114.2 2.6 %gate.4 = (bf16[128,1024]{1,0:T(8,128)(2,1)}, bf16[1,128,1024]{2,1,0:T(8,128)(2,1)}) custom-call(bf16[2,128,512]{2,1,0:T(8,128)(2,1)} %copy-done.6, bf16[2,128,512]{2,1,0:T(8,128)(2,1)} %copy-done.8, bf16[16,128,512]{2,1,0:T(8,128)(2,1)} %long_conv.1.refs_4_.refs_2_), custom_call_target="tpu_custom_call" | custom-call | tf_op jit(solution)/shard_map/gate/pallas_call | solution.py:286
  116.8 1.5 %collective-permute-start.8 = (bf16[128,1024]{1,0:T(8,128)(2,1)}, bf16[128,1024]{1,0:T(8,128)(2,1)S(1)}, u32[]{:S(2)}, u32[]{:S(2)}) collective-permute-start(bf16[128,1024]{1,0:T(8,128)(2,1)} %bitcast.18), channel_id=1, source_target_pairs={{0,1},{1,0},{2,3},{3,2},{4,5},{5,4},{6,7},{7,6},{8,9},{9,8},{10,11... | collective-permute-start | bytes 786440 | tf_op jit(solution)/shard_map/ppermute | solution.py:358
  118.3 2.8 %collective-permute-done.10.refs_1_ = bf16[2,128,512]{2,1,0:T(8,128)(2,1)S(1)} collective-permute-done((bf16[2,128,512]{2,1,0:T(8,128)(2,1)S(1)}, bf16[2,128,512]{2,1,0:T(8,128)(2,1)S(1)}, u32[]{:S(2)}, u32[]{:S(2)}) %collective-permute-start.10) | collective-permute-done | bytes 262176 | tf_op jit(solution)/shard_map/ppermute | solution.py:324
  121.1 4.9 %collective-permute-done.9.refs_0_ = bf16[2,128,512]{2,1,0:T(8,128)(2,1)S(1)} collective-permute-done((bf16[2,128,512]{2,1,0:T(8,128)(2,1)S(1)}, bf16[2,128,512]{2,1,0:T(8,128)(2,1)S(1)}, u32[]{:S(2)}, u32[]{:S(2)}) %collective-permute-start.9) | collective-permute-done | bytes 262176 | tf_op jit(solution)/shard_map/ppermute | solution.py:324
  125.9 0.7 copy-done.7
  126.6 2.5 %gate.5 = (bf16[128,1024]{1,0:T(8,128)(2,1)}, bf16[1,128,1024]{2,1,0:T(8,128)(2,1)}) custom-call(bf16[2,128,512]{2,1,0:T(8,128)(2,1)} %copy-done.7, bf16[2,128,512]{2,1,0:T(8,128)(2,1)} %copy-done.5, bf16[16,128,512]{2,1,0:T(8,128)(2,1)} %long_conv.1.refs_4_.refs_2_), custom_call_target="tpu_custom_call" | custom-call | tf_op jit(solution)/shard_map/gate/pallas_call | solution.py:286
  129.2 1.5 %collective-permute-start.11 = (bf16[128,1024]{1,0:T(8,128)(2,1)}, bf16[128,1024]{1,0:T(8,128)(2,1)S(1)}, u32[]{:S(2)}, u32[]{:S(2)}) collective-permute-start(bf16[128,1024]{1,0:T(8,128)(2,1)} %bitcast.19), channel_id=1, source_target_pairs={{0,1},{1,0},{2,3},{3,2},{4,5},{5,4},{6,7},{7,6},{8,9},{9,8},{10,11... | collective-permute-start | bytes 786440 | tf_op jit(solution)/shard_map/ppermute | solution.py:358
  131.9 4.1 %collective-permute-done.11 = bf16[128,1024]{1,0:T(8,128)(2,1)S(1)} collective-permute-done((bf16[128,1024]{1,0:T(8,128)(2,1)}, bf16[128,1024]{1,0:T(8,128)(2,1)S(1)}, u32[]{:S(2)}, u32[]{:S(2)}) %collective-permute-start.11) | collective-permute-done | bytes 262176 | tf_op jit(solution)/shard_map/ppermute | solution.py:358
  136.0 0.7 bitcast_dynamic-update-slice_fusion.2
  (50 shorter events, 2.3 us)
Async XLA Ops:
  0.0 25.5 %copy-start = (f32[2048]{0:T(1024)S(1)}, f32[2048]{0:T(1024)}, u32[]{:S(2)}) copy-start(f32[2048]{0:T(1024)} %param.9) | copy-start | bytes 24580
  0.9 3.2 %collective-permute-start = (bf16[3,2,2048]{2,1,0:T(2,128)(2,1)S(1)}, bf16[3,2,2048]{2,1,0:T(2,128)(2,1)S(1)}, u32[]{:S(2)}, u32[]{:S(2)}) collective-permute-start(bf16[3,2,2048]{2,1,0:T(2,128)(2,1)S(1)} %slice.3), channel_id=1, source_target_pairs={{0,2},{2,4},{4,6},{6,8},{8,10},{10,12},{12,14},{14,16},{16,18},{18... | collective-permute-start | bytes 73736 | tf_op jit(solution)/shard_map/ppermute | solution.py:313
  4.1 0.6 copy-start.14
  11.1 50.4 %all-to-all-start = ((bf16[16,128,512]{2,1,0:T(8,128)(2,1)}), bf16[16,128,512]{2,1,0:T(8,128)(2,1)S(1)}, u32[]{:S(2)}, u32[]{:S(2)}) async-start(bf16[16,128,512]{2,1,0:T(8,128)(2,1)} %short_kv.1), calls=%async_computation | async-start | bytes 4194304 | tf_op jit(solution)/shard_map/all_to_all | solution.py:329
  25.1 3.1 %collective-permute-start.1 = (bf16[8,128,512]{2,1,0:T(8,128)(2,1)}, bf16[8,128,512]{2,1,0:T(8,128)(2,1)S(1)}, u32[]{:S(2)}, u32[]{:S(2)}) collective-permute-start(bf16[8,128,512]{2,1,0:T(8,128)(2,1)} %get-tuple-element.34), channel_id=1, source_target_pairs={{0,2},{2,0},{4,6},{6,4},{8,10},{10,8},{12,14},{14,12},{16,18},{18,... | collective-permute-start | bytes 3145736 | tf_op jit(solution)/shard_map/ppermute | solution.py:324
  28.2 1.0 copy-start.3
  61.5 11.0 %copy-start.2 = (bf16[16,128,512]{2,1,0:T(8,128)(2,1)}, bf16[16,128,512]{2,1,0:T(8,128)(2,1)S(1)}, u32[]{:S(2)}) copy-start(bf16[16,128,512]{2,1,0:T(8,128)(2,1)S(1)} %all-to-all-done.gated) | copy-start | bytes 6291460
  61.5 37.1 %copy-start.18 = (bf16[2,128,512]{2,1,0:T(8,128)(2,1)S(1)}, bf16[2,128,512]{2,1,0:T(8,128)(2,1)}, u32[]{:S(2)}) copy-start(bf16[2,128,512]{2,1,0:T(8,128)(2,1)} %get-tuple-element.51) | copy-start | bytes 786436
  61.5 38.9 %copy-start.17 = (bf16[2,128,512]{2,1,0:T(8,128)(2,1)S(1)}, bf16[2,128,512]{2,1,0:T(8,128)(2,1)}, u32[]{:S(2)}) copy-start(bf16[2,128,512]{2,1,0:T(8,128)(2,1)} %get-tuple-element.52) | copy-start | bytes 786436
  61.5 40.5 %copy-start.16 = (bf16[2,128,512]{2,1,0:T(8,128)(2,1)S(1)}, bf16[2,128,512]{2,1,0:T(8,128)(2,1)}, u32[]{:S(2)}) copy-start(bf16[2,128,512]{2,1,0:T(8,128)(2,1)} %get-tuple-element.56) | copy-start | bytes 786436
  61.5 42.5 %copy-start.15 = (bf16[2,128,512]{2,1,0:T(8,128)(2,1)S(1)}, bf16[2,128,512]{2,1,0:T(8,128)(2,1)}, u32[]{:S(2)}) copy-start(bf16[2,128,512]{2,1,0:T(8,128)(2,1)} %get-tuple-element.55) | copy-start | bytes 786436
  61.6 40.5 %collective-permute-start.2 = (bf16[2,128,512]{2,1,0:T(8,128)(2,1)}, bf16[2,128,512]{2,1,0:T(8,128)(2,1)S(1)}, u32[]{:S(2)}, u32[]{:S(2)}) collective-permute-start(bf16[2,128,512]{2,1,0:T(8,128)(2,1)} %get-tuple-element.41), channel_id=1, source_target_pairs={{0,16},{2,18},{4,20},{6,22},{8,24},{10,26},{12,28},{14,30},{16,0},... | collective-permute-start | bytes 786440 | tf_op jit(solution)/shard_map/ppermute | solution.py:324
  71.0 33.0 %collective-permute-start.3 = (bf16[2,128,512]{2,1,0:T(8,128)(2,1)}, bf16[2,128,512]{2,1,0:T(8,128)(2,1)S(1)}, u32[]{:S(2)}, u32[]{:S(2)}) collective-permute-start(bf16[2,128,512]{2,1,0:T(8,128)(2,1)} %get-tuple-element.43), channel_id=1, source_target_pairs={{0,20},{2,22},{4,16},{6,18},{8,28},{10,30},{12,24},{14,26},{16,4},... | collective-permute-start | bytes 786440 | tf_op jit(solution)/shard_map/ppermute | solution.py:324
  71.0 34.5 %collective-permute-start.4 = (bf16[2,128,512]{2,1,0:T(8,128)(2,1)}, bf16[2,128,512]{2,1,0:T(8,128)(2,1)S(1)}, u32[]{:S(2)}, u32[]{:S(2)}) collective-permute-start(bf16[2,128,512]{2,1,0:T(8,128)(2,1)} %get-tuple-element.44), channel_id=1, source_target_pairs={{0,4},{2,6},{4,0},{6,2},{8,12},{10,14},{12,8},{14,10},{16,20},{18,... | collective-permute-start | bytes 786440 | tf_op jit(solution)/shard_map/ppermute | solution.py:324
  98.6 12.1 %collective-permute-start.6 = (bf16[2,128,512]{2,1,0:T(8,128)(2,1)S(1)}, bf16[2,128,512]{2,1,0:T(8,128)(2,1)S(1)}, u32[]{:S(2)}, u32[]{:S(2)}) collective-permute-start(bf16[2,128,512]{2,1,0:T(8,128)(2,1)S(1)} %copy-done.18), channel_id=1, source_target_pairs={{0,24},{2,26},{4,28},{6,30},{8,16},{10,18},{12,20},{14,22},{16,8},... | collective-permute-start | bytes 786440 | tf_op jit(solution)/shard_map/ppermute | solution.py:324
  100.5 13.0 %collective-permute-start.7 = (bf16[2,128,512]{2,1,0:T(8,128)(2,1)S(1)}, bf16[2,128,512]{2,1,0:T(8,128)(2,1)S(1)}, u32[]{:S(2)}, u32[]{:S(2)}) collective-permute-start(bf16[2,128,512]{2,1,0:T(8,128)(2,1)S(1)} %copy-done.17), channel_id=1, source_target_pairs={{0,8},{2,10},{4,12},{6,14},{8,0},{10,2},{12,4},{14,6},{16,24},{18,... | collective-permute-start | bytes 786440 | tf_op jit(solution)/shard_map/ppermute | solution.py:324
  102.0 3.5 %copy-start.9 = (bf16[2,128,512]{2,1,0:T(8,128)(2,1)}, bf16[2,128,512]{2,1,0:T(8,128)(2,1)S(1)}, u32[]{:S(2)}) copy-start(bf16[2,128,512]{2,1,0:T(8,128)(2,1)S(1)} %collective-permute-done.2.refs_0_) | copy-start | bytes 786436
  102.0 19.0 %collective-permute-start.10 = (bf16[2,128,512]{2,1,0:T(8,128)(2,1)S(1)}, bf16[2,128,512]{2,1,0:T(8,128)(2,1)S(1)}, u32[]{:S(2)}, u32[]{:S(2)}) collective-permute-start(bf16[2,128,512]{2,1,0:T(8,128)(2,1)S(1)} %copy-done.16), channel_id=1, source_target_pairs={{0,12},{2,14},{4,8},{6,10},{8,4},{10,6},{12,0},{14,2},{16,28},{18,... | collective-permute-start | bytes 786440 | tf_op jit(solution)/shard_map/ppermute | solution.py:324
  104.0 1.5 %copy-start.10 = (bf16[2,128,512]{2,1,0:T(8,128)(2,1)}, bf16[2,128,512]{2,1,0:T(8,128)(2,1)S(1)}, u32[]{:S(2)}) copy-start(bf16[2,128,512]{2,1,0:T(8,128)(2,1)S(1)} %collective-permute-done.3.refs_2_) | copy-start | bytes 786436
  104.0 21.9 %collective-permute-start.9 = (bf16[2,128,512]{2,1,0:T(8,128)(2,1)S(1)}, bf16[2,128,512]{2,1,0:T(8,128)(2,1)S(1)}, u32[]{:S(2)}, u32[]{:S(2)}) collective-permute-start(bf16[2,128,512]{2,1,0:T(8,128)(2,1)S(1)} %copy-done.15), channel_id=1, source_target_pairs={{0,28},{2,30},{4,24},{6,26},{8,20},{10,22},{12,16},{14,18},{16,12}... | collective-permute-start | bytes 786440 | tf_op jit(solution)/shard_map/ppermute | solution.py:324
  105.5 0.7 copy-start.11
  109.1 21.9 %collective-permute-start.5 = (bf16[128,2048]{1,0:T(8,128)(2,1)}, bf16[128,2048]{1,0:T(8,128)(2,1)S(1)}, u32[]{:S(2)}, u32[]{:S(2)}) collective-permute-start(bf16[128,2048]{1,0:T(8,128)(2,1)} %bitcast.17), channel_id=1, source_target_pairs={{0,1},{1,0},{2,3},{3,2},{4,5},{5,4},{6,7},{7,6},{8,9},{9,8},{10,11... | collective-permute-start | bytes 1572872 | tf_op jit(solution)/shard_map/ppermute | solution.py:358
  110.7 2.8 %copy-start.6 = (bf16[2,128,512]{2,1,0:T(8,128)(2,1)}, bf16[2,128,512]{2,1,0:T(8,128)(2,1)S(1)}, u32[]{:S(2)}) copy-start(bf16[2,128,512]{2,1,0:T(8,128)(2,1)S(1)} %collective-permute-done.6.refs_0_) | copy-start | bytes 786436
  113.5 0.7 copy-start.8
  116.8 14.2 %copy-start.4 = (bf16[128,2048]{1,0:T(8,128)(2,1)S(1)}, bf16[128,2048]{1,0:T(8,128)(2,1)}, u32[]{:S(2)}) copy-start(bf16[128,2048]{1,0:T(8,128)(2,1)} %get-tuple-element.49) | copy-start | bytes 1572868
  116.8 14.9 %collective-permute-start.8 = (bf16[128,1024]{1,0:T(8,128)(2,1)}, bf16[128,1024]{1,0:T(8,128)(2,1)S(1)}, u32[]{:S(2)}, u32[]{:S(2)}) collective-permute-start(bf16[128,1024]{1,0:T(8,128)(2,1)} %bitcast.18), channel_id=1, source_target_pairs={{0,1},{1,0},{2,3},{3,2},{4,5},{5,4},{6,7},{7,6},{8,9},{9,8},{10,11... | collective-permute-start | bytes 786440 | tf_op jit(solution)/shard_map/ppermute | solution.py:358
  121.1 4.9 %copy-start.5 = (bf16[2,128,512]{2,1,0:T(8,128)(2,1)}, bf16[2,128,512]{2,1,0:T(8,128)(2,1)S(1)}, u32[]{:S(2)}) copy-start(bf16[2,128,512]{2,1,0:T(8,128)(2,1)S(1)} %collective-permute-done.10.refs_1_) | copy-start | bytes 786436
  125.9 0.7 copy-start.7
  129.2 6.8 %collective-permute-start.11 = (bf16[128,1024]{1,0:T(8,128)(2,1)}, bf16[128,1024]{1,0:T(8,128)(2,1)S(1)}, u32[]{:S(2)}, u32[]{:S(2)}) collective-permute-start(bf16[128,1024]{1,0:T(8,128)(2,1)} %bitcast.19), channel_id=1, source_target_pairs={{0,1},{1,0},{2,3},{3,2},{4,5},{5,4},{6,7},{7,6},{8,9},{9,8},{10,11... | collective-permute-start | bytes 786440 | tf_op jit(solution)/shard_map/ppermute | solution.py:358
  130.7 0.9 copy-start.12
  130.9 1.0 copy-start.13
  131.9 4.1 %copy-start.1 = (bf16[2,128,4096]{2,1,0:T(8,128)(2,1)}, bf16[2,128,4096]{2,1,0:T(8,128)(2,1)S(1)}, u32[]{:S(2)}) copy-start(bf16[2,128,4096]{2,1,0:T(8,128)(2,1)S(1)} %bitcast_dynamic-update-slice_fusion.3) | copy-start | bytes 6291460

commit v2 on v1

--- a/solution.py
+++ b/solution.py
@@ -11,25 +11,34 @@
 UNROLL = 8
 ROWS = 64
 CORES = 2
-FLYING = 5
+FLYING = 6
+CHANS = 32
 VMEM = 56 << 20
 
 
-def short_kernel(count, doc, live, *refs):
-    borders, taps, slabs = refs[:count], refs[count : 2 * count], refs[2 * count : 3 * count]
-    outs, tall, turned = refs[3 * count : -2], refs[-2], refs[-1]
+def shard_facts(doc, live, tok):
     shards = doc.shape[0]
     here = lax.axis_index("ctx")
-    tok = slabs[0].shape[1]
     before = jnp.maximum(here - 1, 0)
     after = jnp.minimum(here + 1, shards - 1)
     joined = (here > 0) & (doc[before] == doc[here])
     closing = (here == shards - 1) | (doc[after] != doc[here])
-    limit = jnp.where(closing, live[here], tok)
+    return joined, jnp.where(closing, live[here], tok)
+
+
+def short_kernel(count, edges, doc, live, *refs):
+    taps, slabs = refs[:count], refs[count : 2 * count]
+    borders, refs = refs[2 * count : 2 * count + edges], refs[2 * count + edges :]
+    outs, tall, turned = refs[:-2], refs[-2], refs[-1]
+    here = lax.axis_index("ctx")
+    tok = slabs[0].shape[1]
+    joined, limit = shard_facts(doc, live, tok)
 
     def short(a):
         x = slabs[a][0].astype(jnp.float32)
-        edge = jnp.where(joined, borders[a][0].astype(jnp.float32), 0.0)
+        edge = jnp.zeros((2, x.shape[1]), jnp.float32)
+        if edges:
+            edge = jnp.where(joined, borders[a][0].astype(jnp.float32), 0.0)
         tall[a, 6:8, :] = edge
         tall[a, pl.ds(8, tok), :] = x
         once = tall[a, pl.ds(7, tok), :]
@@ -55,13 +64,14 @@
                 out[j] = turned[pl.ds(pl.multiple_of(row, part), part), :]
 
 
-def short_convs(qkv, border, short_filter, shard_doc, live, which, split):
+def short_convs(qkv, short_filter, shard_doc, live, which, split, border=None):
     _, tok, width = qkv.shape
     shards = shard_doc.shape[0]
     part = width // shards
     block = min(width, 512)
     smem = pl.BlockSpec(memory_space=pltpu.SMEM)
     count = len(which)
+    borders = [] if border is None else [border] * count
 
     def spec(rows, a):
         return pl.BlockSpec((1, rows, block), lambda i: (a, 0, i))
@@ -69,12 +79,12 @@
     many = CORES if split else 1
     rows = block // part // many
     return pl.pallas_call(
-        functools.partial(short_kernel, count),
+        functools.partial(short_kernel, count, len(borders)),
         grid=(width // block,),
         in_specs=[smem] * 2
-        + [spec(2, a) for a in which]
         + [spec(3, a) for a in which]
-        + [spec(tok, a) for a in which],
+        + [spec(tok, a) for a in which]
+        + [spec(2, a) for a in which if border is not None],
         out_specs=[pl.BlockSpec((rows, part, tok), lambda i: (i, 0, 0))] * many,
         out_shape=[jax.ShapeDtypeStruct((shards // many, part, tok), jnp.bfloat16)] * many,
         scratch_shapes=[
@@ -83,7 +93,47 @@
         ],
         compiler_params=pltpu.CompilerParams(vmem_limit_bytes=VMEM),
         name="short_" + "".join("qkv"[a] for a in which),
-    )(shard_doc, live, *[border] * count, *[short_filter] * count, *[qkv] * count)
+    )(shard_doc, live, *[short_filter] * count, *[qkv] * count, *borders)
+
+
+def first_kernel(doc, live, key_edge, value_edge, key_taps, value_taps, key, value, old, out):
+    shards, part, _ = old.shape
+    tok = 2
+    joined, limit = shard_facts(doc, live, tok)
+
+    def short(edge, taps, slab):
+        x = slab[0, :tok, :].astype(jnp.float32)
+        edge = jnp.where(joined, edge[0].astype(jnp.float32), 0.0)
+        once = jnp.concatenate([edge[1:], x[:1]], axis=0)
+        return taps[0, 0:1, :] * x + taps[0, 1:2, :] * once + taps[0, 2:3, :] * edge
+
+    keep = jnp.where(lax.broadcasted_iota(jnp.int32, (tok, 1), 0) < limit, 1.0, 0.0)
+    both = short(key_edge, key_taps, key) * short(value_edge, value_taps, value) * keep
+    tall = jnp.concatenate([both, jnp.zeros((LANES - tok, both.shape[1]), jnp.float32)], axis=0)
+    new = tall.astype(jnp.bfloat16).T.reshape(shards, part, LANES)
+    place = lax.broadcasted_iota(jnp.int32, new.shape, 2)
+    out[...] = jnp.where(place < tok, new, old[...])
+
+
+def first_tokens(gated, qkv, border, short_filter, shard_doc, live):
+    shards, part, _ = gated.shape
+    width = shards * part
+    smem = pl.BlockSpec(memory_space=pltpu.SMEM)
+
+    def spec(rows, a):
+        return pl.BlockSpec((1, rows, width), lambda i: (a, 0, 0))
+
+    tile = pl.BlockSpec((shards, part, LANES), lambda i: (0, 0, 0))
+    return pl.pallas_call(
+        first_kernel,
+        grid=(1,),
+        in_specs=[smem] * 2 + [spec(rows, a) for rows in (2, 3, 16) for a in (1, 2)] + [tile],
+        out_specs=tile,
+        out_shape=jax.ShapeDtypeStruct(gated.shape, gated.dtype),
+        input_output_aliases={8: 0},
+        compiler_params=pltpu.CompilerParams(vmem_limit_bytes=VMEM),
+        name="first_tokens",
+    )(shard_doc, live, *[border] * 2, *[short_filter] * 2, *[qkv] * 2, gated)
 
 
 def pair_up_kernel(*refs):
@@ -108,7 +158,48 @@
     )(*blocks)
 
 
-def conv_kernel(doc, live, skip, filt, gated, out, taps, masks, wide, one, late, mixed):
+def prepare_kernel(filt, out, taps):
+    step = pl.program_id(0)
+    chans, rows, width = out.shape
+
+    @pl.when(step == 0)
+    def _():
+        taps[...] = filt[...].astype(jnp.float32).T
+
+    def channel(c, _):
+        row = taps[pl.ds(step * chans + c, 1), :]
+        row = jnp.concatenate([row, jnp.zeros((1, width), jnp.float32)], axis=1)
+        spread = jnp.broadcast_to(row, (16, row.shape[1]))
+        band = pltpu.roll(spread, 0, 1, stride=1, stride_axis=0).astype(jnp.bfloat16)
+        bands = [band] + [pltpu.roll(band, 16 * q, 1) for q in range(1, ROWS // 16)]
+        toeplitz = jnp.concatenate(bands, axis=0)
+        for k in range(rows // ROWS):
+            out[c, k * ROWS : (k + 1) * ROWS, :] = toeplitz[:, k * width : (k + 1) * width]
+        return 0
+
+    lax.fori_loop(0, chans, channel, 0, unroll=4)
+
+
+def prepare(filt):
+    lags, part = filt.shape
+    chans = min(CHANS, part)
+    width = 4 * ROWS
+    rows = (lags // width + 1) * ROWS
+    return pl.pallas_call(
+        prepare_kernel,
+        grid=(part // chans,),
+        in_specs=[pl.BlockSpec((lags, part), lambda i: (0, 0))],
+        out_specs=pl.BlockSpec((chans, rows, width), lambda i: (i, 0, 0)),
+        out_shape=jax.ShapeDtypeStruct((part, rows, width), jnp.bfloat16),
+        scratch_shapes=[pltpu.VMEM((part, lags), jnp.float32)],
+        compiler_params=pltpu.CompilerParams(
+            vmem_limit_bytes=VMEM, dimension_semantics=("arbitrary",)
+        ),
+        name="prepare",
+    )(filt)
+
+
+def conv_kernel(doc, live, skip, toeplitz, gated, out, masks, wide, one, late, mixed):
     shards, chans, tok = gated.shape
     pitch = chans + 1
     per = tok // LANES
@@ -117,12 +208,10 @@
     pairs = masks.shape[0] - 1
     pad = 8 * (pairs - 1)
     step = pl.program_id(0)
-    lags = taps.shape[1]
-    spans = lags // (4 * ROWS) + 1
+    depth = toeplitz.shape[1]
 
     @pl.when(step == 0)
     def _():
-        taps[...] = filt[...].astype(jnp.float32).T
         wide[pl.ds(0, pad * pitch), :] = jnp.zeros((pad * pitch, LANES), jnp.float32)
         late[:, pl.ds(0, 8), :] = jnp.zeros((late.shape[0], 8, LANES), jnp.float32)
         start = jnp.int32(0)
@@ -151,22 +240,15 @@
             older = [older[1], (here, turned)]
 
     def channel(c, slot):
-        row = taps[pl.ds(step * chans + c, 1), :]
-        row = jnp.concatenate([row, jnp.zeros((1, 4 * ROWS), jnp.float32)], axis=1)
-        spread = jnp.broadcast_to(row, (16, row.shape[1]))
-        band = pltpu.roll(spread, 0, 1, stride=1, stride_axis=0).astype(jnp.bfloat16)
-        bands = [band] + [pltpu.roll(band, 16 * q, 1) for q in range(1, ROWS // 16)]
-        toeplitz = jnp.concatenate(bands, axis=0)
-        slices = [toeplitz[:, k * 4 * ROWS : (k + 1) * 4 * ROWS] for k in range(spans)]
-        slices += [jnp.zeros_like(slices[0])] * (2 * pairs - spans)
-        weights = jnp.concatenate(slices, axis=0)
         one[slot] = wide[pl.ds(c, blocks + pad, stride=pitch), :]
         lagged = [
             one[slot, pl.ds(pad - 8 * m, blocks), :].astype(jnp.bfloat16) * masks[m]
             for m in range(pairs)
         ]
         sums = jnp.dot(
-            jnp.concatenate(lagged, axis=1), weights, preferred_element_type=jnp.float32
+            jnp.concatenate(lagged, axis=1)[:, :depth],
+            toeplitz[c],
+            preferred_element_type=jnp.float32,
         )
         late[slot, pl.ds(8, blocks), :] = sums[:, LANES:]
         behind = late[slot, pl.ds(6, blocks), :] * masks[pairs].astype(jnp.float32)
@@ -206,12 +288,12 @@
         out[s] = total.astype(jnp.bfloat16)
 
 
-def long_conv(gated, filt, skip, shard_doc, live):
+def long_conv(gated, toeplitz, skip, shard_doc, live):
     shards, width, tok = gated.shape
-    lags, part = filt.shape
-    chans = min(32, width)
+    depth = toeplitz.shape[1]
+    chans = min(CHANS, width)
     blocks = shards * tok // ROWS
-    pairs = (lags // (4 * ROWS) + 2) // 2
+    pairs = (depth // ROWS + 1) // 2
     tall = blocks + 8 * (pairs - 1)
     smem = pl.BlockSpec(memory_space=pltpu.SMEM)
     slab = pl.BlockSpec((shards, chans, tok), lambda i: (0, i, 0))
@@ -222,13 +304,12 @@
             smem,
             smem,
             pl.BlockSpec((chans, 1), lambda i: (i, 0)),
-            pl.BlockSpec((lags, part), lambda i: (0, 0)),
+            pl.BlockSpec((chans, depth, 4 * ROWS), lambda i: (i, 0, 0)),
             slab,
         ],
         out_specs=slab,
         out_shape=jax.ShapeDtypeStruct((shards, width, tok), jnp.bfloat16),
         scratch_shapes=[
-            pltpu.VMEM((part, lags), jnp.float32),
             pltpu.VMEM((pairs + 1, blocks, LANES), jnp.bfloat16),
             pltpu.VMEM((tall * (chans + 1), LANES), jnp.float32),
             pltpu.VMEM((UNROLL, tall, LANES), jnp.float32),
@@ -238,13 +319,9 @@
         compiler_params=pltpu.CompilerParams(
             vmem_limit_bytes=VMEM, dimension_semantics=("arbitrary",)
         ),
-        cost_estimate=pl.CostEstimate(
-            flops=2 * width * shards * tok * lags,
-            bytes_accessed=width * shards * tok * 4 + lags * part * 2,
-            transcendentals=0,
-        ),
+        cost_estimate=pl.CostEstimate(flops=1, bytes_accessed=1, transcendentals=0),
         name="long_conv",
-    )(shard_doc, live, skip, filt, gated)
+    )(shard_doc, live, skip, toeplitz, gated)
 
 
 def gate_kernel(fars, *refs):
@@ -297,6 +374,7 @@
             jax.ShapeDtypeStruct((halves - 1, width, wide), jnp.bfloat16),
         ],
         compiler_params=pltpu.CompilerParams(vmem_limit_bytes=VMEM),
+        cost_estimate=pl.CostEstimate(flops=1, bytes_accessed=1, transcendentals=0),
         name="gate",
     )(*blocks, conv)
 
@@ -315,17 +393,16 @@
     )
     filt = lax.dynamic_slice_in_dim(long_filter, here * part, part, axis=1)
     direct = lax.dynamic_slice_in_dim(skip, here * part, part, axis=0)[:, None]
+    toeplitz = prepare(filt)
     out = jnp.zeros((halves, part, shards * tok // halves), jnp.bfloat16)
-
-    def short(which, split):
-        return short_convs(qkv, border, short_filter, shard_doc, live, which, split)
 
     def across(block, distance):
         return lax.ppermute(block, "ctx", [(i, i ^ distance) for i in range(shards)])
 
-    (gated,) = short((1, 2), False)
+    (gated,) = short_convs(qkv, short_filter, shard_doc, live, (1, 2), False)
+    gated = first_tokens(gated, qkv, border, short_filter, shard_doc, live)
     qkv, gated = lax.optimization_barrier((qkv, gated))
-    queries = short((0,), True)
+    queries = short_convs(qkv, short_filter, shard_doc, live, (0,), True, border)
     gated = lax.all_to_all(gated, "ctx", 0, 0)
     queries = [queries[0]] + [across(queries[k], k) for k in range(1, CORES)]
     queries = pair_up(queries)
@@ -335,6 +412,7 @@
         for low, high in zip(cuts, cuts[1:])
     ]
     order = [far for fars in groups for far in fars if far]
+    order = sorted(order, key=lambda far: far != 1)
     got = {0: queries[0]}
 
     def launch(fars, after):
@@ -343,9 +421,15 @@
             got[far] = across(block, far * CORES)
         return after
 
-    gated = launch(order[:FLYING], gated)
-    conv = long_conv(gated, filt, direct, shard_doc, live)
-    conv = launch(order[FLYING:], conv)
+    early = [1, span]
+    for far in early:
+        got[far] = across(queries[far], far * CORES)
+    order = [far for far in order if far not in early]
+    middle = order[: 3 * len(order) // 5]
+    gated, toeplitz = launch(middle, (gated, toeplitz))
+    got[1], gated = lax.optimization_barrier((got[1], gated))
+    conv = long_conv(gated, toeplitz, direct, shard_doc, live)
+    conv = launch([far for far in order if far not in middle], conv)
     arrived = [[got[far] for far in fars] for fars in groups]
     for fars, blocks in zip(groups, arrived):
         own, sent = gate(fars, blocks, conv, halves)

time: 137 us -> 130 us (0.949)
  waiting for transfers between devices: 44.7 us -> 19.3 us
  Pallas kernels: 48.2 us -> 67.3 us
    pallas_call x2 -> x4, Pallas kernels: 11.1 us -> 37.7 us  [the longest x1 24.4 us: prepare(): pl.pallas_call(prepare_kernel, grid=(part // chans,), in_specs=[pl.BlockS...]
    all_to_all x1, waiting for transfers between devices: 29.3 us -> 4.57 us  [local(): gated = lax.all_to_all(gated, 'ctx', 0, 0)]
    pallas_call x1, Pallas kernels: 26.1 us -> 18.6 us  [long_conv(): pl.pallas_call(conv_kernel, grid=(width // chans,), in_specs=[smem, smem,...]
    ppermute x3, waiting for transfers between devices: 4.06 us -> 10.7 us  [local(): came = lax.ppermute(sent[d - 1], 'ch', route)]
    ppermute x8, waiting for transfers between devices: 10.5 us -> 4.01 us  [across(): lax.ppermute(block, 'ctx', [(i, i ^ distance) for i in range(shards)])]
    ppermute x8, starting transfers between devices: 18.3 us -> 20.4 us  [across(): lax.ppermute(block, 'ctx', [(i, i ^ distance) for i in range(shards)])]
    all_to_all x1, starting transfers between devices: 9.31 us -> 7.19 us  [local(): gated = lax.all_to_all(gated, 'ctx', 0, 0)]
    unnamed x38 -> x30, local copies, waits for them, and re-layouts: 4.44 us -> 4.4 us
  transfers between devices with their start and end apart: 13 -> 13, of which waited for: 6 -> 6; matrix products, arithmetic and copies ran while one was open for 2% -> 2% of each run, Pallas kernels for 31% -> 50%
where the time goes in v2:
time: 130 us; the launch traced here: 129 us
  Pallas kernels  67.3 us (52%)
  starting transfers between devices  33.5 us (26%)
  waiting for transfers between devices  19.3 us (15%)
  local copies, waits for them, and re-layouts  9.16 us (7%)
    pallas_call x1, Pallas kernels, prepare(): pl.pallas_call(prepare_kernel, grid=(part // chans,), in_specs=[pl.BlockS...  24.4 us
    ppermute x8, starting transfers between devices, across(): lax.ppermute(block, 'ctx', [(i, i ^ distance) for i in range(shards)])  20.4 us
    pallas_call x1, Pallas kernels, long_conv(): pl.pallas_call(conv_kernel, grid=(width // chans,), in_specs=[smem, smem,...  18.6 us
    pallas_call x2, Pallas kernels, short_convs(): pl.pallas_call(functools.partial(short_kernel, count, len(borders)), grid...  11 us
    ppermute x3, waiting for transfers between devices, local(): came = lax.ppermute(sent[d - 1], 'ch', route)  10.7 us
    pallas_call x3, Pallas kernels, gate(): pl.pallas_call(functools.partial(gate_kernel, fars), grid=(width // chans...  8.05 us
    all_to_all x1, starting transfers between devices, local(): gated = lax.all_to_all(gated, 'ctx', 0, 0)  7.19 us
    all_to_all x1, waiting for transfers between devices, local(): gated = lax.all_to_all(gated, 'ctx', 0, 0)  4.57 us
  transfers between devices with their start and end apart: 13, of which 6 were waited for; matrix products, arithmetic and copies ran while one was open for 2% of the time, Pallas kernels for 50%

profile of v2, /device:TPU:0, one launch (start us, length us, event | category | flops | bytes accessed | tf_op | source)
XLA Modules:
  0.0 129.4 jit_solution(8228629732078044466)
XLA Ops:
  0.0 0.9 slice.3
  0.9 2.4 %collective-permute-start = (bf16[3,2,2048]{2,1,0:T(2,128)(2,1)S(1)}, bf16[3,2,2048]{2,1,0:T(2,128)(2,1)S(1)}, u32[]{:S(2)}, u32[]{:S(2)}) collective-permute-start(bf16[3,2,2048]{2,1,0:T(2,128)(2,1)S(1)} %slice.3), channel_id=1, source_target_pairs={{0,2},{2,4},{4,6},{6,8},{8,10},{10,12},{12,14},{14,16},{16,18},{18... | collective-permute-start | bytes 73736 | tf_op jit(solution)/shard_map/ppermute | solution.py:391
  3.3 6.4 %short_kv.1.old = bf16[16,128,512]{2,1,0:T(8,128)(2,1)} custom-call(s32[16]{0:T(128)} %doc.7, s32[16]{0:T(128)} %live.7, f32[3,3,2048]{2,1,0:T(4,128)} %refs_0_.3, f32[3,3,2048]{2,1,0:T(4,128)} %refs_0_.3, bf16[3,512,2048]{2,1,0:T(8,128)(2,1)} %refs_1_.2, bf16[3,512,2048]{2,1,0:T(8,128)(2,1)} %refs_1_.2), custom_call_target="tpu_custom_call" | custom-call | tf_op jit(solution)/shard_map/short_kv/pallas_call | solution.py:81
  10.3 2.2 %first_tokens.1 = bf16[16,128,512]{2,1,0:T(8,128)(2,1)} custom-call(s32[16]{0:T(128)} %doc.7, s32[16]{0:T(128)} %live.7, bf16[3,2,2048]{2,1,0:T(2,128)(2,1)} %copy-done.14, bf16[3,2,2048]{2,1,0:T(2,128)(2,1)} %copy-done.14, f32[3,3,2048]{2,1,0:T(4,128)} %refs_0_.3, f32[3,3,2048]{2,1,0:T(4,128)} %refs_0_.3, ...), custom_call_target="tpu_custom_call", output_to_operand_aliasing={{}: (8, {})} | custom-call | tf_op jit(solution)/shard_map/first_tokens/pallas_call | solution.py:127
  12.5 7.2 %all-to-all-start = ((bf16[16,128,512]{2,1,0:T(8,128)(2,1)}), bf16[16,128,512]{2,1,0:T(8,128)(2,1)S(1)}, u32[]{:S(2)}, u32[]{:S(2)}) async-start(bf16[16,128,512]{2,1,0:T(8,128)(2,1)} %first_tokens.1), calls=%async_computation | async-start | bytes 4194304 | tf_op jit(solution)/shard_map/all_to_all | solution.py:406
  19.7 4.7 %short_q.1 = (bf16[8,128,512]{2,1,0:T(8,128)(2,1)}, bf16[8,128,512]{2,1,0:T(8,128)(2,1)}) custom-call(s32[16]{0:T(128)} %doc.7, s32[16]{0:T(128)} %live.7, f32[3,3,2048]{2,1,0:T(4,128)} %refs_0_.3, bf16[3,512,2048]{2,1,0:T(8,128)(2,1)} %refs_1_.2, bf16[3,2,2048]{2,1,0:T(2,128)(2,1)} %copy-done.14), custom_call_target="tpu_custom_call" | custom-call | tf_op jit(solution)/shard_map/short_q/pallas_call | solution.py:81
  24.8 2.5 %collective-permute-done.1.refs_1_ = bf16[8,128,512]{2,1,0:T(8,128)(2,1)S(1)} collective-permute-done((bf16[8,128,512]{2,1,0:T(8,128)(2,1)}, bf16[8,128,512]{2,1,0:T(8,128)(2,1)S(1)}, u32[]{:S(2)}, u32[]{:S(2)}) %collective-permute-start.1) | collective-permute-done | bytes 1048608 | tf_op jit(solution)/shard_map/ppermute | solution.py:400
  27.3 1.0 copy-done.3
  28.3 3.0 %pair_up.1 = (bf16[2,128,512]{2,1,0:T(8,128)(2,1)}, bf16[2,128,512]{2,1,0:T(8,128)(2,1)}, bf16[2,128,512]{2,1,0:T(8,128)(2,1)}, bf16[2,128,512]{2,1,0:T(8,128)(2...) custom-call(bf16[8,128,512]{2,1,0:T(8,128)(2,1)} %get-tuple-element., ...), custom_call_target="tpu_custom_call" | custom-call | tf_op jit(solution)/shard_map/pair_up/pallas_call | solution.py:151
  31.3 1.9 %collective-permute-start.4 = (bf16[2,128,512]{2,1,0:T(8,128)(2,1)}, bf16[2,128,512]{2,1,0:T(8,128)(2,1)S(1)}, u32[]{:S(2)}, u32[]{:S(2)}) collective-permute-start(bf16[2,128,512]{2,1,0:T(8,128)(2,1)} %get-tuple-element.43), channel_id=1, source_target_pairs={{0,4},{2,6},{4,0},{6,2},{8,12},{10,14},{12,8},{14,10},{16,20},{18,... | collective-permute-start | bytes 786440 | tf_op jit(solution)/shard_map/ppermute | solution.py:400
  33.1 2.4 %collective-permute-start.2 = (bf16[2,128,512]{2,1,0:T(8,128)(2,1)}, bf16[2,128,512]{2,1,0:T(8,128)(2,1)S(1)}, u32[]{:S(2)}, u32[]{:S(2)}) collective-permute-start(bf16[2,128,512]{2,1,0:T(8,128)(2,1)} %get-tuple-element.36), channel_id=1, source_target_pairs={{0,16},{2,18},{4,20},{6,22},{8,24},{10,26},{12,28},{14,30},{16,0},... | collective-permute-start | bytes 786440 | tf_op jit(solution)/shard_map/ppermute | solution.py:400
  35.5 1.9 %constant_dynamic-slice_fusion.filt = bf16[2048,128]{1,0:T(8,128)(2,1)} fusion(bf16[2048,2048]{1,0:T(8,128)(2,1)} %param.8, s32[]{:T(128)S(6)} %select_n.48), kind=kLoop, calls=%fused_computation.6 | loop fusion | bytes 1048580 | tf_op jit(solution)/shard_map/dynamic_slice | solution.py:394
  37.4 24.4 %prepare.1.toeplitz = bf16[128,576,256]{2,1,0:T(8,128)(2,1)} custom-call(bf16[2048,128]{1,0:T(8,128)(2,1)} %constant_dynamic-slice_fusion.filt), custom_call_target="tpu_custom_call" | custom-call | tf_op jit(solution)/shard_map/prepare/pallas_call | solution.py:188
  61.8 4.6 %all-to-all-done.gated = bf16[16,128,512]{2,1,0:T(8,128)(2,1)S(1)} async-done(((bf16[16,128,512]{2,1,0:T(8,128)(2,1)}), bf16[16,128,512]{2,1,0:T(8,128)(2,1)S(1)}, u32[]{:S(2)}, u32[]{:S(2)}) %all-to-all-start) | async-done | bytes 2097184 | tf_op jit(solution)/shard_map/all_to_all | solution.py:406
  66.4 9.0 %collective-permute-start.3 = (bf16[2,128,512]{2,1,0:T(8,128)(2,1)}, bf16[2,128,512]{2,1,0:T(8,128)(2,1)S(1)}, u32[]{:S(2)}, u32[]{:S(2)}) collective-permute-start(bf16[2,128,512]{2,1,0:T(8,128)(2,1)} %get-tuple-element.42), channel_id=1, source_target_pairs={{0,20},{2,22},{4,16},{6,18},{8,28},{10,30},{12,24},{14,26},{16,4},... | collective-permute-start | bytes 786440 | tf_op jit(solution)/shard_map/ppermute | solution.py:400
  75.5 0.7 copy.8.skip
  76.3 2.3 %collective-permute-start.6 = (bf16[2,128,512]{2,1,0:T(8,128)(2,1)}, bf16[2,128,512]{2,1,0:T(8,128)(2,1)S(1)}, u32[]{:S(2)}, u32[]{:S(2)}) collective-permute-start(bf16[2,128,512]{2,1,0:T(8,128)(2,1)} %get-tuple-element.53), channel_id=1, source_target_pairs={{0,24},{2,26},{4,28},{6,30},{8,16},{10,18},{12,20},{14,22},{16,8},... | collective-permute-start | bytes 786440 | tf_op jit(solution)/shard_map/ppermute | solution.py:400
  78.6 18.6 %long_conv.1.refs_4_.refs_2_ = bf16[16,128,512]{2,1,0:T(8,128)(2,1)} custom-call(s32[16]{0:T(128)} %doc.7, s32[16]{0:T(128)} %live.7, f32[128,1]{1,0:T(8,128)} %copy.8.skip, bf16[128,576,256]{2,1,0:T(8,128)(2,1)} %prepare.1.toeplitz, bf16[16,128,512]{2,1,0:T(8,128)(2,1)} %copy-done.1), custom_call_target="tpu_custom_call" | custom-call | flops 1 | bytes 1 | tf_op jit(solution)/shard_map/long_conv/pallas_call | solution.py:300
  97.2 1.5 %collective-permute-start.10 = (bf16[2,128,512]{2,1,0:T(8,128)(2,1)}, bf16[2,128,512]{2,1,0:T(8,128)(2,1)S(1)}, u32[]{:S(2)}, u32[]{:S(2)}) collective-permute-start(bf16[2,128,512]{2,1,0:T(8,128)(2,1)} %get-tuple-element.58), channel_id=1, source_target_pairs={{0,12},{2,14},{4,8},{6,10},{8,4},{10,6},{12,0},{14,2},{16,28},{18,... | collective-permute-start | bytes 786440 | tf_op jit(solution)/shard_map/ppermute | solution.py:400
  98.6 2.9 %collective-permute-start.9 = (bf16[2,128,512]{2,1,0:T(8,128)(2,1)}, bf16[2,128,512]{2,1,0:T(8,128)(2,1)S(1)}, u32[]{:S(2)}, u32[]{:S(2)}) collective-permute-start(bf16[2,128,512]{2,1,0:T(8,128)(2,1)} %get-tuple-element.57), channel_id=1, source_target_pairs={{0,28},{2,30},{4,24},{6,26},{8,20},{10,22},{12,16},{14,18},{16,12}... | collective-permute-start | bytes 786440 | tf_op jit(solution)/shard_map/ppermute | solution.py:400
  102.3 2.9 %gate.3 = (bf16[128,2048]{1,0:T(8,128)(2,1)}, bf16[1,128,2048]{2,1,0:T(8,128)(2,1)}) custom-call(bf16[2,128,512]{2,1,0:T(8,128)(2,1)} %copy-done.10, bf16[2,128,512]{2,1,0:T(8,128)(2,1)} %get-tuple-element.37.refs_1_, bf16[2,128,512]{2,1,0:T(8,128)(2,1)} %copy-done.11, bf16[2,128,512]{2,1,0:T(8,128)(2,1)} %copy-done.9, ...), custom_call_target="tpu_custom_call" | custom-call | flops 1 | bytes 1 | tf_op jit(solution)/shard_map/gate/pallas_call | solution.py:363
  105.2 1.5 %collective-permute-start.5 = (bf16[128,2048]{1,0:T(8,128)(2,1)}, bf16[128,2048]{1,0:T(8,128)(2,1)S(1)}, u32[]{:S(2)}, u32[]{:S(2)}) collective-permute-start(bf16[128,2048]{1,0:T(8,128)(2,1)} %bitcast.17), channel_id=1, source_target_pairs={{0,1},{1,0},{2,3},{3,2},{4,5},{5,4},{6,7},{7,6},{8,9},{9,8},{10,11... | collective-permute-start | bytes 1572872 | tf_op jit(solution)/shard_map/ppermute | solution.py:442
  107.4 0.7 copy-done.8
  108.1 2.6 %gate.4 = (bf16[128,1024]{1,0:T(8,128)(2,1)}, bf16[1,128,1024]{2,1,0:T(8,128)(2,1)}) custom-call(bf16[2,128,512]{2,1,0:T(8,128)(2,1)} %copy-done.6, bf16[2,128,512]{2,1,0:T(8,128)(2,1)} %copy-done.8, bf16[16,128,512]{2,1,0:T(8,128)(2,1)} %long_conv.1.refs_4_.refs_2_), custom_call_target="tpu_custom_call" | custom-call | flops 1 | bytes 1 | tf_op jit(solution)/shard_map/gate/pallas_call | solution.py:363
  111.2 1.5 %collective-permute-done.9.refs_0_ = bf16[2,128,512]{2,1,0:T(8,128)(2,1)S(1)} collective-permute-done((bf16[2,128,512]{2,1,0:T(8,128)(2,1)}, bf16[2,128,512]{2,1,0:T(8,128)(2,1)S(1)}, u32[]{:S(2)}, u32[]{:S(2)}) %collective-permute-start.9) | collective-permute-done | bytes 262176 | tf_op jit(solution)/shard_map/ppermute | solution.py:400
  112.7 0.7 copy-done.7
  113.4 2.6 %gate.5 = (bf16[128,1024]{1,0:T(8,128)(2,1)}, bf16[1,128,1024]{2,1,0:T(8,128)(2,1)}) custom-call(bf16[2,128,512]{2,1,0:T(8,128)(2,1)} %copy-done.7, bf16[2,128,512]{2,1,0:T(8,128)(2,1)} %copy-done.5, bf16[16,128,512]{2,1,0:T(8,128)(2,1)} %long_conv.1.refs_4_.refs_2_), custom_call_target="tpu_custom_call" | custom-call | flops 1 | bytes 1 | tf_op jit(solution)/shard_map/gate/pallas_call | solution.py:363
  116.0 1.5 %collective-permute-start.11 = (bf16[128,1024]{1,0:T(8,128)(2,1)}, bf16[128,1024]{1,0:T(8,128)(2,1)S(1)}, u32[]{:S(2)}, u32[]{:S(2)}) collective-permute-start(bf16[128,1024]{1,0:T(8,128)(2,1)} %bitcast.19), channel_id=1, source_target_pairs={{0,1},{1,0},{2,3},{3,2},{4,5},{5,4},{6,7},{7,6},{8,9},{9,8},{10,11... | collective-permute-start | bytes 786440 | tf_op jit(solution)/shard_map/ppermute | solution.py:442
  117.8 2.5 %collective-permute-done.5 = bf16[128,2048]{1,0:T(8,128)(2,1)S(1)} collective-permute-done((bf16[128,2048]{1,0:T(8,128)(2,1)}, bf16[128,2048]{1,0:T(8,128)(2,1)S(1)}, u32[]{:S(2)}, u32[]{:S(2)}) %collective-permute-start.5) | collective-permute-done | bytes 524320 | tf_op jit(solution)/shard_map/ppermute | solution.py:442
  120.4 5.5 %collective-permute-done.8 = bf16[128,1024]{1,0:T(8,128)(2,1)S(1)} collective-permute-done((bf16[128,1024]{1,0:T(8,128)(2,1)}, bf16[128,1024]{1,0:T(8,128)(2,1)S(1)}, u32[]{:S(2)}, u32[]{:S(2)}) %collective-permute-start.8) | collective-permute-done | bytes 262176 | tf_op jit(solution)/shard_map/ppermute | solution.py:442
  126.0 2.7 %collective-permute-done.11 = bf16[128,1024]{1,0:T(8,128)(2,1)S(1)} collective-permute-done((bf16[128,1024]{1,0:T(8,128)(2,1)}, bf16[128,1024]{1,0:T(8,128)(2,1)S(1)}, u32[]{:S(2)}, u32[]{:S(2)}) %collective-permute-start.11) | collective-permute-done | bytes 262176 | tf_op jit(solution)/shard_map/ppermute | solution.py:442
  128.7 0.7 bitcast_dynamic-update-slice_fusion.2
  (44 shorter events, 3.5 us)
Async XLA Ops:
  0.0 75.4 %copy-start = (f32[2048]{0:T(1024)S(1)}, f32[2048]{0:T(1024)}, u32[]{:S(2)}) copy-start(f32[2048]{0:T(1024)} %param.9) | copy-start | bytes 24580
  0.9 8.7 %collective-permute-start = (bf16[3,2,2048]{2,1,0:T(2,128)(2,1)S(1)}, bf16[3,2,2048]{2,1,0:T(2,128)(2,1)S(1)}, u32[]{:S(2)}, u32[]{:S(2)}) collective-permute-start(bf16[3,2,2048]{2,1,0:T(2,128)(2,1)S(1)} %slice.3), channel_id=1, source_target_pairs={{0,2},{2,4},{4,6},{6,8},{8,10},{10,12},{12,14},{14,16},{16,18},{18... | collective-permute-start | bytes 73736 | tf_op jit(solution)/shard_map/ppermute | solution.py:391
  9.7 0.6 copy-start.14
  12.5 53.9 %all-to-all-start = ((bf16[16,128,512]{2,1,0:T(8,128)(2,1)}), bf16[16,128,512]{2,1,0:T(8,128)(2,1)S(1)}, u32[]{:S(2)}, u32[]{:S(2)}) async-start(bf16[16,128,512]{2,1,0:T(8,128)(2,1)} %first_tokens.1), calls=%async_computation | async-start | bytes 4194304 | tf_op jit(solution)/shard_map/all_to_all | solution.py:406
  24.4 2.9 %collective-permute-start.1 = (bf16[8,128,512]{2,1,0:T(8,128)(2,1)}, bf16[8,128,512]{2,1,0:T(8,128)(2,1)S(1)}, u32[]{:S(2)}, u32[]{:S(2)}) collective-permute-start(bf16[8,128,512]{2,1,0:T(8,128)(2,1)} %get-tuple-element.35), channel_id=1, source_target_pairs={{0,2},{2,0},{4,6},{6,4},{8,10},{10,8},{12,14},{14,12},{16,18},{18,... | collective-permute-start | bytes 3145736 | tf_op jit(solution)/shard_map/ppermute | solution.py:400
  27.3 1.0 copy-start.3
  31.3 45.0 %collective-permute-start.4 = (bf16[2,128,512]{2,1,0:T(8,128)(2,1)}, bf16[2,128,512]{2,1,0:T(8,128)(2,1)S(1)}, u32[]{:S(2)}, u32[]{:S(2)}) collective-permute-start(bf16[2,128,512]{2,1,0:T(8,128)(2,1)} %get-tuple-element.43), channel_id=1, source_target_pairs={{0,4},{2,6},{4,0},{6,2},{8,12},{10,14},{12,8},{14,10},{16,20},{18,... | collective-permute-start | bytes 786440 | tf_op jit(solution)/shard_map/ppermute | solution.py:400
  33.1 65.5 %collective-permute-start.2 = (bf16[2,128,512]{2,1,0:T(8,128)(2,1)}, bf16[2,128,512]{2,1,0:T(8,128)(2,1)S(1)}, u32[]{:S(2)}, u32[]{:S(2)}) collective-permute-start(bf16[2,128,512]{2,1,0:T(8,128)(2,1)} %get-tuple-element.36), channel_id=1, source_target_pairs={{0,16},{2,18},{4,20},{6,22},{8,24},{10,26},{12,28},{14,30},{16,0},... | collective-permute-start | bytes 786440 | tf_op jit(solution)/shard_map/ppermute | solution.py:400
  66.4 12.2 %copy-start.1 = (bf16[16,128,512]{2,1,0:T(8,128)(2,1)}, bf16[16,128,512]{2,1,0:T(8,128)(2,1)S(1)}, u32[]{:S(2)}) copy-start(bf16[16,128,512]{2,1,0:T(8,128)(2,1)S(1)} %all-to-all-done.gated) | copy-start | bytes 6291460
  66.4 35.2 %collective-permute-start.3 = (bf16[2,128,512]{2,1,0:T(8,128)(2,1)}, bf16[2,128,512]{2,1,0:T(8,128)(2,1)S(1)}, u32[]{:S(2)}, u32[]{:S(2)}) collective-permute-start(bf16[2,128,512]{2,1,0:T(8,128)(2,1)} %get-tuple-element.42), channel_id=1, source_target_pairs={{0,20},{2,22},{4,16},{6,18},{8,28},{10,30},{12,24},{14,26},{16,4},... | collective-permute-start | bytes 786440 | tf_op jit(solution)/shard_map/ppermute | solution.py:400
  76.3 20.9 %copy-start.9 = (bf16[2,128,512]{2,1,0:T(8,128)(2,1)}, bf16[2,128,512]{2,1,0:T(8,128)(2,1)S(1)}, u32[]{:S(2)}) copy-start(bf16[2,128,512]{2,1,0:T(8,128)(2,1)S(1)} %collective-permute-done.4.refs_3_) | copy-start | bytes 786436
  76.3 30.5 %collective-permute-start.6 = (bf16[2,128,512]{2,1,0:T(8,128)(2,1)}, bf16[2,128,512]{2,1,0:T(8,128)(2,1)S(1)}, u32[]{:S(2)}, u32[]{:S(2)}) collective-permute-start(bf16[2,128,512]{2,1,0:T(8,128)(2,1)} %get-tuple-element.53), channel_id=1, source_target_pairs={{0,24},{2,26},{4,28},{6,30},{8,16},{10,18},{12,20},{14,22},{16,8},... | collective-permute-start | bytes 786440 | tf_op jit(solution)/shard_map/ppermute | solution.py:400
  78.6 28.2 %collective-permute-start.7 = (bf16[2,128,512]{2,1,0:T(8,128)(2,1)}, bf16[2,128,512]{2,1,0:T(8,128)(2,1)S(1)}, u32[]{:S(2)}, u32[]{:S(2)}) collective-permute-start(bf16[2,128,512]{2,1,0:T(8,128)(2,1)} %get-tuple-element.54), channel_id=1, source_target_pairs={{0,8},{2,10},{4,12},{6,14},{8,0},{10,2},{12,4},{14,6},{16,24},{18,... | collective-permute-start | bytes 786440 | tf_op jit(solution)/shard_map/ppermute | solution.py:400
  97.2 14.1 %collective-permute-start.10 = (bf16[2,128,512]{2,1,0:T(8,128)(2,1)}, bf16[2,128,512]{2,1,0:T(8,128)(2,1)S(1)}, u32[]{:S(2)}, u32[]{:S(2)}) collective-permute-start(bf16[2,128,512]{2,1,0:T(8,128)(2,1)} %get-tuple-element.58), channel_id=1, source_target_pairs={{0,12},{2,14},{4,8},{6,10},{8,4},{10,6},{12,0},{14,2},{16,28},{18,... | collective-permute-start | bytes 786440 | tf_op jit(solution)/shard_map/ppermute | solution.py:400
  98.6 2.9 %copy-start.10 = (bf16[2,128,512]{2,1,0:T(8,128)(2,1)}, bf16[2,128,512]{2,1,0:T(8,128)(2,1)S(1)}, u32[]{:S(2)}) copy-start(bf16[2,128,512]{2,1,0:T(8,128)(2,1)S(1)} %collective-permute-done.2.refs_0_) | copy-start | bytes 786436
  98.6 14.1 %collective-permute-start.9 = (bf16[2,128,512]{2,1,0:T(8,128)(2,1)}, bf16[2,128,512]{2,1,0:T(8,128)(2,1)S(1)}, u32[]{:S(2)}, u32[]{:S(2)}) collective-permute-start(bf16[2,128,512]{2,1,0:T(8,128)(2,1)} %get-tuple-element.57), channel_id=1, source_target_pairs={{0,28},{2,30},{4,24},{6,26},{8,20},{10,22},{12,16},{14,18},{16,12}... | collective-permute-start | bytes 786440 | tf_op jit(solution)/shard_map/ppermute | solution.py:400
  101.6 0.7 copy-start.11
  105.2 15.1 %collective-permute-start.5 = (bf16[128,2048]{1,0:T(8,128)(2,1)}, bf16[128,2048]{1,0:T(8,128)(2,1)S(1)}, u32[]{:S(2)}, u32[]{:S(2)}) collective-permute-start(bf16[128,2048]{1,0:T(8,128)(2,1)} %bitcast.17), channel_id=1, source_target_pairs={{0,1},{1,0},{2,3},{3,2},{4,5},{5,4},{6,7},{7,6},{8,9},{9,8},{10,11... | collective-permute-start | bytes 1572872 | tf_op jit(solution)/shard_map/ppermute | solution.py:442
  106.7 0.7 copy-start.6
  107.4 0.7 copy-start.8
  110.7 7.0 %copy-start.4 = (bf16[128,2048]{1,0:T(8,128)(2,1)S(1)}, bf16[128,2048]{1,0:T(8,128)(2,1)}, u32[]{:S(2)}) copy-start(bf16[128,2048]{1,0:T(8,128)(2,1)} %get-tuple-element.51) | copy-start | bytes 1572868
  110.7 15.2 %collective-permute-start.8 = (bf16[128,1024]{1,0:T(8,128)(2,1)}, bf16[128,1024]{1,0:T(8,128)(2,1)S(1)}, u32[]{:S(2)}, u32[]{:S(2)}) collective-permute-start(bf16[128,1024]{1,0:T(8,128)(2,1)} %bitcast.18), channel_id=1, source_target_pairs={{0,1},{1,0},{2,3},{3,2},{4,5},{5,4},{6,7},{7,6},{8,9},{9,8},{10,11... | collective-permute-start | bytes 786440 | tf_op jit(solution)/shard_map/ppermute | solution.py:442
  111.2 1.5 %copy-start.5 = (bf16[2,128,512]{2,1,0:T(8,128)(2,1)}, bf16[2,128,512]{2,1,0:T(8,128)(2,1)S(1)}, u32[]{:S(2)}) copy-start(bf16[2,128,512]{2,1,0:T(8,128)(2,1)S(1)} %collective-permute-done.10.refs_1_) | copy-start | bytes 786436
  112.7 0.7 copy-start.7
  116.0 12.7 %collective-permute-start.11 = (bf16[128,1024]{1,0:T(8,128)(2,1)}, bf16[128,1024]{1,0:T(8,128)(2,1)S(1)}, u32[]{:S(2)}, u32[]{:S(2)}) collective-permute-start(bf16[128,1024]{1,0:T(8,128)(2,1)} %bitcast.19), channel_id=1, source_target_pairs={{0,1},{1,0},{2,3},{3,2},{4,5},{5,4},{6,7},{7,6},{8,9},{9,8},{10,11... | collective-permute-start | bytes 786440 | tf_op jit(solution)/shard_map/ppermute | solution.py:442
  117.5 2.9 %copy-start.12 = (bf16[128,1024]{1,0:T(8,128)(2,1)S(1)}, bf16[128,1024]{1,0:T(8,128)(2,1)}, u32[]{:S(2)}) copy-start(bf16[128,1024]{1,0:T(8,128)(2,1)} %get-tuple-element.55) | copy-start | bytes 786436
  117.7 8.2 %copy-start.13 = (bf16[128,1024]{1,0:T(8,128)(2,1)S(1)}, bf16[128,1024]{1,0:T(8,128)(2,1)}, u32[]{:S(2)}) copy-start(bf16[128,1024]{1,0:T(8,128)(2,1)} %get-tuple-element.59) | copy-start | bytes 786436
  126.0 2.7 %copy-start.2 = (bf16[2,128,4096]{2,1,0:T(8,128)(2,1)}, bf16[2,128,4096]{2,1,0:T(8,128)(2,1)S(1)}, u32[]{:S(2)}) copy-start(bf16[2,128,4096]{2,1,0:T(8,128)(2,1)S(1)} %bitcast_dynamic-update-slice_fusion.3) | copy-start | bytes 6291460

commit v3 on v2

--- a/solution.py
+++ b/solution.py
@@ -11,7 +11,6 @@
 UNROLL = 8
 ROWS = 64
 CORES = 2
-FLYING = 6
 CHANS = 32
 VMEM = 56 << 20
 
@@ -158,13 +157,15 @@
     )(*blocks)
 
 
-def prepare_kernel(filt, out, taps):
+def prepare_kernel(filt, skip, out, column, taps):
     step = pl.program_id(0)
     chans, rows, width = out.shape
 
     @pl.when(step == 0)
     def _():
         taps[...] = filt[...].astype(jnp.float32).T
+
+        column[...] = jnp.broadcast_to(skip[...], (8, skip.shape[1])).T[:, :1]
 
     def channel(c, _):
         row = taps[pl.ds(step * chans + c, 1), :]
@@ -180,7 +181,7 @@
     lax.fori_loop(0, chans, channel, 0, unroll=4)
 
 
-def prepare(filt):
+def prepare(filt, skip):
     lags, part = filt.shape
     chans = min(CHANS, part)
     width = 4 * ROWS
@@ -188,15 +189,24 @@
     return pl.pallas_call(
         prepare_kernel,
         grid=(part // chans,),
-        in_specs=[pl.BlockSpec((lags, part), lambda i: (0, 0))],
-        out_specs=pl.BlockSpec((chans, rows, width), lambda i: (i, 0, 0)),
-        out_shape=jax.ShapeDtypeStruct((part, rows, width), jnp.bfloat16),
+        in_specs=[
+            pl.BlockSpec((lags, part), lambda i: (0, 0)),
+            pl.BlockSpec((1, part), lambda i: (0, 0)),
+        ],
+        out_specs=[
+            pl.BlockSpec((chans, rows, width), lambda i: (i, 0, 0)),
+            pl.BlockSpec((part, 1), lambda i: (0, 0)),
+        ],
+        out_shape=[
+            jax.ShapeDtypeStruct((part, rows, width), jnp.bfloat16),
+            jax.ShapeDtypeStruct((part, 1), jnp.float32),
+        ],
         scratch_shapes=[pltpu.VMEM((part, lags), jnp.float32)],
         compiler_params=pltpu.CompilerParams(
             vmem_limit_bytes=VMEM, dimension_semantics=("arbitrary",)
         ),
         name="prepare",
-    )(filt)
+    )(filt, skip[None, :])
 
 
 def conv_kernel(doc, live, skip, toeplitz, gated, out, masks, wide, one, late, mixed):
@@ -392,8 +402,7 @@
         qkv[:, tok - 2 :, :], "ctx", [(i, i + 1) for i in range(shards - 1)]
     )
     filt = lax.dynamic_slice_in_dim(long_filter, here * part, part, axis=1)
-    direct = lax.dynamic_slice_in_dim(skip, here * part, part, axis=0)[:, None]
-    toeplitz = prepare(filt)
+    direct = lax.dynamic_slice_in_dim(skip, here * part, part, axis=0)
     out = jnp.zeros((halves, part, shards * tok // halves), jnp.bfloat16)
 
     def across(block, distance):
@@ -421,18 +430,24 @@
             got[far] = across(block, far * CORES)
         return after
 
-    early = [1, span]
+    early = [1, span, span - 1]
     for far in early:
         got[far] = across(queries[far], far * CORES)
+    got[1], filt = lax.optimization_barrier((got[1], filt))
+    toeplitz, direct = prepare(filt, direct)
     order = [far for far in order if far not in early]
-    middle = order[: 3 * len(order) // 5]
+    order = sorted(order, key=lambda far: (far not in groups[0], far < span))
+    last = [far for far in order if far in groups[2]]
+    middle = [far for far in order if far not in last]
+    late = last
     gated, toeplitz = launch(middle, (gated, toeplitz))
     got[1], gated = lax.optimization_barrier((got[1], gated))
     conv = long_conv(gated, toeplitz, direct, shard_doc, live)
-    conv = launch([far for far in order if far not in middle], conv)
-    arrived = [[got[far] for far in fars] for fars in groups]
-    for fars, blocks in zip(groups, arrived):
-        own, sent = gate(fars, blocks, conv, halves)
+    for fars in groups:
+        own, sent = gate(fars, [got[far] for far in fars], conv, halves)
+        if late:
+            sent = launch(late, sent)
+            late = []
         wide = own.shape[1]
         first = (here // CORES) % span ^ fars[-1]
         start = first // (len(fars) // halves) * wide

time: 130 us -> 129 us (level)
  starting transfers between devices: 33.5 us -> 26.7 us
  waiting for transfers between devices: 19.3 us -> 24.2 us
    ppermute x8, waiting for transfers between devices: 4.01 us -> 18.6 us  [across(): lax.ppermute(block, 'ctx', [(i, i ^ distance) for i in range(shards)])]
    ppermute x8, starting transfers between devices: 20.4 us -> 14.6 us  [across(): lax.ppermute(block, 'ctx', [(i, i ^ distance) for i in range(shards)])]
    ppermute x3, waiting for transfers between devices: 10.7 us -> 5.6 us  [local(): came = lax.ppermute(sent[d - 1], 'ch', route)]
    all_to_all x1, waiting for transfers between devices: 4.57 us -> 0.01 us  [local(): gated = lax.all_to_all(gated, 'ctx', 0, 0)]
    unnamed x30 -> x36, local copies, waits for them, and re-layouts: 4.4 us -> 5.39 us
  transfers between devices with their start and end apart: 13 -> 13, of which waited for: 6 -> 5; matrix products, arithmetic and copies ran while one was open for 2% -> 2% of each run, Pallas kernels for 50% -> 51%
where the time goes in v3:
time: 129 us; the launch traced here: 128 us
  Pallas kernels  67.4 us (52%)
  starting transfers between devices  26.7 us (21%)
  waiting for transfers between devices  24.2 us (19%)
  local copies, waits for them, and re-layouts  9.89 us (8%)
    pallas_call x1, Pallas kernels, prepare(): pl.pallas_call(prepare_kernel, grid=(part // chans,), in_specs=[pl.BlockS...  24.6 us
    ppermute x8, waiting for transfers between devices, across(): lax.ppermute(block, 'ctx', [(i, i ^ distance) for i in range(shards)])  18.6 us
    pallas_call x1, Pallas kernels, long_conv(): pl.pallas_call(conv_kernel, grid=(width // chans,), in_specs=[smem, smem,...  18.6 us
    ppermute x8, starting transfers between devices, across(): lax.ppermute(block, 'ctx', [(i, i ^ distance) for i in range(shards)])  14.6 us
    pallas_call x2, Pallas kernels, short_convs(): pl.pallas_call(functools.partial(short_kernel, count, len(borders)), grid...  11 us
    pallas_call x3, Pallas kernels, gate(): pl.pallas_call(functools.partial(gate_kernel, fars), grid=(width // chans...  8.06 us
    all_to_all x1, starting transfers between devices, local(): gated = lax.all_to_all(gated, 'ctx', 0, 0)  7.19 us
    ppermute x3, waiting for transfers between devices, local(): came = lax.ppermute(sent[d - 1], 'ch', route)  5.6 us
  transfers between devices with their start and end apart: 13, of which 5 were waited for; matrix products, arithmetic and copies ran while one was open for 2% of the time, Pallas kernels for 51%

profile of v3, /device:TPU:0, one launch (start us, length us, event | category | flops | bytes accessed | tf_op | source)
XLA Modules:
  0.0 128.4 jit_solution(17473919762244053492)
XLA Ops:
  0.0 0.9 slice.3
  0.9 2.4 %collective-permute-start = (bf16[3,2,2048]{2,1,0:T(2,128)(2,1)S(1)}, bf16[3,2,2048]{2,1,0:T(2,128)(2,1)S(1)}, u32[]{:S(2)}, u32[]{:S(2)}) collective-permute-start(bf16[3,2,2048]{2,1,0:T(2,128)(2,1)S(1)} %slice.3), channel_id=1, source_target_pairs={{0,2},{2,4},{4,6},{6,8},{8,10},{10,12},{12,14},{14,16},{16,18},{18... | collective-permute-start | bytes 73736 | tf_op jit(solution)/shard_map/ppermute | solution.py:401
  3.3 6.4 %short_kv.1.old = bf16[16,128,512]{2,1,0:T(8,128)(2,1)} custom-call(s32[16]{0:T(128)} %doc.7, s32[16]{0:T(128)} %live.7, f32[3,3,2048]{2,1,0:T(4,128)} %refs_0_.3, f32[3,3,2048]{2,1,0:T(4,128)} %refs_0_.3, bf16[3,512,2048]{2,1,0:T(8,128)(2,1)} %refs_1_.2, bf16[3,512,2048]{2,1,0:T(8,128)(2,1)} %refs_1_.2), custom_call_target="tpu_custom_call" | custom-call | tf_op jit(solution)/shard_map/short_kv/pallas_call | solution.py:80
  9.7 0.6 copy-done.15
  10.3 2.2 %first_tokens.1 = bf16[16,128,512]{2,1,0:T(8,128)(2,1)} custom-call(s32[16]{0:T(128)} %doc.7, s32[16]{0:T(128)} %live.7, bf16[3,2,2048]{2,1,0:T(2,128)(2,1)} %copy-done.15, bf16[3,2,2048]{2,1,0:T(2,128)(2,1)} %copy-done.15, f32[3,3,2048]{2,1,0:T(4,128)} %refs_0_.3, f32[3,3,2048]{2,1,0:T(4,128)} %refs_0_.3, ...), custom_call_target="tpu_custom_call", output_to_operand_aliasing={{}: (8, {})} | custom-call | tf_op jit(solution)/shard_map/first_tokens/pallas_call | solution.py:126
  12.5 7.2 %all-to-all-start = ((bf16[16,128,512]{2,1,0:T(8,128)(2,1)}), bf16[16,128,512]{2,1,0:T(8,128)(2,1)S(1)}, u32[]{:S(2)}, u32[]{:S(2)}) async-start(bf16[16,128,512]{2,1,0:T(8,128)(2,1)} %first_tokens.1), calls=%async_computation | async-start | bytes 4194304 | tf_op jit(solution)/shard_map/all_to_all | solution.py:415
  19.7 4.7 %short_q.1 = (bf16[8,128,512]{2,1,0:T(8,128)(2,1)}, bf16[8,128,512]{2,1,0:T(8,128)(2,1)}) custom-call(s32[16]{0:T(128)} %doc.7, s32[16]{0:T(128)} %live.7, f32[3,3,2048]{2,1,0:T(4,128)} %refs_0_.3, bf16[3,512,2048]{2,1,0:T(8,128)(2,1)} %refs_1_.2, bf16[3,2,2048]{2,1,0:T(2,128)(2,1)} %copy-done.15), custom_call_target="tpu_custom_call" | custom-call | tf_op jit(solution)/shard_map/short_q/pallas_call | solution.py:80
  24.8 2.5 %collective-permute-done.1.refs_1_ = bf16[8,128,512]{2,1,0:T(8,128)(2,1)S(1)} collective-permute-done((bf16[8,128,512]{2,1,0:T(8,128)(2,1)}, bf16[8,128,512]{2,1,0:T(8,128)(2,1)S(1)}, u32[]{:S(2)}, u32[]{:S(2)}) %collective-permute-start.1) | collective-permute-done | bytes 1048608 | tf_op jit(solution)/shard_map/ppermute | solution.py:409
  27.3 1.0 copy-done.4
  28.2 3.0 %pair_up.1 = (bf16[2,128,512]{2,1,0:T(8,128)(2,1)}, bf16[2,128,512]{2,1,0:T(8,128)(2,1)}, bf16[2,128,512]{2,1,0:T(8,128)(2,1)}, bf16[2,128,512]{2,1,0:T(8,128)(2...) custom-call(bf16[8,128,512]{2,1,0:T(8,128)(2,1)} %get-tuple-element., ...), custom_call_target="tpu_custom_call" | custom-call | tf_op jit(solution)/shard_map/pair_up/pallas_call | solution.py:150
  31.2 1.9 %collective-permute-start.3 = (bf16[2,128,512]{2,1,0:T(8,128)(2,1)}, bf16[2,128,512]{2,1,0:T(8,128)(2,1)S(1)}, u32[]{:S(2)}, u32[]{:S(2)}) collective-permute-start(bf16[2,128,512]{2,1,0:T(8,128)(2,1)} %get-tuple-element.45), channel_id=1, source_target_pairs={{0,4},{2,6},{4,0},{6,2},{8,12},{10,14},{12,8},{14,10},{16,20},{18,... | collective-permute-start | bytes 786440 | tf_op jit(solution)/shard_map/ppermute | solution.py:409
  33.7 1.9 %constant_dynamic-slice_fusion.filt = bf16[2048,128]{1,0:T(8,128)(2,1)} fusion(bf16[2048,2048]{1,0:T(8,128)(2,1)} %param.8, s32[]{:T(128)S(6)} %select_n.48), kind=kLoop, calls=%fused_computation.6 | loop fusion | bytes 1048580 | tf_op jit(solution)/shard_map/dynamic_slice | solution.py:404
  35.5 2.4 %collective-permute-start.2 = (bf16[2,128,512]{2,1,0:T(8,128)(2,1)}, bf16[2,128,512]{2,1,0:T(8,128)(2,1)S(1)}, u32[]{:S(2)}, u32[]{:S(2)}) collective-permute-start(bf16[2,128,512]{2,1,0:T(8,128)(2,1)} %get-tuple-element.39), channel_id=1, source_target_pairs={{0,16},{2,18},{4,20},{6,22},{8,24},{10,26},{12,28},{14,30},{16,0},... | collective-permute-start | bytes 786440 | tf_op jit(solution)/shard_map/ppermute | solution.py:409
  37.9 7.9 %collective-permute-done.3.refs_3_ = bf16[2,128,512]{2,1,0:T(8,128)(2,1)S(1)} collective-permute-done((bf16[2,128,512]{2,1,0:T(8,128)(2,1)}, bf16[2,128,512]{2,1,0:T(8,128)(2,1)S(1)}, u32[]{:S(2)}, u32[]{:S(2)}) %collective-permute-start.3) | collective-permute-done | bytes 262176 | tf_op jit(solution)/shard_map/ppermute | solution.py:409
  45.8 24.6 %prepare.1 = (bf16[128,576,256]{2,1,0:T(8,128)(2,1)}, f32[128,1]{1,0:T(8,128)}) custom-call(bf16[2048,128]{1,0:T(8,128)(2,1)} %constant_dynamic-slice_fusion.filt, f32[1,128]{1,0:T(1,128)} %dynamic-slice_bitcast_fusion.skip), custom_call_target="tpu_custom_call" | custom-call | tf_op jit(solution)/shard_map/prepare/pallas_call | solution.py:189
  70.4 5.0 %collective-permute-start.4 = (bf16[2,128,512]{2,1,0:T(8,128)(2,1)}, bf16[2,128,512]{2,1,0:T(8,128)(2,1)S(1)}, u32[]{:S(2)}, u32[]{:S(2)}) collective-permute-start(bf16[2,128,512]{2,1,0:T(8,128)(2,1)} %get-tuple-element.48), channel_id=1, source_target_pairs={{0,20},{2,22},{4,16},{6,18},{8,28},{10,30},{12,24},{14,26},{16,4},... | collective-permute-start | bytes 786440 | tf_op jit(solution)/shard_map/ppermute | solution.py:409
  75.4 2.3 %collective-permute-start.6 = (bf16[2,128,512]{2,1,0:T(8,128)(2,1)}, bf16[2,128,512]{2,1,0:T(8,128)(2,1)S(1)}, u32[]{:S(2)}, u32[]{:S(2)}) collective-permute-start(bf16[2,128,512]{2,1,0:T(8,128)(2,1)} %get-tuple-element.59), channel_id=1, source_target_pairs={{0,24},{2,26},{4,28},{6,30},{8,16},{10,18},{12,20},{14,22},{16,8},... | collective-permute-start | bytes 786440 | tf_op jit(solution)/shard_map/ppermute | solution.py:409
  77.8 18.6 %long_conv.1.refs_4_.refs_2_ = bf16[16,128,512]{2,1,0:T(8,128)(2,1)} custom-call(s32[16]{0:T(128)} %doc.7, s32[16]{0:T(128)} %live.7, f32[128,1]{1,0:T(8,128)} %get-tuple-element.52.skip, bf16[128,576,256]{2,1,0:T(8,128)(2,1)} %get-tuple-element.53.toeplitz, bf16[16,128,512]{2,1,0:T(8,128)(2,1)} %copy-done.2), custom_call_target="tpu_custom_call" | custom-call | flops 1 | bytes 1 | tf_op jit(solution)/shard_map/long_conv/pallas_call | solution.py:310
  96.4 1.9 %collective-permute-done.4.refs_2_ = bf16[2,128,512]{2,1,0:T(8,128)(2,1)S(1)} collective-permute-done((bf16[2,128,512]{2,1,0:T(8,128)(2,1)}, bf16[2,128,512]{2,1,0:T(8,128)(2,1)S(1)}, u32[]{:S(2)}, u32[]{:S(2)}) %collective-permute-start.4) | collective-permute-done | bytes 262176 | tf_op jit(solution)/shard_map/ppermute | solution.py:409
  98.3 0.7 copy-done.12
  99.0 3.0 %gate.3 = (bf16[128,2048]{1,0:T(8,128)(2,1)}, bf16[1,128,2048]{2,1,0:T(8,128)(2,1)}) custom-call(bf16[2,128,512]{2,1,0:T(8,128)(2,1)} %copy-done.9, bf16[2,128,512]{2,1,0:T(8,128)(2,1)} %get-tuple-element.40.refs_1_, bf16[2,128,512]{2,1,0:T(8,128)(2,1)} %copy-done.12, bf16[2,128,512]{2,1,0:T(8,128)(2,1)} %copy-done.8, ...), custom_call_target="tpu_custom_call" | custom-call | flops 1 | bytes 1 | tf_op jit(solution)/shard_map/gate/pallas_call | solution.py:373
  102.0 1.5 %collective-permute-start.5 = (bf16[128,2048]{1,0:T(8,128)(2,1)}, bf16[128,2048]{1,0:T(8,128)(2,1)S(1)}, u32[]{:S(2)}, u32[]{:S(2)}) collective-permute-start(bf16[128,2048]{1,0:T(8,128)(2,1)} %bitcast.17), channel_id=1, source_target_pairs={{0,1},{1,0},{2,3},{3,2},{4,5},{5,4},{6,7},{7,6},{8,9},{9,8},{10,11... | collective-permute-start | bytes 1572872 | tf_op jit(solution)/shard_map/ppermute | solution.py:457
  103.5 2.6 %collective-permute-start.9 = (bf16[2,128,512]{2,1,0:T(8,128)(2,1)S(1)}, bf16[2,128,512]{2,1,0:T(8,128)(2,1)S(1)}, u32[]{:S(2)}, u32[]{:S(2)}) collective-permute-start(bf16[2,128,512]{2,1,0:T(8,128)(2,1)S(1)} %copy-done.16), channel_id=1, source_target_pairs={{0,28},{2,30},{4,24},{6,26},{8,20},{10,22},{12,16},{14,18},{16,12}... | collective-permute-start | bytes 786440 | tf_op jit(solution)/shard_map/ppermute | solution.py:409
  106.1 0.7 copy-done.6
  106.8 0.7 copy-done.7
  107.5 2.5 %gate.4 = (bf16[128,1024]{1,0:T(8,128)(2,1)}, bf16[1,128,1024]{2,1,0:T(8,128)(2,1)}) custom-call(bf16[2,128,512]{2,1,0:T(8,128)(2,1)} %copy-done.6, bf16[2,128,512]{2,1,0:T(8,128)(2,1)} %copy-done.7, bf16[16,128,512]{2,1,0:T(8,128)(2,1)} %long_conv.1.refs_4_.refs_2_), custom_call_target="tpu_custom_call" | custom-call | flops 1 | bytes 1 | tf_op jit(solution)/shard_map/gate/pallas_call | solution.py:373
  110.8 6.3 %collective-permute-done.10.refs_1_ = bf16[2,128,512]{2,1,0:T(8,128)(2,1)S(1)} collective-permute-done((bf16[2,128,512]{2,1,0:T(8,128)(2,1)S(1)}, bf16[2,128,512]{2,1,0:T(8,128)(2,1)S(1)}, u32[]{:S(2)}, u32[]{:S(2)}) %collective-permute-start.10) | collective-permute-done | bytes 262176 | tf_op jit(solution)/shard_map/ppermute | solution.py:409
  117.1 0.7 copy-done.10
  117.8 0.7 copy-done.11
  118.5 2.6 %gate.5 = (bf16[128,1024]{1,0:T(8,128)(2,1)}, bf16[1,128,1024]{2,1,0:T(8,128)(2,1)}) custom-call(bf16[2,128,512]{2,1,0:T(8,128)(2,1)} %copy-done.11, bf16[2,128,512]{2,1,0:T(8,128)(2,1)} %copy-done.10, bf16[16,128,512]{2,1,0:T(8,128)(2,1)} %long_conv.1.refs_4_.refs_2_), custom_call_target="tpu_custom_call" | custom-call | flops 1 | bytes 1 | tf_op jit(solution)/shard_map/gate/pallas_call | solution.py:373
  122.1 5.6 %collective-permute-done.11 = bf16[128,1024]{1,0:T(8,128)(2,1)S(1)} collective-permute-done((bf16[128,1024]{1,0:T(8,128)(2,1)}, bf16[128,1024]{1,0:T(8,128)(2,1)S(1)}, u32[]{:S(2)}, u32[]{:S(2)}) %collective-permute-start.11) | collective-permute-done | bytes 262176 | tf_op jit(solution)/shard_map/ppermute | solution.py:457
  127.7 0.7 bitcast_dynamic-update-slice_fusion.2
  (49 shorter events, 2.8 us)
Async XLA Ops:
  0.0 33.1 %copy-start = (f32[2048]{0:T(1024)S(1)}, f32[2048]{0:T(1024)}, u32[]{:S(2)}) copy-start(f32[2048]{0:T(1024)} %param.9) | copy-start | bytes 24580
  0.9 8.7 %collective-permute-start = (bf16[3,2,2048]{2,1,0:T(2,128)(2,1)S(1)}, bf16[3,2,2048]{2,1,0:T(2,128)(2,1)S(1)}, u32[]{:S(2)}, u32[]{:S(2)}) collective-permute-start(bf16[3,2,2048]{2,1,0:T(2,128)(2,1)S(1)} %slice.3), channel_id=1, source_target_pairs={{0,2},{2,4},{4,6},{6,8},{8,10},{10,12},{12,14},{14,16},{16,18},{18... | collective-permute-start | bytes 73736 | tf_op jit(solution)/shard_map/ppermute | solution.py:401
  9.7 0.6 copy-start.15
  12.5 57.9 %all-to-all-start = ((bf16[16,128,512]{2,1,0:T(8,128)(2,1)}), bf16[16,128,512]{2,1,0:T(8,128)(2,1)S(1)}, u32[]{:S(2)}, u32[]{:S(2)}) async-start(bf16[16,128,512]{2,1,0:T(8,128)(2,1)} %first_tokens.1), calls=%async_computation | async-start | bytes 4194304 | tf_op jit(solution)/shard_map/all_to_all | solution.py:415
  24.3 2.9 %collective-permute-start.1 = (bf16[8,128,512]{2,1,0:T(8,128)(2,1)}, bf16[8,128,512]{2,1,0:T(8,128)(2,1)S(1)}, u32[]{:S(2)}, u32[]{:S(2)}) collective-permute-start(bf16[8,128,512]{2,1,0:T(8,128)(2,1)} %get-tuple-element.38), channel_id=1, source_target_pairs={{0,2},{2,0},{4,6},{6,4},{8,10},{10,8},{12,14},{14,12},{16,18},{18,... | collective-permute-start | bytes 3145736 | tf_op jit(solution)/shard_map/ppermute | solution.py:409
  27.3 1.0 copy-start.4
  31.2 14.6 %collective-permute-start.3 = (bf16[2,128,512]{2,1,0:T(8,128)(2,1)}, bf16[2,128,512]{2,1,0:T(8,128)(2,1)S(1)}, u32[]{:S(2)}, u32[]{:S(2)}) collective-permute-start(bf16[2,128,512]{2,1,0:T(8,128)(2,1)} %get-tuple-element.45), channel_id=1, source_target_pairs={{0,4},{2,6},{4,0},{6,2},{8,12},{10,14},{12,8},{14,10},{16,20},{18,... | collective-permute-start | bytes 786440 | tf_op jit(solution)/shard_map/ppermute | solution.py:409
  35.5 60.8 %collective-permute-start.2 = (bf16[2,128,512]{2,1,0:T(8,128)(2,1)}, bf16[2,128,512]{2,1,0:T(8,128)(2,1)S(1)}, u32[]{:S(2)}, u32[]{:S(2)}) collective-permute-start(bf16[2,128,512]{2,1,0:T(8,128)(2,1)} %get-tuple-element.39), channel_id=1, source_target_pairs={{0,16},{2,18},{4,20},{6,22},{8,24},{10,26},{12,28},{14,30},{16,0},... | collective-permute-start | bytes 786440 | tf_op jit(solution)/shard_map/ppermute | solution.py:409
  45.8 50.6 %copy-start.8 = (bf16[2,128,512]{2,1,0:T(8,128)(2,1)}, bf16[2,128,512]{2,1,0:T(8,128)(2,1)S(1)}, u32[]{:S(2)}) copy-start(bf16[2,128,512]{2,1,0:T(8,128)(2,1)S(1)} %collective-permute-done.3.refs_3_) | copy-start | bytes 786436
  70.4 7.4 %copy-start.2 = (bf16[16,128,512]{2,1,0:T(8,128)(2,1)}, bf16[16,128,512]{2,1,0:T(8,128)(2,1)S(1)}, u32[]{:S(2)}) copy-start(bf16[16,128,512]{2,1,0:T(8,128)(2,1)S(1)} %all-to-all-done.gated) | copy-start | bytes 6291460
  70.4 27.9 %collective-permute-start.4 = (bf16[2,128,512]{2,1,0:T(8,128)(2,1)}, bf16[2,128,512]{2,1,0:T(8,128)(2,1)S(1)}, u32[]{:S(2)}, u32[]{:S(2)}) collective-permute-start(bf16[2,128,512]{2,1,0:T(8,128)(2,1)} %get-tuple-element.48), channel_id=1, source_target_pairs={{0,20},{2,22},{4,16},{6,18},{8,28},{10,30},{12,24},{14,26},{16,4},... | collective-permute-start | bytes 786440 | tf_op jit(solution)/shard_map/ppermute | solution.py:409
  75.4 30.6 %collective-permute-start.6 = (bf16[2,128,512]{2,1,0:T(8,128)(2,1)}, bf16[2,128,512]{2,1,0:T(8,128)(2,1)S(1)}, u32[]{:S(2)}, u32[]{:S(2)}) collective-permute-start(bf16[2,128,512]{2,1,0:T(8,128)(2,1)} %get-tuple-element.59), channel_id=1, source_target_pairs={{0,24},{2,26},{4,28},{6,30},{8,16},{10,18},{12,20},{14,22},{16,8},... | collective-permute-start | bytes 786440 | tf_op jit(solution)/shard_map/ppermute | solution.py:409
  77.8 28.3 %collective-permute-start.7 = (bf16[2,128,512]{2,1,0:T(8,128)(2,1)}, bf16[2,128,512]{2,1,0:T(8,128)(2,1)S(1)}, u32[]{:S(2)}, u32[]{:S(2)}) collective-permute-start(bf16[2,128,512]{2,1,0:T(8,128)(2,1)} %get-tuple-element.60), channel_id=1, source_target_pairs={{0,8},{2,10},{4,12},{6,14},{8,0},{10,2},{12,4},{14,6},{16,24},{18,... | collective-permute-start | bytes 786440 | tf_op jit(solution)/shard_map/ppermute | solution.py:409
  96.3 7.1 %copy-start.17 = (bf16[2,128,512]{2,1,0:T(8,128)(2,1)S(1)}, bf16[2,128,512]{2,1,0:T(8,128)(2,1)}, u32[]{:S(2)}) copy-start(bf16[2,128,512]{2,1,0:T(8,128)(2,1)} %get-tuple-element.64) | copy-start | bytes 786436
  96.3 7.1 %copy-start.16 = (bf16[2,128,512]{2,1,0:T(8,128)(2,1)S(1)}, bf16[2,128,512]{2,1,0:T(8,128)(2,1)}, u32[]{:S(2)}) copy-start(bf16[2,128,512]{2,1,0:T(8,128)(2,1)} %get-tuple-element.63) | copy-start | bytes 786436
  96.4 1.9 %copy-start.9 = (bf16[2,128,512]{2,1,0:T(8,128)(2,1)}, bf16[2,128,512]{2,1,0:T(8,128)(2,1)S(1)}, u32[]{:S(2)}) copy-start(bf16[2,128,512]{2,1,0:T(8,128)(2,1)S(1)} %collective-permute-done.2.refs_0_) | copy-start | bytes 786436
  98.3 0.7 copy-start.12
  102.0 19.6 %collective-permute-start.5 = (bf16[128,2048]{1,0:T(8,128)(2,1)}, bf16[128,2048]{1,0:T(8,128)(2,1)S(1)}, u32[]{:S(2)}, u32[]{:S(2)}) collective-permute-start(bf16[128,2048]{1,0:T(8,128)(2,1)} %bitcast.17), channel_id=1, source_target_pairs={{0,1},{1,0},{2,3},{3,2},{4,5},{5,4},{6,7},{7,6},{8,9},{9,8},{10,11... | collective-permute-start | bytes 1572872 | tf_op jit(solution)/shard_map/ppermute | solution.py:457
  103.5 7.3 %copy-start.5 = (bf16[128,2048]{1,0:T(8,128)(2,1)S(1)}, bf16[128,2048]{1,0:T(8,128)(2,1)}, u32[]{:S(2)}) copy-start(bf16[128,2048]{1,0:T(8,128)(2,1)} %get-tuple-element.55) | copy-start | bytes 1572868
  103.5 13.6 %collective-permute-start.10 = (bf16[2,128,512]{2,1,0:T(8,128)(2,1)S(1)}, bf16[2,128,512]{2,1,0:T(8,128)(2,1)S(1)}, u32[]{:S(2)}, u32[]{:S(2)}) collective-permute-start(bf16[2,128,512]{2,1,0:T(8,128)(2,1)S(1)} %copy-done.17), channel_id=1, source_target_pairs={{0,12},{2,14},{4,8},{6,10},{8,4},{10,6},{12,0},{14,2},{16,28},{18,... | collective-permute-start | bytes 786440 | tf_op jit(solution)/shard_map/ppermute | solution.py:409
  103.5 13.6 %collective-permute-start.9 = (bf16[2,128,512]{2,1,0:T(8,128)(2,1)S(1)}, bf16[2,128,512]{2,1,0:T(8,128)(2,1)S(1)}, u32[]{:S(2)}, u32[]{:S(2)}) collective-permute-start(bf16[2,128,512]{2,1,0:T(8,128)(2,1)S(1)} %copy-done.16), channel_id=1, source_target_pairs={{0,28},{2,30},{4,24},{6,26},{8,20},{10,22},{12,16},{14,18},{16,12}... | collective-permute-start | bytes 786440 | tf_op jit(solution)/shard_map/ppermute | solution.py:409
  106.1 0.7 copy-start.6
  106.8 0.7 copy-start.7
  110.0 11.7 %collective-permute-start.8 = (bf16[128,1024]{1,0:T(8,128)(2,1)}, bf16[128,1024]{1,0:T(8,128)(2,1)S(1)}, u32[]{:S(2)}, u32[]{:S(2)}) collective-permute-start(bf16[128,1024]{1,0:T(8,128)(2,1)} %bitcast.18), channel_id=1, source_target_pairs={{0,1},{1,0},{2,3},{3,2},{4,5},{5,4},{6,7},{7,6},{8,9},{9,8},{10,11... | collective-permute-start | bytes 786440 | tf_op jit(solution)/shard_map/ppermute | solution.py:457
  110.8 10.8 %copy-start.13 = (bf16[128,1024]{1,0:T(8,128)(2,1)S(1)}, bf16[128,1024]{1,0:T(8,128)(2,1)}, u32[]{:S(2)}) copy-start(bf16[128,1024]{1,0:T(8,128)(2,1)} %get-tuple-element.61) | copy-start | bytes 786436
  117.1 0.7 copy-start.10
  117.8 0.7 copy-start.11
  118.5 9.9 %copy-start.1 = (f32[2048]{0:T(1024)S(1)}, f32[2048]{0:T(1024)}, u32[]{:S(2)}) copy-start(f32[2048]{0:T(1024)} %param.9) | copy-start | bytes 24580
  121.1 0.9 copy-start.14
  121.1 6.6 %collective-permute-start.11 = (bf16[128,1024]{1,0:T(8,128)(2,1)}, bf16[128,1024]{1,0:T(8,128)(2,1)S(1)}, u32[]{:S(2)}, u32[]{:S(2)}) collective-permute-start(bf16[128,1024]{1,0:T(8,128)(2,1)} %bitcast.19), channel_id=1, source_target_pairs={{0,1},{1,0},{2,3},{3,2},{4,5},{5,4},{6,7},{7,6},{8,9},{9,8},{10,11... | collective-permute-start | bytes 786440 | tf_op jit(solution)/shard_map/ppermute | solution.py:457
  122.1 5.6 %copy-start.3 = (bf16[2,128,4096]{2,1,0:T(8,128)(2,1)}, bf16[2,128,4096]{2,1,0:T(8,128)(2,1)S(1)}, u32[]{:S(2)}) copy-start(bf16[2,128,4096]{2,1,0:T(8,128)(2,1)S(1)} %bitcast_dynamic-update-slice_fusion.3) | copy-start | bytes 6291460

commit v4 on v3

--- a/solution.py
+++ b/solution.py
@@ -8,7 +8,7 @@
 from jax.sharding import PartitionSpec as P
 
 LANES = 128
-UNROLL = 8
+UNROLL = 16
 ROWS = 64
 CORES = 2
 CHANS = 32
@@ -178,7 +178,7 @@
             out[c, k * ROWS : (k + 1) * ROWS, :] = toeplitz[:, k * width : (k + 1) * width]
         return 0
 
-    lax.fori_loop(0, chans, channel, 0, unroll=4)
+    lax.fori_loop(0, chans, channel, 0, unroll=8)
 
 
 def prepare(filt, skip):
@@ -415,7 +415,7 @@
     gated = lax.all_to_all(gated, "ctx", 0, 0)
     queries = [queries[0]] + [across(queries[k], k) for k in range(1, CORES)]
     queries = pair_up(queries)
-    cuts = [0, span // 2, span * 3 // 4, span]
+    cuts = [0, span // 4, span // 2, span * 3 // 4, span]
     groups = [
         [near + h * span for near in range(low, high) for h in reversed(range(halves))]
         for low, high in zip(cuts, cuts[1:])
@@ -436,8 +436,8 @@
     got[1], filt = lax.optimization_barrier((got[1], filt))
     toeplitz, direct = prepare(filt, direct)
     order = [far for far in order if far not in early]
-    order = sorted(order, key=lambda far: (far not in groups[0], far < span))
-    last = [far for far in order if far in groups[2]]
+    order = sorted(order, key=lambda far: (far not in groups[0] + groups[1], far < span))
+    last = [far for far in order if far in groups[-1]]
     middle = [far for far in order if far not in last]
     late = last
     gated, toeplitz = launch(middle, (gated, toeplitz))

time: 129 us -> 128 us (level)
  starting transfers between devices: 26.7 us -> 31 us
  waiting for transfers between devices: 24.2 us -> 20.6 us
  local copies, waits for them, and re-layouts: 9.89 us -> 8.4 us
    ppermute x8, waiting for transfers between devices: 18.6 us -> 10.3 us  [across(): lax.ppermute(block, 'ctx', [(i, i ^ distance) for i in range(shards)])]
    ppermute x3 -> x4, waiting for transfers between devices: 5.6 us -> 10.3 us  [local(): came = lax.ppermute(sent[d - 1], 'ch', route)]
    ppermute x8, starting transfers between devices: 14.6 us -> 17.3 us  [across(): lax.ppermute(block, 'ctx', [(i, i ^ distance) for i in range(shards)])]
    pallas_call x3 -> x4, Pallas kernels: 8.06 us -> 10.3 us  [gate(): pl.pallas_call(functools.partial(gate_kernel, fars), grid=(width // chans...]
    ppermute x3 -> x4, starting transfers between devices: 2.53 us -> 4.18 us  [local(): came = lax.ppermute(sent[d - 1], 'ch', route)]
    unnamed x36 -> x34, local copies, waits for them, and re-layouts: 5.39 us -> 3.86 us
    pallas_call x1, Pallas kernels: 24.6 us -> 23.2 us  [prepare(): pl.pallas_call(prepare_kernel, grid=(part // chans,), in_specs=[pl.BlockS...]
  transfers between devices with their start and end apart: 13 -> 14, of which waited for: 5 -> 5; matrix products, arithmetic and copies ran while one was open for 2% -> 2% of each run, Pallas kernels for 51% -> 51%
where the time goes in v4:
time: 128 us
  Pallas kernels  67.5 us (53%)
  starting transfers between devices  31 us (24%)
  waiting for transfers between devices  20.6 us (16%)
  local copies, waits for them, and re-layouts  8.4 us (7%)
    pallas_call x1, Pallas kernels, prepare(): pl.pallas_call(prepare_kernel, grid=(part // chans,), in_specs=[pl.BlockS...  23.2 us
    pallas_call x1, Pallas kernels, long_conv(): pl.pallas_call(conv_kernel, grid=(width // chans,), in_specs=[smem, smem,...  17.7 us
    ppermute x8, starting transfers between devices, across(): lax.ppermute(block, 'ctx', [(i, i ^ distance) for i in range(shards)])  17.3 us
    pallas_call x2, Pallas kernels, short_convs(): pl.pallas_call(functools.partial(short_kernel, count, len(borders)), grid...  11 us
    ppermute x8, waiting for transfers between devices, across(): lax.ppermute(block, 'ctx', [(i, i ^ distance) for i in range(shards)])  10.3 us
    pallas_call x4, Pallas kernels, gate(): pl.pallas_call(functools.partial(gate_kernel, fars), grid=(width // chans...  10.3 us
    ppermute x4, waiting for transfers between devices, local(): came = lax.ppermute(sent[d - 1], 'ch', route)  10.3 us
    all_to_all x1, starting transfers between devices, local(): gated = lax.all_to_all(gated, 'ctx', 0, 0)  7.19 us
  transfers between devices with their start and end apart: 14, of which 5 were waited for; matrix products, arithmetic and copies ran while one was open for 2% of the time, Pallas kernels for 51%

profile of v4, /device:TPU:0, one launch (start us, length us, event | category | flops | bytes accessed | tf_op | source)
XLA Modules:
  0.0 127.7 jit_solution(5978119743710930443)
XLA Ops:
  0.0 0.9 slice.3
  0.9 2.4 %collective-permute-start = (bf16[3,2,2048]{2,1,0:T(2,128)(2,1)S(1)}, bf16[3,2,2048]{2,1,0:T(2,128)(2,1)S(1)}, u32[]{:S(2)}, u32[]{:S(2)}) collective-permute-start(bf16[3,2,2048]{2,1,0:T(2,128)(2,1)S(1)} %slice.3), channel_id=1, source_target_pairs={{0,2},{2,4},{4,6},{6,8},{8,10},{10,12},{12,14},{14,16},{16,18},{18... | collective-permute-start | bytes 73736 | tf_op jit(solution)/shard_map/ppermute | solution.py:401
  3.3 6.4 %short_kv.1.old = bf16[16,128,512]{2,1,0:T(8,128)(2,1)} custom-call(s32[16]{0:T(128)} %doc.7, s32[16]{0:T(128)} %live.7, f32[3,3,2048]{2,1,0:T(4,128)} %refs_0_.3, f32[3,3,2048]{2,1,0:T(4,128)} %refs_0_.3, bf16[3,512,2048]{2,1,0:T(8,128)(2,1)} %refs_1_.2, bf16[3,512,2048]{2,1,0:T(8,128)(2,1)} %refs_1_.2), custom_call_target="tpu_custom_call" | custom-call | tf_op jit(solution)/shard_map/short_kv/pallas_call | solution.py:80
  10.3 2.2 %first_tokens.1 = bf16[16,128,512]{2,1,0:T(8,128)(2,1)} custom-call(s32[16]{0:T(128)} %doc.7, s32[16]{0:T(128)} %live.7, bf16[3,2,2048]{2,1,0:T(2,128)(2,1)} %copy-done.15, bf16[3,2,2048]{2,1,0:T(2,128)(2,1)} %copy-done.15, f32[3,3,2048]{2,1,0:T(4,128)} %refs_0_.3, f32[3,3,2048]{2,1,0:T(4,128)} %refs_0_.3, ...), custom_call_target="tpu_custom_call", output_to_operand_aliasing={{}: (8, {})} | custom-call | tf_op jit(solution)/shard_map/first_tokens/pallas_call | solution.py:126
  12.5 7.2 %all-to-all-start = ((bf16[16,128,512]{2,1,0:T(8,128)(2,1)}), bf16[16,128,512]{2,1,0:T(8,128)(2,1)S(1)}, u32[]{:S(2)}, u32[]{:S(2)}) async-start(bf16[16,128,512]{2,1,0:T(8,128)(2,1)} %first_tokens.1), calls=%async_computation | async-start | bytes 4194304 | tf_op jit(solution)/shard_map/all_to_all | solution.py:415
  19.7 4.7 %short_q.1 = (bf16[8,128,512]{2,1,0:T(8,128)(2,1)}, bf16[8,128,512]{2,1,0:T(8,128)(2,1)}) custom-call(s32[16]{0:T(128)} %doc.7, s32[16]{0:T(128)} %live.7, f32[3,3,2048]{2,1,0:T(4,128)} %refs_0_.3, bf16[3,512,2048]{2,1,0:T(8,128)(2,1)} %refs_1_.2, bf16[3,2,2048]{2,1,0:T(2,128)(2,1)} %copy-done.15), custom_call_target="tpu_custom_call" | custom-call | tf_op jit(solution)/shard_map/short_q/pallas_call | solution.py:80
  24.8 2.5 %collective-permute-done.1.refs_1_ = bf16[8,128,512]{2,1,0:T(8,128)(2,1)S(1)} collective-permute-done((bf16[8,128,512]{2,1,0:T(8,128)(2,1)}, bf16[8,128,512]{2,1,0:T(8,128)(2,1)S(1)}, u32[]{:S(2)}, u32[]{:S(2)}) %collective-permute-start.1) | collective-permute-done | bytes 1048608 | tf_op jit(solution)/shard_map/ppermute | solution.py:409
  27.3 1.0 copy-done.4
  28.3 3.0 %pair_up.1 = (bf16[2,128,512]{2,1,0:T(8,128)(2,1)}, bf16[2,128,512]{2,1,0:T(8,128)(2,1)}, bf16[2,128,512]{2,1,0:T(8,128)(2,1)}, bf16[2,128,512]{2,1,0:T(8,128)(2...) custom-call(bf16[8,128,512]{2,1,0:T(8,128)(2,1)} %get-tuple-element., ...), custom_call_target="tpu_custom_call" | custom-call | tf_op jit(solution)/shard_map/pair_up/pallas_call | solution.py:150
  31.3 1.9 %collective-permute-start.3 = (bf16[2,128,512]{2,1,0:T(8,128)(2,1)}, bf16[2,128,512]{2,1,0:T(8,128)(2,1)S(1)}, u32[]{:S(2)}, u32[]{:S(2)}) collective-permute-start(bf16[2,128,512]{2,1,0:T(8,128)(2,1)} %get-tuple-element.43), channel_id=1, source_target_pairs={{0,4},{2,6},{4,0},{6,2},{8,12},{10,14},{12,8},{14,10},{16,20},{18,... | collective-permute-start | bytes 786440 | tf_op jit(solution)/shard_map/ppermute | solution.py:409
  33.7 1.9 %constant_dynamic-slice_fusion.filt = bf16[2048,128]{1,0:T(8,128)(2,1)} fusion(bf16[2048,2048]{1,0:T(8,128)(2,1)} %param.8, s32[]{:T(128)S(6)} %select_n.56), kind=kLoop, calls=%fused_computation.8 | loop fusion | bytes 1048580 | tf_op jit(solution)/shard_map/dynamic_slice | solution.py:404
  35.6 2.4 %collective-permute-start.2 = (bf16[2,128,512]{2,1,0:T(8,128)(2,1)}, bf16[2,128,512]{2,1,0:T(8,128)(2,1)}, u32[]{:S(2)}, u32[]{:S(2)}) collective-permute-start(bf16[2,128,512]{2,1,0:T(8,128)(2,1)} %get-tuple-element.41), channel_id=1, source_target_pairs={{0,16},{2,18},{4,20},{6,22},{8,24},{10,26},{12,28},{14,30},{16,0},... | collective-permute-start | bytes 786440 | tf_op jit(solution)/shard_map/ppermute | solution.py:409
  38.0 7.8 %collective-permute-done.3.refs_1_ = bf16[2,128,512]{2,1,0:T(8,128)(2,1)S(1)} collective-permute-done((bf16[2,128,512]{2,1,0:T(8,128)(2,1)}, bf16[2,128,512]{2,1,0:T(8,128)(2,1)S(1)}, u32[]{:S(2)}, u32[]{:S(2)}) %collective-permute-start.3) | collective-permute-done | bytes 262176 | tf_op jit(solution)/shard_map/ppermute | solution.py:409
  45.8 23.2 %prepare.1 = (bf16[128,576,256]{2,1,0:T(8,128)(2,1)}, f32[128,1]{1,0:T(8,128)}) custom-call(bf16[2048,128]{1,0:T(8,128)(2,1)} %constant_dynamic-slice_fusion.filt, f32[1,128]{1,0:T(1,128)} %dynamic-slice_bitcast_fusion.skip), custom_call_target="tpu_custom_call" | custom-call | tf_op jit(solution)/shard_map/prepare/pallas_call | solution.py:189
  69.1 6.4 %collective-permute-start.5 = (bf16[2,128,512]{2,1,0:T(8,128)(2,1)}, bf16[2,128,512]{2,1,0:T(8,128)(2,1)S(1)}, u32[]{:S(2)}, u32[]{:S(2)}) collective-permute-start(bf16[2,128,512]{2,1,0:T(8,128)(2,1)} %get-tuple-element.59), channel_id=1, source_target_pairs={{0,20},{2,22},{4,16},{6,18},{8,28},{10,30},{12,24},{14,26},{16,4},... | collective-permute-start | bytes 786440 | tf_op jit(solution)/shard_map/ppermute | solution.py:409
  75.5 2.3 %collective-permute-start.7 = (bf16[2,128,512]{2,1,0:T(8,128)(2,1)}, bf16[2,128,512]{2,1,0:T(8,128)(2,1)S(1)}, u32[]{:S(2)}, u32[]{:S(2)}) collective-permute-start(bf16[2,128,512]{2,1,0:T(8,128)(2,1)} %get-tuple-element.63), channel_id=1, source_target_pairs={{0,24},{2,26},{4,28},{6,30},{8,16},{10,18},{12,20},{14,22},{16,8},... | collective-permute-start | bytes 786440 | tf_op jit(solution)/shard_map/ppermute | solution.py:409
  77.8 1.4 %collective-permute-start.8 = (bf16[2,128,512]{2,1,0:T(8,128)(2,1)}, bf16[2,128,512]{2,1,0:T(8,128)(2,1)S(1)}, u32[]{:S(2)}, u32[]{:S(2)}) collective-permute-start(bf16[2,128,512]{2,1,0:T(8,128)(2,1)} %get-tuple-element.64), channel_id=1, source_target_pairs={{0,8},{2,10},{4,12},{6,14},{8,0},{10,2},{12,4},{14,6},{16,24},{18,... | collective-permute-start | bytes 786440 | tf_op jit(solution)/shard_map/ppermute | solution.py:409
  79.2 17.7 %long_conv.1.refs_2_ = bf16[16,128,512]{2,1,0:T(8,128)(2,1)} custom-call(s32[16]{0:T(128)} %doc.7, s32[16]{0:T(128)} %live.7, f32[128,1]{1,0:T(8,128)} %get-tuple-element.45.skip, bf16[128,576,256]{2,1,0:T(8,128)(2,1)} %get-tuple-element.51.toeplitz, bf16[16,128,512]{2,1,0:T(8,128)(2,1)} %copy-done.2), custom_call_target="tpu_custom_call" | custom-call | flops 1 | bytes 1 | tf_op jit(solution)/shard_map/long_conv/pallas_call | solution.py:310
  97.0 2.6 %gate.4 = (bf16[128,1024]{1,0:T(8,128)(2,1)}, bf16[1,128,1024]{2,1,0:T(8,128)(2,1)}) custom-call(bf16[2,128,512]{2,1,0:T(8,128)(2,1)} %collective-permute-done.2.refs_0_, bf16[2,128,512]{2,1,0:T(8,128)(2,1)} %get-tuple-element.42.refs_1_, bf16[16,128,512]{2,1,0:T(8,128)(2,1)} %long_conv.1.refs_2_), custom_call_target="tpu_custom_call" | custom-call | flops 1 | bytes 1 | tf_op jit(solution)/shard_map/gate/pallas_call | solution.py:373
  99.6 2.5 %collective-permute-start.10 = (bf16[2,128,512]{2,1,0:T(8,128)(2,1)S(1)}, bf16[2,128,512]{2,1,0:T(8,128)(2,1)S(1)}, u32[]{:S(2)}, u32[]{:S(2)}) collective-permute-start(bf16[2,128,512]{2,1,0:T(8,128)(2,1)S(1)} %copy-done.16), channel_id=1, source_target_pairs={{0,28},{2,30},{4,24},{6,26},{8,20},{10,22},{12,16},{14,18},{16,12}... | collective-permute-start | bytes 786440 | tf_op jit(solution)/shard_map/ppermute | solution.py:409
  102.0 1.5 %collective-permute-start.4 = (bf16[128,1024]{1,0:T(8,128)(2,1)}, bf16[128,1024]{1,0:T(8,128)(2,1)S(1)}, u32[]{:S(2)}, u32[]{:S(2)}) collective-permute-start(bf16[128,1024]{1,0:T(8,128)(2,1)} %bitcast.22), channel_id=1, source_target_pairs={{0,1},{1,0},{2,3},{3,2},{4,5},{5,4},{6,7},{7,6},{8,9},{9,8},{10,11... | collective-permute-start | bytes 786440 | tf_op jit(solution)/shard_map/ppermute | solution.py:457
  103.9 2.6 %gate.5 = (bf16[128,1024]{1,0:T(8,128)(2,1)}, bf16[1,128,1024]{2,1,0:T(8,128)(2,1)}) custom-call(bf16[2,128,512]{2,1,0:T(8,128)(2,1)} %copy-done.10, bf16[2,128,512]{2,1,0:T(8,128)(2,1)} %copy-done.6, bf16[16,128,512]{2,1,0:T(8,128)(2,1)} %long_conv.1.refs_2_), custom_call_target="tpu_custom_call" | custom-call | flops 1 | bytes 1 | tf_op jit(solution)/shard_map/gate/pallas_call | solution.py:373
  107.1 0.7 copy-done.8
  107.8 2.5 %gate.6 = (bf16[128,1024]{1,0:T(8,128)(2,1)}, bf16[1,128,1024]{2,1,0:T(8,128)(2,1)}) custom-call(bf16[2,128,512]{2,1,0:T(8,128)(2,1)} %copy-done.7, bf16[2,128,512]{2,1,0:T(8,128)(2,1)} %copy-done.8, bf16[16,128,512]{2,1,0:T(8,128)(2,1)} %long_conv.1.refs_2_), custom_call_target="tpu_custom_call" | custom-call | flops 1 | bytes 1 | tf_op jit(solution)/shard_map/gate/pallas_call | solution.py:373
  110.4 1.5 %collective-permute-start.9 = (bf16[128,1024]{1,0:T(8,128)(2,1)}, bf16[128,1024]{1,0:T(8,128)(2,1)S(1)}, u32[]{:S(2)}, u32[]{:S(2)}) collective-permute-start(bf16[128,1024]{1,0:T(8,128)(2,1)} %bitcast.24), channel_id=1, source_target_pairs={{0,1},{1,0},{2,3},{3,2},{4,5},{5,4},{6,7},{7,6},{8,9},{9,8},{10,11... | collective-permute-start | bytes 786440 | tf_op jit(solution)/shard_map/ppermute | solution.py:457
  111.9 0.7 copy-done.5
  112.6 0.7 copy-done.9
  113.3 2.6 %gate.7 = (bf16[128,1024]{1,0:T(8,128)(2,1)}, bf16[1,128,1024]{2,1,0:T(8,128)(2,1)}) custom-call(bf16[2,128,512]{2,1,0:T(8,128)(2,1)} %copy-done.9, bf16[2,128,512]{2,1,0:T(8,128)(2,1)} %copy-done.5, bf16[16,128,512]{2,1,0:T(8,128)(2,1)} %long_conv.1.refs_2_), custom_call_target="tpu_custom_call" | custom-call | flops 1 | bytes 1 | tf_op jit(solution)/shard_map/gate/pallas_call | solution.py:373
  115.9 0.6 collective-permute-start.12
  117.2 5.5 %collective-permute-done.9 = bf16[128,1024]{1,0:T(8,128)(2,1)S(1)} collective-permute-done((bf16[128,1024]{1,0:T(8,128)(2,1)}, bf16[128,1024]{1,0:T(8,128)(2,1)S(1)}, u32[]{:S(2)}, u32[]{:S(2)}) %collective-permute-start.9) | collective-permute-done | bytes 262176 | tf_op jit(solution)/shard_map/ppermute | solution.py:457
  122.8 4.2 %collective-permute-done.12 = bf16[128,1024]{1,0:T(8,128)(2,1)S(1)} collective-permute-done((bf16[128,1024]{1,0:T(8,128)(2,1)}, bf16[128,1024]{1,0:T(8,128)(2,1)S(1)}, u32[]{:S(2)}, u32[]{:S(2)}) %collective-permute-start.12) | collective-permute-done | bytes 262176 | tf_op jit(solution)/shard_map/ppermute | solution.py:457
  127.0 0.7 bitcast_dynamic-update-slice_fusion
  (52 shorter events, 3.3 us)
Async XLA Ops:
  0.0 33.1 %copy-start = (f32[2048]{0:T(1024)S(1)}, f32[2048]{0:T(1024)}, u32[]{:S(2)}) copy-start(f32[2048]{0:T(1024)} %param.9) | copy-start | bytes 24580
  0.9 8.7 %collective-permute-start = (bf16[3,2,2048]{2,1,0:T(2,128)(2,1)S(1)}, bf16[3,2,2048]{2,1,0:T(2,128)(2,1)S(1)}, u32[]{:S(2)}, u32[]{:S(2)}) collective-permute-start(bf16[3,2,2048]{2,1,0:T(2,128)(2,1)S(1)} %slice.3), channel_id=1, source_target_pairs={{0,2},{2,4},{4,6},{6,8},{8,10},{10,12},{12,14},{14,16},{16,18},{18... | collective-permute-start | bytes 73736 | tf_op jit(solution)/shard_map/ppermute | solution.py:401
  9.7 0.6 copy-start.15
  12.5 56.5 %all-to-all-start = ((bf16[16,128,512]{2,1,0:T(8,128)(2,1)}), bf16[16,128,512]{2,1,0:T(8,128)(2,1)S(1)}, u32[]{:S(2)}, u32[]{:S(2)}) async-start(bf16[16,128,512]{2,1,0:T(8,128)(2,1)} %first_tokens.1), calls=%async_computation | async-start | bytes 4194304 | tf_op jit(solution)/shard_map/all_to_all | solution.py:415
  24.4 2.9 %collective-permute-start.1 = (bf16[8,128,512]{2,1,0:T(8,128)(2,1)}, bf16[8,128,512]{2,1,0:T(8,128)(2,1)S(1)}, u32[]{:S(2)}, u32[]{:S(2)}) collective-permute-start(bf16[8,128,512]{2,1,0:T(8,128)(2,1)} %get-tuple-element.40), channel_id=1, source_target_pairs={{0,2},{2,0},{4,6},{6,4},{8,10},{10,8},{12,14},{14,12},{16,18},{18,... | collective-permute-start | bytes 3145736 | tf_op jit(solution)/shard_map/ppermute | solution.py:409
  27.3 1.0 copy-start.4
  31.3 14.5 %collective-permute-start.3 = (bf16[2,128,512]{2,1,0:T(8,128)(2,1)}, bf16[2,128,512]{2,1,0:T(8,128)(2,1)S(1)}, u32[]{:S(2)}, u32[]{:S(2)}) collective-permute-start(bf16[2,128,512]{2,1,0:T(8,128)(2,1)} %get-tuple-element.43), channel_id=1, source_target_pairs={{0,4},{2,6},{4,0},{6,2},{8,12},{10,14},{12,8},{14,10},{16,20},{18,... | collective-permute-start | bytes 786440 | tf_op jit(solution)/shard_map/ppermute | solution.py:409
  35.6 61.3 %collective-permute-start.2 = (bf16[2,128,512]{2,1,0:T(8,128)(2,1)}, bf16[2,128,512]{2,1,0:T(8,128)(2,1)}, u32[]{:S(2)}, u32[]{:S(2)}) collective-permute-start(bf16[2,128,512]{2,1,0:T(8,128)(2,1)} %get-tuple-element.41), channel_id=1, source_target_pairs={{0,16},{2,18},{4,20},{6,22},{8,24},{10,26},{12,28},{14,30},{16,0},... | collective-permute-start | bytes 786440 | tf_op jit(solution)/shard_map/ppermute | solution.py:409
  45.8 51.1 %copy-start.6 = (bf16[2,128,512]{2,1,0:T(8,128)(2,1)}, bf16[2,128,512]{2,1,0:T(8,128)(2,1)S(1)}, u32[]{:S(2)}) copy-start(bf16[2,128,512]{2,1,0:T(8,128)(2,1)S(1)} %collective-permute-done.3.refs_1_) | copy-start | bytes 786436
  69.0 10.2 %copy-start.2 = (bf16[16,128,512]{2,1,0:T(8,128)(2,1)}, bf16[16,128,512]{2,1,0:T(8,128)(2,1)S(1)}, u32[]{:S(2)}) copy-start(bf16[16,128,512]{2,1,0:T(8,128)(2,1)S(1)} %all-to-all-done.gated) | copy-start | bytes 6291460
  69.1 33.0 %collective-permute-start.5 = (bf16[2,128,512]{2,1,0:T(8,128)(2,1)}, bf16[2,128,512]{2,1,0:T(8,128)(2,1)S(1)}, u32[]{:S(2)}, u32[]{:S(2)}) collective-permute-start(bf16[2,128,512]{2,1,0:T(8,128)(2,1)} %get-tuple-element.59), channel_id=1, source_target_pairs={{0,20},{2,22},{4,16},{6,18},{8,28},{10,30},{12,24},{14,26},{16,4},... | collective-permute-start | bytes 786440 | tf_op jit(solution)/shard_map/ppermute | solution.py:409
  75.5 36.4 %collective-permute-start.11 = (bf16[2,128,512]{2,1,0:T(8,128)(2,1)}, bf16[2,128,512]{2,1,0:T(8,128)(2,1)S(1)}, u32[]{:S(2)}, u32[]{:S(2)}) collective-permute-start(bf16[2,128,512]{2,1,0:T(8,128)(2,1)} %get-tuple-element.68), channel_id=1, source_target_pairs={{0,12},{2,14},{4,8},{6,10},{8,4},{10,6},{12,0},{14,2},{16,28},{18,... | collective-permute-start | bytes 786440 | tf_op jit(solution)/shard_map/ppermute | solution.py:409
  75.5 31.0 %collective-permute-start.7 = (bf16[2,128,512]{2,1,0:T(8,128)(2,1)}, bf16[2,128,512]{2,1,0:T(8,128)(2,1)S(1)}, u32[]{:S(2)}, u32[]{:S(2)}) collective-permute-start(bf16[2,128,512]{2,1,0:T(8,128)(2,1)} %get-tuple-element.63), channel_id=1, source_target_pairs={{0,24},{2,26},{4,28},{6,30},{8,16},{10,18},{12,20},{14,22},{16,8},... | collective-permute-start | bytes 786440 | tf_op jit(solution)/shard_map/ppermute | solution.py:409
  77.8 29.2 %collective-permute-start.8 = (bf16[2,128,512]{2,1,0:T(8,128)(2,1)}, bf16[2,128,512]{2,1,0:T(8,128)(2,1)S(1)}, u32[]{:S(2)}, u32[]{:S(2)}) collective-permute-start(bf16[2,128,512]{2,1,0:T(8,128)(2,1)} %get-tuple-element.64), channel_id=1, source_target_pairs={{0,8},{2,10},{4,12},{6,14},{8,0},{10,2},{12,4},{14,6},{16,24},{18,... | collective-permute-start | bytes 786440 | tf_op jit(solution)/shard_map/ppermute | solution.py:409
  96.9 2.6 %copy-start.16 = (bf16[2,128,512]{2,1,0:T(8,128)(2,1)S(1)}, bf16[2,128,512]{2,1,0:T(8,128)(2,1)}, u32[]{:S(2)}) copy-start(bf16[2,128,512]{2,1,0:T(8,128)(2,1)} %get-tuple-element.67) | copy-start | bytes 786436
  99.6 4.2 %copy-start.11 = (bf16[128,1024]{1,0:T(8,128)(2,1)S(1)}, bf16[128,1024]{1,0:T(8,128)(2,1)}, u32[]{:S(2)}) copy-start(bf16[128,1024]{1,0:T(8,128)(2,1)} %get-tuple-element.55) | copy-start | bytes 786436
  99.6 12.3 %collective-permute-start.10 = (bf16[2,128,512]{2,1,0:T(8,128)(2,1)S(1)}, bf16[2,128,512]{2,1,0:T(8,128)(2,1)S(1)}, u32[]{:S(2)}, u32[]{:S(2)}) collective-permute-start(bf16[2,128,512]{2,1,0:T(8,128)(2,1)S(1)} %copy-done.16), channel_id=1, source_target_pairs={{0,28},{2,30},{4,24},{6,26},{8,20},{10,22},{12,16},{14,18},{16,12}... | collective-permute-start | bytes 786440 | tf_op jit(solution)/shard_map/ppermute | solution.py:409
  102.0 1.8 %copy-start.10 = (bf16[2,128,512]{2,1,0:T(8,128)(2,1)}, bf16[2,128,512]{2,1,0:T(8,128)(2,1)S(1)}, u32[]{:S(2)}) copy-start(bf16[2,128,512]{2,1,0:T(8,128)(2,1)S(1)} %collective-permute-done.5.refs_0_) | copy-start | bytes 786436
  102.0 14.4 %collective-permute-start.4 = (bf16[128,1024]{1,0:T(8,128)(2,1)}, bf16[128,1024]{1,0:T(8,128)(2,1)S(1)}, u32[]{:S(2)}, u32[]{:S(2)}) collective-permute-start(bf16[128,1024]{1,0:T(8,128)(2,1)} %bitcast.22), channel_id=1, source_target_pairs={{0,1},{1,0},{2,3},{3,2},{4,5},{5,4},{6,7},{7,6},{8,9},{9,8},{10,11... | collective-permute-start | bytes 786440 | tf_op jit(solution)/shard_map/ppermute | solution.py:457
  106.4 0.7 copy-start.7
  106.4 10.7 %collective-permute-start.6 = (bf16[128,1024]{1,0:T(8,128)(2,1)}, bf16[128,1024]{1,0:T(8,128)(2,1)S(1)}, u32[]{:S(2)}, u32[]{:S(2)}) collective-permute-start(bf16[128,1024]{1,0:T(8,128)(2,1)} %bitcast.23), channel_id=1, source_target_pairs={{0,1},{1,0},{2,3},{3,2},{4,5},{5,4},{6,7},{7,6},{8,9},{9,8},{10,11... | collective-permute-start | bytes 786440 | tf_op jit(solution)/shard_map/ppermute | solution.py:457
  107.1 0.7 copy-start.8
  110.4 6.1 %copy-start.12 = (bf16[128,1024]{1,0:T(8,128)(2,1)S(1)}, bf16[128,1024]{1,0:T(8,128)(2,1)}, u32[]{:S(2)}) copy-start(bf16[128,1024]{1,0:T(8,128)(2,1)} %get-tuple-element.61) | copy-start | bytes 786436
  110.4 6.8 %copy-start.13 = (bf16[128,1024]{1,0:T(8,128)(2,1)S(1)}, bf16[128,1024]{1,0:T(8,128)(2,1)}, u32[]{:S(2)}) copy-start(bf16[128,1024]{1,0:T(8,128)(2,1)} %get-tuple-element.65) | copy-start | bytes 786436
  110.4 12.3 %collective-permute-start.9 = (bf16[128,1024]{1,0:T(8,128)(2,1)}, bf16[128,1024]{1,0:T(8,128)(2,1)S(1)}, u32[]{:S(2)}, u32[]{:S(2)}) collective-permute-start(bf16[128,1024]{1,0:T(8,128)(2,1)} %bitcast.24), channel_id=1, source_target_pairs={{0,1},{1,0},{2,3},{3,2},{4,5},{5,4},{6,7},{7,6},{8,9},{9,8},{10,11... | collective-permute-start | bytes 786440 | tf_op jit(solution)/shard_map/ppermute | solution.py:457
  111.9 0.7 copy-start.5
  112.6 0.7 copy-start.9
  113.3 14.4 %copy-start.1 = (f32[2048]{0:T(1024)S(1)}, f32[2048]{0:T(1024)}, u32[]{:S(2)}) copy-start(f32[2048]{0:T(1024)} %param.9) | copy-start | bytes 24580
  115.9 6.9 %copy-start.14 = (bf16[128,1024]{1,0:T(8,128)(2,1)S(1)}, bf16[128,1024]{1,0:T(8,128)(2,1)}, u32[]{:S(2)}) copy-start(bf16[128,1024]{1,0:T(8,128)(2,1)} %get-tuple-element.69) | copy-start | bytes 786436
  115.9 11.1 %collective-permute-start.12 = (bf16[128,1024]{1,0:T(8,128)(2,1)}, bf16[128,1024]{1,0:T(8,128)(2,1)S(1)}, u32[]{:S(2)}, u32[]{:S(2)}) collective-permute-start(bf16[128,1024]{1,0:T(8,128)(2,1)} %bitcast.25), channel_id=1, source_target_pairs={{0,1},{1,0},{2,3},{3,2},{4,5},{5,4},{6,7},{7,6},{8,9},{9,8},{10,11... | collective-permute-start | bytes 786440 | tf_op jit(solution)/shard_map/ppermute | solution.py:457
  122.8 4.2 %copy-start.3 = (bf16[2,128,4096]{2,1,0:T(8,128)(2,1)}, bf16[2,128,4096]{2,1,0:T(8,128)(2,1)S(1)}, u32[]{:S(2)}) copy-start(bf16[2,128,4096]{2,1,0:T(8,128)(2,1)S(1)} %bitcast_dynamic-update-slice_fusion.1) | copy-start | bytes 6291460

commit v5 on v4

--- a/solution.py
+++ b/solution.py
@@ -321,10 +321,10 @@
         out_shape=jax.ShapeDtypeStruct((shards, width, tok), jnp.bfloat16),
         scratch_shapes=[
             pltpu.VMEM((pairs + 1, blocks, LANES), jnp.bfloat16),
-            pltpu.VMEM((tall * (chans + 1), LANES), jnp.float32),
+            pltpu.VMEM(((tall + 1) * (chans + 1), LANES), jnp.float32),
             pltpu.VMEM((UNROLL, tall, LANES), jnp.float32),
             pltpu.VMEM((UNROLL, blocks + 8, LANES), jnp.float32),
-            pltpu.VMEM((blocks * (chans + 1), LANES), jnp.float32),
+            pltpu.VMEM(((blocks + 1) * (chans + 1), LANES), jnp.float32),
         ],
         compiler_params=pltpu.CompilerParams(
             vmem_limit_bytes=VMEM, dimension_semantics=("arbitrary",)

time: 128 us -> 128 us (level)
  no operation moved by 1% of the time
where the time goes in v5:
time: 128 us; the launch traced here: 127 us
  Pallas kernels  67.3 us (53%)
  starting transfers between devices  31 us (24%)
  waiting for transfers between devices  20.6 us (16%)
  local copies, waits for them, and re-layouts  8.4 us (7%)
    pallas_call x1, Pallas kernels, prepare(): pl.pallas_call(prepare_kernel, grid=(part // chans,), in_specs=[pl.BlockS...  23.2 us
    pallas_call x1, Pallas kernels, long_conv(): pl.pallas_call(conv_kernel, grid=(width // chans,), in_specs=[smem, smem,...  17.5 us
    ppermute x8, starting transfers between devices, across(): lax.ppermute(block, 'ctx', [(i, i ^ distance) for i in range(shards)])  17.3 us
    pallas_call x2, Pallas kernels, short_convs(): pl.pallas_call(functools.partial(short_kernel, count, len(borders)), grid...  11 us
    ppermute x8, waiting for transfers between devices, across(): lax.ppermute(block, 'ctx', [(i, i ^ distance) for i in range(shards)])  10.3 us
    pallas_call x4, Pallas kernels, gate(): pl.pallas_call(functools.partial(gate_kernel, fars), grid=(width // chans...  10.3 us
    ppermute x4, waiting for transfers between devices, local(): came = lax.ppermute(sent[d - 1], 'ch', route)  10.3 us
    all_to_all x1, starting transfers between devices, local(): gated = lax.all_to_all(gated, 'ctx', 0, 0)  7.19 us
  transfers between devices with their start and end apart: 14, of which 5 were waited for; matrix products, arithmetic and copies ran while one was open for 2% of the time, Pallas kernels for 51%

profile of v5, /device:TPU:0, one launch (start us, length us, event | category | flops | bytes accessed | tf_op | source)
XLA Modules:
  0.0 127.5 jit_solution(15059437235501925584)
XLA Ops:
  0.0 0.9 slice.3
  0.9 2.4 %collective-permute-start = (bf16[3,2,2048]{2,1,0:T(2,128)(2,1)S(1)}, bf16[3,2,2048]{2,1,0:T(2,128)(2,1)S(1)}, u32[]{:S(2)}, u32[]{:S(2)}) collective-permute-start(bf16[3,2,2048]{2,1,0:T(2,128)(2,1)S(1)} %slice.3), channel_id=1, source_target_pairs={{0,2},{2,4},{4,6},{6,8},{8,10},{10,12},{12,14},{14,16},{16,18},{18... | collective-permute-start | bytes 73736 | tf_op jit(solution)/shard_map/ppermute | solution.py:401
  3.3 6.4 %short_kv.1.old = bf16[16,128,512]{2,1,0:T(8,128)(2,1)} custom-call(s32[16]{0:T(128)} %doc.7, s32[16]{0:T(128)} %live.7, f32[3,3,2048]{2,1,0:T(4,128)} %refs_0_.3, f32[3,3,2048]{2,1,0:T(4,128)} %refs_0_.3, bf16[3,512,2048]{2,1,0:T(8,128)(2,1)} %refs_1_.2, bf16[3,512,2048]{2,1,0:T(8,128)(2,1)} %refs_1_.2), custom_call_target="tpu_custom_call" | custom-call | tf_op jit(solution)/shard_map/short_kv/pallas_call | solution.py:80
  10.3 2.2 %first_tokens.1 = bf16[16,128,512]{2,1,0:T(8,128)(2,1)} custom-call(s32[16]{0:T(128)} %doc.7, s32[16]{0:T(128)} %live.7, bf16[3,2,2048]{2,1,0:T(2,128)(2,1)} %copy-done.15, bf16[3,2,2048]{2,1,0:T(2,128)(2,1)} %copy-done.15, f32[3,3,2048]{2,1,0:T(4,128)} %refs_0_.3, f32[3,3,2048]{2,1,0:T(4,128)} %refs_0_.3, ...), custom_call_target="tpu_custom_call", output_to_operand_aliasing={{}: (8, {})} | custom-call | tf_op jit(solution)/shard_map/first_tokens/pallas_call | solution.py:126
  12.5 7.2 %all-to-all-start = ((bf16[16,128,512]{2,1,0:T(8,128)(2,1)}), bf16[16,128,512]{2,1,0:T(8,128)(2,1)S(1)}, u32[]{:S(2)}, u32[]{:S(2)}) async-start(bf16[16,128,512]{2,1,0:T(8,128)(2,1)} %first_tokens.1), calls=%async_computation | async-start | bytes 4194304 | tf_op jit(solution)/shard_map/all_to_all | solution.py:415
  19.7 4.7 %short_q.1 = (bf16[8,128,512]{2,1,0:T(8,128)(2,1)}, bf16[8,128,512]{2,1,0:T(8,128)(2,1)}) custom-call(s32[16]{0:T(128)} %doc.7, s32[16]{0:T(128)} %live.7, f32[3,3,2048]{2,1,0:T(4,128)} %refs_0_.3, bf16[3,512,2048]{2,1,0:T(8,128)(2,1)} %refs_1_.2, bf16[3,2,2048]{2,1,0:T(2,128)(2,1)} %copy-done.15), custom_call_target="tpu_custom_call" | custom-call | tf_op jit(solution)/shard_map/short_q/pallas_call | solution.py:80
  24.8 2.5 %collective-permute-done.1.refs_1_ = bf16[8,128,512]{2,1,0:T(8,128)(2,1)S(1)} collective-permute-done((bf16[8,128,512]{2,1,0:T(8,128)(2,1)}, bf16[8,128,512]{2,1,0:T(8,128)(2,1)S(1)}, u32[]{:S(2)}, u32[]{:S(2)}) %collective-permute-start.1) | collective-permute-done | bytes 1048608 | tf_op jit(solution)/shard_map/ppermute | solution.py:409
  27.3 1.0 copy-done.4
  28.3 3.0 %pair_up.1 = (bf16[2,128,512]{2,1,0:T(8,128)(2,1)}, bf16[2,128,512]{2,1,0:T(8,128)(2,1)}, bf16[2,128,512]{2,1,0:T(8,128)(2,1)}, bf16[2,128,512]{2,1,0:T(8,128)(2...) custom-call(bf16[8,128,512]{2,1,0:T(8,128)(2,1)} %get-tuple-element., ...), custom_call_target="tpu_custom_call" | custom-call | tf_op jit(solution)/shard_map/pair_up/pallas_call | solution.py:150
  31.3 1.9 %collective-permute-start.3 = (bf16[2,128,512]{2,1,0:T(8,128)(2,1)}, bf16[2,128,512]{2,1,0:T(8,128)(2,1)S(1)}, u32[]{:S(2)}, u32[]{:S(2)}) collective-permute-start(bf16[2,128,512]{2,1,0:T(8,128)(2,1)} %get-tuple-element.43), channel_id=1, source_target_pairs={{0,4},{2,6},{4,0},{6,2},{8,12},{10,14},{12,8},{14,10},{16,20},{18,... | collective-permute-start | bytes 786440 | tf_op jit(solution)/shard_map/ppermute | solution.py:409
  33.7 1.9 %constant_dynamic-slice_fusion.filt = bf16[2048,128]{1,0:T(8,128)(2,1)} fusion(bf16[2048,2048]{1,0:T(8,128)(2,1)} %param.8, s32[]{:T(128)S(6)} %select_n.56), kind=kLoop, calls=%fused_computation.8 | loop fusion | bytes 1048580 | tf_op jit(solution)/shard_map/dynamic_slice | solution.py:404
  35.6 2.4 %collective-permute-start.2 = (bf16[2,128,512]{2,1,0:T(8,128)(2,1)}, bf16[2,128,512]{2,1,0:T(8,128)(2,1)}, u32[]{:S(2)}, u32[]{:S(2)}) collective-permute-start(bf16[2,128,512]{2,1,0:T(8,128)(2,1)} %get-tuple-element.41), channel_id=1, source_target_pairs={{0,16},{2,18},{4,20},{6,22},{8,24},{10,26},{12,28},{14,30},{16,0},... | collective-permute-start | bytes 786440 | tf_op jit(solution)/shard_map/ppermute | solution.py:409
  38.0 7.8 %collective-permute-done.3.refs_1_ = bf16[2,128,512]{2,1,0:T(8,128)(2,1)S(1)} collective-permute-done((bf16[2,128,512]{2,1,0:T(8,128)(2,1)}, bf16[2,128,512]{2,1,0:T(8,128)(2,1)S(1)}, u32[]{:S(2)}, u32[]{:S(2)}) %collective-permute-start.3) | collective-permute-done | bytes 262176 | tf_op jit(solution)/shard_map/ppermute | solution.py:409
  45.8 23.2 %prepare.1 = (bf16[128,576,256]{2,1,0:T(8,128)(2,1)}, f32[128,1]{1,0:T(8,128)}) custom-call(bf16[2048,128]{1,0:T(8,128)(2,1)} %constant_dynamic-slice_fusion.filt, f32[1,128]{1,0:T(1,128)} %dynamic-slice_bitcast_fusion.skip), custom_call_target="tpu_custom_call" | custom-call | tf_op jit(solution)/shard_map/prepare/pallas_call | solution.py:189
  69.1 6.4 %collective-permute-start.5 = (bf16[2,128,512]{2,1,0:T(8,128)(2,1)}, bf16[2,128,512]{2,1,0:T(8,128)(2,1)S(1)}, u32[]{:S(2)}, u32[]{:S(2)}) collective-permute-start(bf16[2,128,512]{2,1,0:T(8,128)(2,1)} %get-tuple-element.59), channel_id=1, source_target_pairs={{0,20},{2,22},{4,16},{6,18},{8,28},{10,30},{12,24},{14,26},{16,4},... | collective-permute-start | bytes 786440 | tf_op jit(solution)/shard_map/ppermute | solution.py:409
  75.5 2.3 %collective-permute-start.7 = (bf16[2,128,512]{2,1,0:T(8,128)(2,1)}, bf16[2,128,512]{2,1,0:T(8,128)(2,1)S(1)}, u32[]{:S(2)}, u32[]{:S(2)}) collective-permute-start(bf16[2,128,512]{2,1,0:T(8,128)(2,1)} %get-tuple-element.63), channel_id=1, source_target_pairs={{0,24},{2,26},{4,28},{6,30},{8,16},{10,18},{12,20},{14,22},{16,8},... | collective-permute-start | bytes 786440 | tf_op jit(solution)/shard_map/ppermute | solution.py:409
  77.8 1.4 %collective-permute-start.8 = (bf16[2,128,512]{2,1,0:T(8,128)(2,1)}, bf16[2,128,512]{2,1,0:T(8,128)(2,1)S(1)}, u32[]{:S(2)}, u32[]{:S(2)}) collective-permute-start(bf16[2,128,512]{2,1,0:T(8,128)(2,1)} %get-tuple-element.64), channel_id=1, source_target_pairs={{0,8},{2,10},{4,12},{6,14},{8,0},{10,2},{12,4},{14,6},{16,24},{18,... | collective-permute-start | bytes 786440 | tf_op jit(solution)/shard_map/ppermute | solution.py:409
  79.2 17.5 %long_conv.1.refs_2_ = bf16[16,128,512]{2,1,0:T(8,128)(2,1)} custom-call(s32[16]{0:T(128)} %doc.7, s32[16]{0:T(128)} %live.7, f32[128,1]{1,0:T(8,128)} %get-tuple-element.45.skip, bf16[128,576,256]{2,1,0:T(8,128)(2,1)} %get-tuple-element.51.toeplitz, bf16[16,128,512]{2,1,0:T(8,128)(2,1)} %copy-done.2), custom_call_target="tpu_custom_call" | custom-call | flops 1 | bytes 1 | tf_op jit(solution)/shard_map/long_conv/pallas_call | solution.py:310
  96.7 2.6 %gate.4 = (bf16[128,1024]{1,0:T(8,128)(2,1)}, bf16[1,128,1024]{2,1,0:T(8,128)(2,1)}) custom-call(bf16[2,128,512]{2,1,0:T(8,128)(2,1)} %collective-permute-done.2.refs_0_, bf16[2,128,512]{2,1,0:T(8,128)(2,1)} %get-tuple-element.42.refs_1_, bf16[16,128,512]{2,1,0:T(8,128)(2,1)} %long_conv.1.refs_2_), custom_call_target="tpu_custom_call" | custom-call | flops 1 | bytes 1 | tf_op jit(solution)/shard_map/gate/pallas_call | solution.py:373
  99.3 2.5 %collective-permute-start.10 = (bf16[2,128,512]{2,1,0:T(8,128)(2,1)S(1)}, bf16[2,128,512]{2,1,0:T(8,128)(2,1)S(1)}, u32[]{:S(2)}, u32[]{:S(2)}) collective-permute-start(bf16[2,128,512]{2,1,0:T(8,128)(2,1)S(1)} %copy-done.16), channel_id=1, source_target_pairs={{0,28},{2,30},{4,24},{6,26},{8,20},{10,22},{12,16},{14,18},{16,12}... | collective-permute-start | bytes 786440 | tf_op jit(solution)/shard_map/ppermute | solution.py:409
  101.8 1.5 %collective-permute-start.4 = (bf16[128,1024]{1,0:T(8,128)(2,1)}, bf16[128,1024]{1,0:T(8,128)(2,1)S(1)}, u32[]{:S(2)}, u32[]{:S(2)}) collective-permute-start(bf16[128,1024]{1,0:T(8,128)(2,1)} %bitcast.22), channel_id=1, source_target_pairs={{0,1},{1,0},{2,3},{3,2},{4,5},{5,4},{6,7},{7,6},{8,9},{9,8},{10,11... | collective-permute-start | bytes 786440 | tf_op jit(solution)/shard_map/ppermute | solution.py:457
  103.6 2.6 %gate.5 = (bf16[128,1024]{1,0:T(8,128)(2,1)}, bf16[1,128,1024]{2,1,0:T(8,128)(2,1)}) custom-call(bf16[2,128,512]{2,1,0:T(8,128)(2,1)} %copy-done.10, bf16[2,128,512]{2,1,0:T(8,128)(2,1)} %copy-done.6, bf16[16,128,512]{2,1,0:T(8,128)(2,1)} %long_conv.1.refs_2_), custom_call_target="tpu_custom_call" | custom-call | flops 1 | bytes 1 | tf_op jit(solution)/shard_map/gate/pallas_call | solution.py:373
  106.9 0.7 copy-done.8
  107.6 2.5 %gate.6 = (bf16[128,1024]{1,0:T(8,128)(2,1)}, bf16[1,128,1024]{2,1,0:T(8,128)(2,1)}) custom-call(bf16[2,128,512]{2,1,0:T(8,128)(2,1)} %copy-done.7, bf16[2,128,512]{2,1,0:T(8,128)(2,1)} %copy-done.8, bf16[16,128,512]{2,1,0:T(8,128)(2,1)} %long_conv.1.refs_2_), custom_call_target="tpu_custom_call" | custom-call | flops 1 | bytes 1 | tf_op jit(solution)/shard_map/gate/pallas_call | solution.py:373
  110.2 1.5 %collective-permute-start.9 = (bf16[128,1024]{1,0:T(8,128)(2,1)}, bf16[128,1024]{1,0:T(8,128)(2,1)S(1)}, u32[]{:S(2)}, u32[]{:S(2)}) collective-permute-start(bf16[128,1024]{1,0:T(8,128)(2,1)} %bitcast.24), channel_id=1, source_target_pairs={{0,1},{1,0},{2,3},{3,2},{4,5},{5,4},{6,7},{7,6},{8,9},{9,8},{10,11... | collective-permute-start | bytes 786440 | tf_op jit(solution)/shard_map/ppermute | solution.py:457
  111.6 0.7 copy-done.5
  112.4 0.7 copy-done.9
  113.0 2.6 %gate.7 = (bf16[128,1024]{1,0:T(8,128)(2,1)}, bf16[1,128,1024]{2,1,0:T(8,128)(2,1)}) custom-call(bf16[2,128,512]{2,1,0:T(8,128)(2,1)} %copy-done.9, bf16[2,128,512]{2,1,0:T(8,128)(2,1)} %copy-done.5, bf16[16,128,512]{2,1,0:T(8,128)(2,1)} %long_conv.1.refs_2_), custom_call_target="tpu_custom_call" | custom-call | flops 1 | bytes 1 | tf_op jit(solution)/shard_map/gate/pallas_call | solution.py:373
  115.6 0.6 collective-permute-start.12
  117.0 5.5 %collective-permute-done.9 = bf16[128,1024]{1,0:T(8,128)(2,1)S(1)} collective-permute-done((bf16[128,1024]{1,0:T(8,128)(2,1)}, bf16[128,1024]{1,0:T(8,128)(2,1)S(1)}, u32[]{:S(2)}, u32[]{:S(2)}) %collective-permute-start.9) | collective-permute-done | bytes 262176 | tf_op jit(solution)/shard_map/ppermute | solution.py:457
  122.6 4.2 %collective-permute-done.12 = bf16[128,1024]{1,0:T(8,128)(2,1)S(1)} collective-permute-done((bf16[128,1024]{1,0:T(8,128)(2,1)}, bf16[128,1024]{1,0:T(8,128)(2,1)S(1)}, u32[]{:S(2)}, u32[]{:S(2)}) %collective-permute-start.12) | collective-permute-done | bytes 262176 | tf_op jit(solution)/shard_map/ppermute | solution.py:457
  126.8 0.7 bitcast_dynamic-update-slice_fusion
  (52 shorter events, 3.3 us)
Async XLA Ops:
  0.0 33.1 %copy-start = (f32[2048]{0:T(1024)S(1)}, f32[2048]{0:T(1024)}, u32[]{:S(2)}) copy-start(f32[2048]{0:T(1024)} %param.9) | copy-start | bytes 24580
  0.9 8.7 %collective-permute-start = (bf16[3,2,2048]{2,1,0:T(2,128)(2,1)S(1)}, bf16[3,2,2048]{2,1,0:T(2,128)(2,1)S(1)}, u32[]{:S(2)}, u32[]{:S(2)}) collective-permute-start(bf16[3,2,2048]{2,1,0:T(2,128)(2,1)S(1)} %slice.3), channel_id=1, source_target_pairs={{0,2},{2,4},{4,6},{6,8},{8,10},{10,12},{12,14},{14,16},{16,18},{18... | collective-permute-start | bytes 73736 | tf_op jit(solution)/shard_map/ppermute | solution.py:401
  9.7 0.6 copy-start.15
  12.5 56.5 %all-to-all-start = ((bf16[16,128,512]{2,1,0:T(8,128)(2,1)}), bf16[16,128,512]{2,1,0:T(8,128)(2,1)S(1)}, u32[]{:S(2)}, u32[]{:S(2)}) async-start(bf16[16,128,512]{2,1,0:T(8,128)(2,1)} %first_tokens.1), calls=%async_computation | async-start | bytes 4194304 | tf_op jit(solution)/shard_map/all_to_all | solution.py:415
  24.4 2.9 %collective-permute-start.1 = (bf16[8,128,512]{2,1,0:T(8,128)(2,1)}, bf16[8,128,512]{2,1,0:T(8,128)(2,1)S(1)}, u32[]{:S(2)}, u32[]{:S(2)}) collective-permute-start(bf16[8,128,512]{2,1,0:T(8,128)(2,1)} %get-tuple-element.40), channel_id=1, source_target_pairs={{0,2},{2,0},{4,6},{6,4},{8,10},{10,8},{12,14},{14,12},{16,18},{18,... | collective-permute-start | bytes 3145736 | tf_op jit(solution)/shard_map/ppermute | solution.py:409
  27.3 1.0 copy-start.4
  31.3 14.5 %collective-permute-start.3 = (bf16[2,128,512]{2,1,0:T(8,128)(2,1)}, bf16[2,128,512]{2,1,0:T(8,128)(2,1)S(1)}, u32[]{:S(2)}, u32[]{:S(2)}) collective-permute-start(bf16[2,128,512]{2,1,0:T(8,128)(2,1)} %get-tuple-element.43), channel_id=1, source_target_pairs={{0,4},{2,6},{4,0},{6,2},{8,12},{10,14},{12,8},{14,10},{16,20},{18,... | collective-permute-start | bytes 786440 | tf_op jit(solution)/shard_map/ppermute | solution.py:409
  35.6 61.1 %collective-permute-start.2 = (bf16[2,128,512]{2,1,0:T(8,128)(2,1)}, bf16[2,128,512]{2,1,0:T(8,128)(2,1)}, u32[]{:S(2)}, u32[]{:S(2)}) collective-permute-start(bf16[2,128,512]{2,1,0:T(8,128)(2,1)} %get-tuple-element.41), channel_id=1, source_target_pairs={{0,16},{2,18},{4,20},{6,22},{8,24},{10,26},{12,28},{14,30},{16,0},... | collective-permute-start | bytes 786440 | tf_op jit(solution)/shard_map/ppermute | solution.py:409
  45.8 50.9 %copy-start.6 = (bf16[2,128,512]{2,1,0:T(8,128)(2,1)}, bf16[2,128,512]{2,1,0:T(8,128)(2,1)S(1)}, u32[]{:S(2)}) copy-start(bf16[2,128,512]{2,1,0:T(8,128)(2,1)S(1)} %collective-permute-done.3.refs_1_) | copy-start | bytes 786436
  69.0 10.2 %copy-start.2 = (bf16[16,128,512]{2,1,0:T(8,128)(2,1)}, bf16[16,128,512]{2,1,0:T(8,128)(2,1)S(1)}, u32[]{:S(2)}) copy-start(bf16[16,128,512]{2,1,0:T(8,128)(2,1)S(1)} %all-to-all-done.gated) | copy-start | bytes 6291460
  69.1 32.8 %collective-permute-start.5 = (bf16[2,128,512]{2,1,0:T(8,128)(2,1)}, bf16[2,128,512]{2,1,0:T(8,128)(2,1)S(1)}, u32[]{:S(2)}, u32[]{:S(2)}) collective-permute-start(bf16[2,128,512]{2,1,0:T(8,128)(2,1)} %get-tuple-element.59), channel_id=1, source_target_pairs={{0,20},{2,22},{4,16},{6,18},{8,28},{10,30},{12,24},{14,26},{16,4},... | collective-permute-start | bytes 786440 | tf_op jit(solution)/shard_map/ppermute | solution.py:409
  75.5 36.2 %collective-permute-start.11 = (bf16[2,128,512]{2,1,0:T(8,128)(2,1)}, bf16[2,128,512]{2,1,0:T(8,128)(2,1)S(1)}, u32[]{:S(2)}, u32[]{:S(2)}) collective-permute-start(bf16[2,128,512]{2,1,0:T(8,128)(2,1)} %get-tuple-element.68), channel_id=1, source_target_pairs={{0,12},{2,14},{4,8},{6,10},{8,4},{10,6},{12,0},{14,2},{16,28},{18,... | collective-permute-start | bytes 786440 | tf_op jit(solution)/shard_map/ppermute | solution.py:409
  75.5 30.8 %collective-permute-start.7 = (bf16[2,128,512]{2,1,0:T(8,128)(2,1)}, bf16[2,128,512]{2,1,0:T(8,128)(2,1)S(1)}, u32[]{:S(2)}, u32[]{:S(2)}) collective-permute-start(bf16[2,128,512]{2,1,0:T(8,128)(2,1)} %get-tuple-element.63), channel_id=1, source_target_pairs={{0,24},{2,26},{4,28},{6,30},{8,16},{10,18},{12,20},{14,22},{16,8},... | collective-permute-start | bytes 786440 | tf_op jit(solution)/shard_map/ppermute | solution.py:409
  77.8 29.0 %collective-permute-start.8 = (bf16[2,128,512]{2,1,0:T(8,128)(2,1)}, bf16[2,128,512]{2,1,0:T(8,128)(2,1)S(1)}, u32[]{:S(2)}, u32[]{:S(2)}) collective-permute-start(bf16[2,128,512]{2,1,0:T(8,128)(2,1)} %get-tuple-element.64), channel_id=1, source_target_pairs={{0,8},{2,10},{4,12},{6,14},{8,0},{10,2},{12,4},{14,6},{16,24},{18,... | collective-permute-start | bytes 786440 | tf_op jit(solution)/shard_map/ppermute | solution.py:409
  96.7 2.6 %copy-start.16 = (bf16[2,128,512]{2,1,0:T(8,128)(2,1)S(1)}, bf16[2,128,512]{2,1,0:T(8,128)(2,1)}, u32[]{:S(2)}) copy-start(bf16[2,128,512]{2,1,0:T(8,128)(2,1)} %get-tuple-element.67) | copy-start | bytes 786436
  99.3 4.2 %copy-start.11 = (bf16[128,1024]{1,0:T(8,128)(2,1)S(1)}, bf16[128,1024]{1,0:T(8,128)(2,1)}, u32[]{:S(2)}) copy-start(bf16[128,1024]{1,0:T(8,128)(2,1)} %get-tuple-element.55) | copy-start | bytes 786436
  99.3 12.3 %collective-permute-start.10 = (bf16[2,128,512]{2,1,0:T(8,128)(2,1)S(1)}, bf16[2,128,512]{2,1,0:T(8,128)(2,1)S(1)}, u32[]{:S(2)}, u32[]{:S(2)}) collective-permute-start(bf16[2,128,512]{2,1,0:T(8,128)(2,1)S(1)} %copy-done.16), channel_id=1, source_target_pairs={{0,28},{2,30},{4,24},{6,26},{8,20},{10,22},{12,16},{14,18},{16,12}... | collective-permute-start | bytes 786440 | tf_op jit(solution)/shard_map/ppermute | solution.py:409
  101.8 1.8 %copy-start.10 = (bf16[2,128,512]{2,1,0:T(8,128)(2,1)}, bf16[2,128,512]{2,1,0:T(8,128)(2,1)S(1)}, u32[]{:S(2)}) copy-start(bf16[2,128,512]{2,1,0:T(8,128)(2,1)S(1)} %collective-permute-done.5.refs_0_) | copy-start | bytes 786436
  101.8 14.4 %collective-permute-start.4 = (bf16[128,1024]{1,0:T(8,128)(2,1)}, bf16[128,1024]{1,0:T(8,128)(2,1)S(1)}, u32[]{:S(2)}, u32[]{:S(2)}) collective-permute-start(bf16[128,1024]{1,0:T(8,128)(2,1)} %bitcast.22), channel_id=1, source_target_pairs={{0,1},{1,0},{2,3},{3,2},{4,5},{5,4},{6,7},{7,6},{8,9},{9,8},{10,11... | collective-permute-start | bytes 786440 | tf_op jit(solution)/shard_map/ppermute | solution.py:457
  106.2 0.7 copy-start.7
  106.2 10.7 %collective-permute-start.6 = (bf16[128,1024]{1,0:T(8,128)(2,1)}, bf16[128,1024]{1,0:T(8,128)(2,1)S(1)}, u32[]{:S(2)}, u32[]{:S(2)}) collective-permute-start(bf16[128,1024]{1,0:T(8,128)(2,1)} %bitcast.23), channel_id=1, source_target_pairs={{0,1},{1,0},{2,3},{3,2},{4,5},{5,4},{6,7},{7,6},{8,9},{9,8},{10,11... | collective-permute-start | bytes 786440 | tf_op jit(solution)/shard_map/ppermute | solution.py:457
  106.9 0.7 copy-start.8
  110.2 6.1 %copy-start.12 = (bf16[128,1024]{1,0:T(8,128)(2,1)S(1)}, bf16[128,1024]{1,0:T(8,128)(2,1)}, u32[]{:S(2)}) copy-start(bf16[128,1024]{1,0:T(8,128)(2,1)} %get-tuple-element.61) | copy-start | bytes 786436
  110.2 6.8 %copy-start.13 = (bf16[128,1024]{1,0:T(8,128)(2,1)S(1)}, bf16[128,1024]{1,0:T(8,128)(2,1)}, u32[]{:S(2)}) copy-start(bf16[128,1024]{1,0:T(8,128)(2,1)} %get-tuple-element.65) | copy-start | bytes 786436
  110.2 12.3 %collective-permute-start.9 = (bf16[128,1024]{1,0:T(8,128)(2,1)}, bf16[128,1024]{1,0:T(8,128)(2,1)S(1)}, u32[]{:S(2)}, u32[]{:S(2)}) collective-permute-start(bf16[128,1024]{1,0:T(8,128)(2,1)} %bitcast.24), channel_id=1, source_target_pairs={{0,1},{1,0},{2,3},{3,2},{4,5},{5,4},{6,7},{7,6},{8,9},{9,8},{10,11... | collective-permute-start | bytes 786440 | tf_op jit(solution)/shard_map/ppermute | solution.py:457
  111.6 0.7 copy-start.5
  112.3 0.7 copy-start.9
  113.0 14.4 %copy-start.1 = (f32[2048]{0:T(1024)S(1)}, f32[2048]{0:T(1024)}, u32[]{:S(2)}) copy-start(f32[2048]{0:T(1024)} %param.9) | copy-start | bytes 24580
  115.6 6.9 %copy-start.14 = (bf16[128,1024]{1,0:T(8,128)(2,1)S(1)}, bf16[128,1024]{1,0:T(8,128)(2,1)}, u32[]{:S(2)}) copy-start(bf16[128,1024]{1,0:T(8,128)(2,1)} %get-tuple-element.69) | copy-start | bytes 786436
  115.6 11.1 %collective-permute-start.12 = (bf16[128,1024]{1,0:T(8,128)(2,1)}, bf16[128,1024]{1,0:T(8,128)(2,1)S(1)}, u32[]{:S(2)}, u32[]{:S(2)}) collective-permute-start(bf16[128,1024]{1,0:T(8,128)(2,1)} %bitcast.25), channel_id=1, source_target_pairs={{0,1},{1,0},{2,3},{3,2},{4,5},{5,4},{6,7},{7,6},{8,9},{9,8},{10,11... | collective-permute-start | bytes 786440 | tf_op jit(solution)/shard_map/ppermute | solution.py:457
  122.6 4.2 %copy-start.3 = (bf16[2,128,4096]{2,1,0:T(8,128)(2,1)}, bf16[2,128,4096]{2,1,0:T(8,128)(2,1)S(1)}, u32[]{:S(2)}) copy-start(bf16[2,128,4096]{2,1,0:T(8,128)(2,1)S(1)} %bitcast_dynamic-update-slice_fusion.1) | copy-start | bytes 6291460

commit v6 on v5

--- a/solution.py
+++ b/solution.py
@@ -8,7 +8,7 @@
 from jax.sharding import PartitionSpec as P
 
 LANES = 128
-UNROLL = 16
+UNROLL = 32
 ROWS = 64
 CORES = 2
 CHANS = 32

time: 128 us -> 127 us (level)
  no operation moved by 1% of the time
where the time goes in v6:
time: 127 us; the launch traced here: 126 us
  Pallas kernels  66.2 us (52%)
  starting transfers between devices  31 us (24%)
  waiting for transfers between devices  20.6 us (16%)
  local copies, waits for them, and re-layouts  8.4 us (7%)
    pallas_call x1, Pallas kernels, prepare(): pl.pallas_call(prepare_kernel, grid=(part // chans,), in_specs=[pl.BlockS...  23.2 us
    ppermute x8, starting transfers between devices, across(): lax.ppermute(block, 'ctx', [(i, i ^ distance) for i in range(shards)])  17.3 us
    pallas_call x1, Pallas kernels, long_conv(): pl.pallas_call(conv_kernel, grid=(width // chans,), in_specs=[smem, smem,...  16.4 us
    pallas_call x2, Pallas kernels, short_convs(): pl.pallas_call(functools.partial(short_kernel, count, len(borders)), grid...  11 us
    ppermute x8, waiting for transfers between devices, across(): lax.ppermute(block, 'ctx', [(i, i ^ distance) for i in range(shards)])  10.3 us
    pallas_call x4, Pallas kernels, gate(): pl.pallas_call(functools.partial(gate_kernel, fars), grid=(width // chans...  10.3 us
    ppermute x4, waiting for transfers between devices, local(): came = lax.ppermute(sent[d - 1], 'ch', route)  10.3 us
    all_to_all x1, starting transfers between devices, local(): gated = lax.all_to_all(gated, 'ctx', 0, 0)  7.19 us
  transfers between devices with their start and end apart: 14, of which 5 were waited for; matrix products, arithmetic and copies ran while one was open for 2% of the time, Pallas kernels for 51%

profile of v6, /device:TPU:0, one launch (start us, length us, event | category | flops | bytes accessed | tf_op | source)
XLA Modules:
  0.0 126.4 jit_solution(14342480214243637118)
XLA Ops:
  0.0 0.9 slice.3
  0.9 2.4 %collective-permute-start = (bf16[3,2,2048]{2,1,0:T(2,128)(2,1)S(1)}, bf16[3,2,2048]{2,1,0:T(2,128)(2,1)S(1)}, u32[]{:S(2)}, u32[]{:S(2)}) collective-permute-start(bf16[3,2,2048]{2,1,0:T(2,128)(2,1)S(1)} %slice.3), channel_id=1, source_target_pairs={{0,2},{2,4},{4,6},{6,8},{8,10},{10,12},{12,14},{14,16},{16,18},{18... | collective-permute-start | bytes 73736 | tf_op jit(solution)/shard_map/ppermute | solution.py:401
  3.3 6.4 %short_kv.1.old = bf16[16,128,512]{2,1,0:T(8,128)(2,1)} custom-call(s32[16]{0:T(128)} %doc.7, s32[16]{0:T(128)} %live.7, f32[3,3,2048]{2,1,0:T(4,128)} %refs_0_.3, f32[3,3,2048]{2,1,0:T(4,128)} %refs_0_.3, bf16[3,512,2048]{2,1,0:T(8,128)(2,1)} %refs_1_.2, bf16[3,512,2048]{2,1,0:T(8,128)(2,1)} %refs_1_.2), custom_call_target="tpu_custom_call" | custom-call | tf_op jit(solution)/shard_map/short_kv/pallas_call | solution.py:80
  10.3 2.2 %first_tokens.1 = bf16[16,128,512]{2,1,0:T(8,128)(2,1)} custom-call(s32[16]{0:T(128)} %doc.7, s32[16]{0:T(128)} %live.7, bf16[3,2,2048]{2,1,0:T(2,128)(2,1)} %copy-done.15, bf16[3,2,2048]{2,1,0:T(2,128)(2,1)} %copy-done.15, f32[3,3,2048]{2,1,0:T(4,128)} %refs_0_.3, f32[3,3,2048]{2,1,0:T(4,128)} %refs_0_.3, ...), custom_call_target="tpu_custom_call", output_to_operand_aliasing={{}: (8, {})} | custom-call | tf_op jit(solution)/shard_map/first_tokens/pallas_call | solution.py:126
  12.5 7.2 %all-to-all-start = ((bf16[16,128,512]{2,1,0:T(8,128)(2,1)}), bf16[16,128,512]{2,1,0:T(8,128)(2,1)S(1)}, u32[]{:S(2)}, u32[]{:S(2)}) async-start(bf16[16,128,512]{2,1,0:T(8,128)(2,1)} %first_tokens.1), calls=%async_computation | async-start | bytes 4194304 | tf_op jit(solution)/shard_map/all_to_all | solution.py:415
  19.7 4.7 %short_q.1 = (bf16[8,128,512]{2,1,0:T(8,128)(2,1)}, bf16[8,128,512]{2,1,0:T(8,128)(2,1)}) custom-call(s32[16]{0:T(128)} %doc.7, s32[16]{0:T(128)} %live.7, f32[3,3,2048]{2,1,0:T(4,128)} %refs_0_.3, bf16[3,512,2048]{2,1,0:T(8,128)(2,1)} %refs_1_.2, bf16[3,2,2048]{2,1,0:T(2,128)(2,1)} %copy-done.15), custom_call_target="tpu_custom_call" | custom-call | tf_op jit(solution)/shard_map/short_q/pallas_call | solution.py:80
  24.8 2.5 %collective-permute-done.1.refs_1_ = bf16[8,128,512]{2,1,0:T(8,128)(2,1)S(1)} collective-permute-done((bf16[8,128,512]{2,1,0:T(8,128)(2,1)}, bf16[8,128,512]{2,1,0:T(8,128)(2,1)S(1)}, u32[]{:S(2)}, u32[]{:S(2)}) %collective-permute-start.1) | collective-permute-done | bytes 1048608 | tf_op jit(solution)/shard_map/ppermute | solution.py:409
  27.3 1.0 copy-done.4
  28.3 3.0 %pair_up.1 = (bf16[2,128,512]{2,1,0:T(8,128)(2,1)}, bf16[2,128,512]{2,1,0:T(8,128)(2,1)}, bf16[2,128,512]{2,1,0:T(8,128)(2,1)}, bf16[2,128,512]{2,1,0:T(8,128)(2...) custom-call(bf16[8,128,512]{2,1,0:T(8,128)(2,1)} %get-tuple-element., ...), custom_call_target="tpu_custom_call" | custom-call | tf_op jit(solution)/shard_map/pair_up/pallas_call | solution.py:150
  31.3 1.9 %collective-permute-start.3 = (bf16[2,128,512]{2,1,0:T(8,128)(2,1)}, bf16[2,128,512]{2,1,0:T(8,128)(2,1)S(1)}, u32[]{:S(2)}, u32[]{:S(2)}) collective-permute-start(bf16[2,128,512]{2,1,0:T(8,128)(2,1)} %get-tuple-element.43), channel_id=1, source_target_pairs={{0,4},{2,6},{4,0},{6,2},{8,12},{10,14},{12,8},{14,10},{16,20},{18,... | collective-permute-start | bytes 786440 | tf_op jit(solution)/shard_map/ppermute | solution.py:409
  33.7 1.9 %constant_dynamic-slice_fusion.filt = bf16[2048,128]{1,0:T(8,128)(2,1)} fusion(bf16[2048,2048]{1,0:T(8,128)(2,1)} %param.8, s32[]{:T(128)S(6)} %select_n.56), kind=kLoop, calls=%fused_computation.8 | loop fusion | bytes 1048580 | tf_op jit(solution)/shard_map/dynamic_slice | solution.py:404
  35.6 2.4 %collective-permute-start.2 = (bf16[2,128,512]{2,1,0:T(8,128)(2,1)}, bf16[2,128,512]{2,1,0:T(8,128)(2,1)}, u32[]{:S(2)}, u32[]{:S(2)}) collective-permute-start(bf16[2,128,512]{2,1,0:T(8,128)(2,1)} %get-tuple-element.41), channel_id=1, source_target_pairs={{0,16},{2,18},{4,20},{6,22},{8,24},{10,26},{12,28},{14,30},{16,0},... | collective-permute-start | bytes 786440 | tf_op jit(solution)/shard_map/ppermute | solution.py:409
  38.0 7.8 %collective-permute-done.3.refs_1_ = bf16[2,128,512]{2,1,0:T(8,128)(2,1)S(1)} collective-permute-done((bf16[2,128,512]{2,1,0:T(8,128)(2,1)}, bf16[2,128,512]{2,1,0:T(8,128)(2,1)S(1)}, u32[]{:S(2)}, u32[]{:S(2)}) %collective-permute-start.3) | collective-permute-done | bytes 262176 | tf_op jit(solution)/shard_map/ppermute | solution.py:409
  45.8 23.2 %prepare.1 = (bf16[128,576,256]{2,1,0:T(8,128)(2,1)}, f32[128,1]{1,0:T(8,128)}) custom-call(bf16[2048,128]{1,0:T(8,128)(2,1)} %constant_dynamic-slice_fusion.filt, f32[1,128]{1,0:T(1,128)} %dynamic-slice_bitcast_fusion.skip), custom_call_target="tpu_custom_call" | custom-call | tf_op jit(solution)/shard_map/prepare/pallas_call | solution.py:189
  69.1 6.4 %collective-permute-start.5 = (bf16[2,128,512]{2,1,0:T(8,128)(2,1)}, bf16[2,128,512]{2,1,0:T(8,128)(2,1)S(1)}, u32[]{:S(2)}, u32[]{:S(2)}) collective-permute-start(bf16[2,128,512]{2,1,0:T(8,128)(2,1)} %get-tuple-element.59), channel_id=1, source_target_pairs={{0,20},{2,22},{4,16},{6,18},{8,28},{10,30},{12,24},{14,26},{16,4},... | collective-permute-start | bytes 786440 | tf_op jit(solution)/shard_map/ppermute | solution.py:409
  75.5 2.3 %collective-permute-start.7 = (bf16[2,128,512]{2,1,0:T(8,128)(2,1)}, bf16[2,128,512]{2,1,0:T(8,128)(2,1)S(1)}, u32[]{:S(2)}, u32[]{:S(2)}) collective-permute-start(bf16[2,128,512]{2,1,0:T(8,128)(2,1)} %get-tuple-element.63), channel_id=1, source_target_pairs={{0,24},{2,26},{4,28},{6,30},{8,16},{10,18},{12,20},{14,22},{16,8},... | collective-permute-start | bytes 786440 | tf_op jit(solution)/shard_map/ppermute | solution.py:409
  77.8 1.4 %collective-permute-start.8 = (bf16[2,128,512]{2,1,0:T(8,128)(2,1)}, bf16[2,128,512]{2,1,0:T(8,128)(2,1)S(1)}, u32[]{:S(2)}, u32[]{:S(2)}) collective-permute-start(bf16[2,128,512]{2,1,0:T(8,128)(2,1)} %get-tuple-element.64), channel_id=1, source_target_pairs={{0,8},{2,10},{4,12},{6,14},{8,0},{10,2},{12,4},{14,6},{16,24},{18,... | collective-permute-start | bytes 786440 | tf_op jit(solution)/shard_map/ppermute | solution.py:409
  79.2 16.4 %long_conv.1.refs_2_ = bf16[16,128,512]{2,1,0:T(8,128)(2,1)} custom-call(s32[16]{0:T(128)} %doc.7, s32[16]{0:T(128)} %live.7, f32[128,1]{1,0:T(8,128)} %get-tuple-element.45.skip, bf16[128,576,256]{2,1,0:T(8,128)(2,1)} %get-tuple-element.51.toeplitz, bf16[16,128,512]{2,1,0:T(8,128)(2,1)} %copy-done.2), custom_call_target="tpu_custom_call" | custom-call | flops 1 | bytes 1 | tf_op jit(solution)/shard_map/long_conv/pallas_call | solution.py:310
  95.6 2.6 %gate.4 = (bf16[128,1024]{1,0:T(8,128)(2,1)}, bf16[1,128,1024]{2,1,0:T(8,128)(2,1)}) custom-call(bf16[2,128,512]{2,1,0:T(8,128)(2,1)} %collective-permute-done.2.refs_0_, bf16[2,128,512]{2,1,0:T(8,128)(2,1)} %get-tuple-element.42.refs_1_, bf16[16,128,512]{2,1,0:T(8,128)(2,1)} %long_conv.1.refs_2_), custom_call_target="tpu_custom_call" | custom-call | flops 1 | bytes 1 | tf_op jit(solution)/shard_map/gate/pallas_call | solution.py:373
  98.2 2.5 %collective-permute-start.10 = (bf16[2,128,512]{2,1,0:T(8,128)(2,1)S(1)}, bf16[2,128,512]{2,1,0:T(8,128)(2,1)S(1)}, u32[]{:S(2)}, u32[]{:S(2)}) collective-permute-start(bf16[2,128,512]{2,1,0:T(8,128)(2,1)S(1)} %copy-done.16), channel_id=1, source_target_pairs={{0,28},{2,30},{4,24},{6,26},{8,20},{10,22},{12,16},{14,18},{16,12}... | collective-permute-start | bytes 786440 | tf_op jit(solution)/shard_map/ppermute | solution.py:409
  100.7 1.5 %collective-permute-start.4 = (bf16[128,1024]{1,0:T(8,128)(2,1)}, bf16[128,1024]{1,0:T(8,128)(2,1)S(1)}, u32[]{:S(2)}, u32[]{:S(2)}) collective-permute-start(bf16[128,1024]{1,0:T(8,128)(2,1)} %bitcast.22), channel_id=1, source_target_pairs={{0,1},{1,0},{2,3},{3,2},{4,5},{5,4},{6,7},{7,6},{8,9},{9,8},{10,11... | collective-permute-start | bytes 786440 | tf_op jit(solution)/shard_map/ppermute | solution.py:457
  102.5 2.6 %gate.5 = (bf16[128,1024]{1,0:T(8,128)(2,1)}, bf16[1,128,1024]{2,1,0:T(8,128)(2,1)}) custom-call(bf16[2,128,512]{2,1,0:T(8,128)(2,1)} %copy-done.10, bf16[2,128,512]{2,1,0:T(8,128)(2,1)} %copy-done.6, bf16[16,128,512]{2,1,0:T(8,128)(2,1)} %long_conv.1.refs_2_), custom_call_target="tpu_custom_call" | custom-call | flops 1 | bytes 1 | tf_op jit(solution)/shard_map/gate/pallas_call | solution.py:373
  105.8 0.7 copy-done.8
  106.5 2.5 %gate.6 = (bf16[128,1024]{1,0:T(8,128)(2,1)}, bf16[1,128,1024]{2,1,0:T(8,128)(2,1)}) custom-call(bf16[2,128,512]{2,1,0:T(8,128)(2,1)} %copy-done.7, bf16[2,128,512]{2,1,0:T(8,128)(2,1)} %copy-done.8, bf16[16,128,512]{2,1,0:T(8,128)(2,1)} %long_conv.1.refs_2_), custom_call_target="tpu_custom_call" | custom-call | flops 1 | bytes 1 | tf_op jit(solution)/shard_map/gate/pallas_call | solution.py:373
  109.1 1.5 %collective-permute-start.9 = (bf16[128,1024]{1,0:T(8,128)(2,1)}, bf16[128,1024]{1,0:T(8,128)(2,1)S(1)}, u32[]{:S(2)}, u32[]{:S(2)}) collective-permute-start(bf16[128,1024]{1,0:T(8,128)(2,1)} %bitcast.24), channel_id=1, source_target_pairs={{0,1},{1,0},{2,3},{3,2},{4,5},{5,4},{6,7},{7,6},{8,9},{9,8},{10,11... | collective-permute-start | bytes 786440 | tf_op jit(solution)/shard_map/ppermute | solution.py:457
  110.5 0.7 copy-done.5
  111.2 0.7 copy-done.9
  111.9 2.6 %gate.7 = (bf16[128,1024]{1,0:T(8,128)(2,1)}, bf16[1,128,1024]{2,1,0:T(8,128)(2,1)}) custom-call(bf16[2,128,512]{2,1,0:T(8,128)(2,1)} %copy-done.9, bf16[2,128,512]{2,1,0:T(8,128)(2,1)} %copy-done.5, bf16[16,128,512]{2,1,0:T(8,128)(2,1)} %long_conv.1.refs_2_), custom_call_target="tpu_custom_call" | custom-call | flops 1 | bytes 1 | tf_op jit(solution)/shard_map/gate/pallas_call | solution.py:373
  114.5 0.6 collective-permute-start.12
  115.8 5.5 %collective-permute-done.9 = bf16[128,1024]{1,0:T(8,128)(2,1)S(1)} collective-permute-done((bf16[128,1024]{1,0:T(8,128)(2,1)}, bf16[128,1024]{1,0:T(8,128)(2,1)S(1)}, u32[]{:S(2)}, u32[]{:S(2)}) %collective-permute-start.9) | collective-permute-done | bytes 262176 | tf_op jit(solution)/shard_map/ppermute | solution.py:457
  121.5 4.2 %collective-permute-done.12 = bf16[128,1024]{1,0:T(8,128)(2,1)S(1)} collective-permute-done((bf16[128,1024]{1,0:T(8,128)(2,1)}, bf16[128,1024]{1,0:T(8,128)(2,1)S(1)}, u32[]{:S(2)}, u32[]{:S(2)}) %collective-permute-start.12) | collective-permute-done | bytes 262176 | tf_op jit(solution)/shard_map/ppermute | solution.py:457
  125.6 0.7 bitcast_dynamic-update-slice_fusion
  (52 shorter events, 3.3 us)
Async XLA Ops:
  0.0 33.1 %copy-start = (f32[2048]{0:T(1024)S(1)}, f32[2048]{0:T(1024)}, u32[]{:S(2)}) copy-start(f32[2048]{0:T(1024)} %param.9) | copy-start | bytes 24580
  0.9 8.7 %collective-permute-start = (bf16[3,2,2048]{2,1,0:T(2,128)(2,1)S(1)}, bf16[3,2,2048]{2,1,0:T(2,128)(2,1)S(1)}, u32[]{:S(2)}, u32[]{:S(2)}) collective-permute-start(bf16[3,2,2048]{2,1,0:T(2,128)(2,1)S(1)} %slice.3), channel_id=1, source_target_pairs={{0,2},{2,4},{4,6},{6,8},{8,10},{10,12},{12,14},{14,16},{16,18},{18... | collective-permute-start | bytes 73736 | tf_op jit(solution)/shard_map/ppermute | solution.py:401
  9.7 0.6 copy-start.15
  12.5 56.5 %all-to-all-start = ((bf16[16,128,512]{2,1,0:T(8,128)(2,1)}), bf16[16,128,512]{2,1,0:T(8,128)(2,1)S(1)}, u32[]{:S(2)}, u32[]{:S(2)}) async-start(bf16[16,128,512]{2,1,0:T(8,128)(2,1)} %first_tokens.1), calls=%async_computation | async-start | bytes 4194304 | tf_op jit(solution)/shard_map/all_to_all | solution.py:415
  24.4 2.9 %collective-permute-start.1 = (bf16[8,128,512]{2,1,0:T(8,128)(2,1)}, bf16[8,128,512]{2,1,0:T(8,128)(2,1)S(1)}, u32[]{:S(2)}, u32[]{:S(2)}) collective-permute-start(bf16[8,128,512]{2,1,0:T(8,128)(2,1)} %get-tuple-element.40), channel_id=1, source_target_pairs={{0,2},{2,0},{4,6},{6,4},{8,10},{10,8},{12,14},{14,12},{16,18},{18,... | collective-permute-start | bytes 3145736 | tf_op jit(solution)/shard_map/ppermute | solution.py:409
  27.3 1.0 copy-start.4
  31.3 14.5 %collective-permute-start.3 = (bf16[2,128,512]{2,1,0:T(8,128)(2,1)}, bf16[2,128,512]{2,1,0:T(8,128)(2,1)S(1)}, u32[]{:S(2)}, u32[]{:S(2)}) collective-permute-start(bf16[2,128,512]{2,1,0:T(8,128)(2,1)} %get-tuple-element.43), channel_id=1, source_target_pairs={{0,4},{2,6},{4,0},{6,2},{8,12},{10,14},{12,8},{14,10},{16,20},{18,... | collective-permute-start | bytes 786440 | tf_op jit(solution)/shard_map/ppermute | solution.py:409
  35.6 60.0 %collective-permute-start.2 = (bf16[2,128,512]{2,1,0:T(8,128)(2,1)}, bf16[2,128,512]{2,1,0:T(8,128)(2,1)}, u32[]{:S(2)}, u32[]{:S(2)}) collective-permute-start(bf16[2,128,512]{2,1,0:T(8,128)(2,1)} %get-tuple-element.41), channel_id=1, source_target_pairs={{0,16},{2,18},{4,20},{6,22},{8,24},{10,26},{12,28},{14,30},{16,0},... | collective-permute-start | bytes 786440 | tf_op jit(solution)/shard_map/ppermute | solution.py:409
  45.8 49.8 %copy-start.6 = (bf16[2,128,512]{2,1,0:T(8,128)(2,1)}, bf16[2,128,512]{2,1,0:T(8,128)(2,1)S(1)}, u32[]{:S(2)}) copy-start(bf16[2,128,512]{2,1,0:T(8,128)(2,1)S(1)} %collective-permute-done.3.refs_1_) | copy-start | bytes 786436
  69.0 10.2 %copy-start.2 = (bf16[16,128,512]{2,1,0:T(8,128)(2,1)}, bf16[16,128,512]{2,1,0:T(8,128)(2,1)S(1)}, u32[]{:S(2)}) copy-start(bf16[16,128,512]{2,1,0:T(8,128)(2,1)S(1)} %all-to-all-done.gated) | copy-start | bytes 6291460
  69.1 31.7 %collective-permute-start.5 = (bf16[2,128,512]{2,1,0:T(8,128)(2,1)}, bf16[2,128,512]{2,1,0:T(8,128)(2,1)S(1)}, u32[]{:S(2)}, u32[]{:S(2)}) collective-permute-start(bf16[2,128,512]{2,1,0:T(8,128)(2,1)} %get-tuple-element.59), channel_id=1, source_target_pairs={{0,20},{2,22},{4,16},{6,18},{8,28},{10,30},{12,24},{14,26},{16,4},... | collective-permute-start | bytes 786440 | tf_op jit(solution)/shard_map/ppermute | solution.py:409
  75.5 35.1 %collective-permute-start.11 = (bf16[2,128,512]{2,1,0:T(8,128)(2,1)}, bf16[2,128,512]{2,1,0:T(8,128)(2,1)S(1)}, u32[]{:S(2)}, u32[]{:S(2)}) collective-permute-start(bf16[2,128,512]{2,1,0:T(8,128)(2,1)} %get-tuple-element.68), channel_id=1, source_target_pairs={{0,12},{2,14},{4,8},{6,10},{8,4},{10,6},{12,0},{14,2},{16,28},{18,... | collective-permute-start | bytes 786440 | tf_op jit(solution)/shard_map/ppermute | solution.py:409
  75.5 29.7 %collective-permute-start.7 = (bf16[2,128,512]{2,1,0:T(8,128)(2,1)}, bf16[2,128,512]{2,1,0:T(8,128)(2,1)S(1)}, u32[]{:S(2)}, u32[]{:S(2)}) collective-permute-start(bf16[2,128,512]{2,1,0:T(8,128)(2,1)} %get-tuple-element.63), channel_id=1, source_target_pairs={{0,24},{2,26},{4,28},{6,30},{8,16},{10,18},{12,20},{14,22},{16,8},... | collective-permute-start | bytes 786440 | tf_op jit(solution)/shard_map/ppermute | solution.py:409
  77.8 27.9 %collective-permute-start.8 = (bf16[2,128,512]{2,1,0:T(8,128)(2,1)}, bf16[2,128,512]{2,1,0:T(8,128)(2,1)S(1)}, u32[]{:S(2)}, u32[]{:S(2)}) collective-permute-start(bf16[2,128,512]{2,1,0:T(8,128)(2,1)} %get-tuple-element.64), channel_id=1, source_target_pairs={{0,8},{2,10},{4,12},{6,14},{8,0},{10,2},{12,4},{14,6},{16,24},{18,... | collective-permute-start | bytes 786440 | tf_op jit(solution)/shard_map/ppermute | solution.py:409
  95.6 2.6 %copy-start.16 = (bf16[2,128,512]{2,1,0:T(8,128)(2,1)S(1)}, bf16[2,128,512]{2,1,0:T(8,128)(2,1)}, u32[]{:S(2)}) copy-start(bf16[2,128,512]{2,1,0:T(8,128)(2,1)} %get-tuple-element.67) | copy-start | bytes 786436
  98.2 4.2 %copy-start.11 = (bf16[128,1024]{1,0:T(8,128)(2,1)S(1)}, bf16[128,1024]{1,0:T(8,128)(2,1)}, u32[]{:S(2)}) copy-start(bf16[128,1024]{1,0:T(8,128)(2,1)} %get-tuple-element.55) | copy-start | bytes 786436
  98.2 12.3 %collective-permute-start.10 = (bf16[2,128,512]{2,1,0:T(8,128)(2,1)S(1)}, bf16[2,128,512]{2,1,0:T(8,128)(2,1)S(1)}, u32[]{:S(2)}, u32[]{:S(2)}) collective-permute-start(bf16[2,128,512]{2,1,0:T(8,128)(2,1)S(1)} %copy-done.16), channel_id=1, source_target_pairs={{0,28},{2,30},{4,24},{6,26},{8,20},{10,22},{12,16},{14,18},{16,12}... | collective-permute-start | bytes 786440 | tf_op jit(solution)/shard_map/ppermute | solution.py:409
  100.7 1.8 %copy-start.10 = (bf16[2,128,512]{2,1,0:T(8,128)(2,1)}, bf16[2,128,512]{2,1,0:T(8,128)(2,1)S(1)}, u32[]{:S(2)}) copy-start(bf16[2,128,512]{2,1,0:T(8,128)(2,1)S(1)} %collective-permute-done.5.refs_0_) | copy-start | bytes 786436
  100.7 14.4 %collective-permute-start.4 = (bf16[128,1024]{1,0:T(8,128)(2,1)}, bf16[128,1024]{1,0:T(8,128)(2,1)S(1)}, u32[]{:S(2)}, u32[]{:S(2)}) collective-permute-start(bf16[128,1024]{1,0:T(8,128)(2,1)} %bitcast.22), channel_id=1, source_target_pairs={{0,1},{1,0},{2,3},{3,2},{4,5},{5,4},{6,7},{7,6},{8,9},{9,8},{10,11... | collective-permute-start | bytes 786440 | tf_op jit(solution)/shard_map/ppermute | solution.py:457
  105.1 0.7 copy-start.7
  105.1 10.7 %collective-permute-start.6 = (bf16[128,1024]{1,0:T(8,128)(2,1)}, bf16[128,1024]{1,0:T(8,128)(2,1)S(1)}, u32[]{:S(2)}, u32[]{:S(2)}) collective-permute-start(bf16[128,1024]{1,0:T(8,128)(2,1)} %bitcast.23), channel_id=1, source_target_pairs={{0,1},{1,0},{2,3},{3,2},{4,5},{5,4},{6,7},{7,6},{8,9},{9,8},{10,11... | collective-permute-start | bytes 786440 | tf_op jit(solution)/shard_map/ppermute | solution.py:457
  105.8 0.7 copy-start.8
  109.0 6.1 %copy-start.12 = (bf16[128,1024]{1,0:T(8,128)(2,1)S(1)}, bf16[128,1024]{1,0:T(8,128)(2,1)}, u32[]{:S(2)}) copy-start(bf16[128,1024]{1,0:T(8,128)(2,1)} %get-tuple-element.61) | copy-start | bytes 786436
  109.0 6.8 %copy-start.13 = (bf16[128,1024]{1,0:T(8,128)(2,1)S(1)}, bf16[128,1024]{1,0:T(8,128)(2,1)}, u32[]{:S(2)}) copy-start(bf16[128,1024]{1,0:T(8,128)(2,1)} %get-tuple-element.65) | copy-start | bytes 786436
  109.1 12.3 %collective-permute-start.9 = (bf16[128,1024]{1,0:T(8,128)(2,1)}, bf16[128,1024]{1,0:T(8,128)(2,1)S(1)}, u32[]{:S(2)}, u32[]{:S(2)}) collective-permute-start(bf16[128,1024]{1,0:T(8,128)(2,1)} %bitcast.24), channel_id=1, source_target_pairs={{0,1},{1,0},{2,3},{3,2},{4,5},{5,4},{6,7},{7,6},{8,9},{9,8},{10,11... | collective-permute-start | bytes 786440 | tf_op jit(solution)/shard_map/ppermute | solution.py:457
  110.5 0.7 copy-start.5
  111.2 0.7 copy-start.9
  111.9 14.4 %copy-start.1 = (f32[2048]{0:T(1024)S(1)}, f32[2048]{0:T(1024)}, u32[]{:S(2)}) copy-start(f32[2048]{0:T(1024)} %param.9) | copy-start | bytes 24580
  114.5 6.9 %copy-start.14 = (bf16[128,1024]{1,0:T(8,128)(2,1)S(1)}, bf16[128,1024]{1,0:T(8,128)(2,1)}, u32[]{:S(2)}) copy-start(bf16[128,1024]{1,0:T(8,128)(2,1)} %get-tuple-element.69) | copy-start | bytes 786436
  114.5 11.1 %collective-permute-start.12 = (bf16[128,1024]{1,0:T(8,128)(2,1)}, bf16[128,1024]{1,0:T(8,128)(2,1)S(1)}, u32[]{:S(2)}, u32[]{:S(2)}) collective-permute-start(bf16[128,1024]{1,0:T(8,128)(2,1)} %bitcast.25), channel_id=1, source_target_pairs={{0,1},{1,0},{2,3},{3,2},{4,5},{5,4},{6,7},{7,6},{8,9},{9,8},{10,11... | collective-permute-start | bytes 786440 | tf_op jit(solution)/shard_map/ppermute | solution.py:457
  121.5 4.2 %copy-start.3 = (bf16[2,128,4096]{2,1,0:T(8,128)(2,1)}, bf16[2,128,4096]{2,1,0:T(8,128)(2,1)S(1)}, u32[]{:S(2)}) copy-start(bf16[2,128,4096]{2,1,0:T(8,128)(2,1)S(1)} %bitcast_dynamic-update-slice_fusion.1) | copy-start | bytes 6291460
